TPU v7x, 128 devices: a whole 4x4x4 slice. The times are simulated.
128 devices in a mesh: gx: 8 (over y, x_hi), gy: 16 (over z, x_lo, core).
Axes of the slice: x: 4 (x_hi: 2, x_lo: 2; x = x_hi * 2 + x_lo), y: 4, z: 4, core: 2. Of those that a mesh axis runs over, the one named last changes fastest.
Arguments:
- displacement: float32 [3, 16, 512, 2048], P(None, None, 'gx', 'gy'), may hold values from -1.2 to 1.2
- velocity: float32 [3, 16, 512, 2048], P(None, None, 'gx', 'gy'), may hold values from -6 to 6
- shear: float32 [15, 512, 2048], P(None, 'gx', 'gy'), may hold values from 0.3 to 3
- normals: float32 [3, 512, 2048], P(None, 'gx', 'gy'), may hold values from -1 to 1
- gap_zero: float32 [512, 2048], P('gx', 'gy'), may hold values from -0.3 to 0.1
- mortar: bfloat16 [512, 16, 128, 128], P('gx', 'gy'), may hold values from -1 to 1
- owner: int32 [512, 16], P('gx', 'gy'), may hold values from 0 to 15, as said below
- blocks: int32 [512, 16], P('gx', 'gy'), may hold values from 0 to 63
- live_rows: int32 [8, 16], P('gx', 'gy'), may hold values from 16 to 64, as said below
Outputs:
- new_displacement: float32 [3, 16, 512, 2048], P(None, None, 'gx', 'gy')
- new_velocity: float32 [3, 16, 512, 2048], P(None, None, 'gx', 'gy')
Inputs may be any that keep to these rules, and one draw needn't show every extreme that they name: owner[r, j] = (j + 8 + e) mod 2048 / 128 with e one of -1, 0, 1. Slave blocks of rows 0 to live_rows - 1 of a tile are in contact; some tile has all 64 in every draw.
All inputs are finite; a program needn't handle non-finite values.
Results may differ from a plain program's by a relative error of at most 0.0003.
Values sent between devices are 32-bit elements; how exact they have to be, the bound alone decides.
No kernel may reach another device: no remote copies, remote signals or barrier semaphores. Data moves between devices by JAX's collectives and lax.ppermute only.
A program may use at most 64 MiB of HBM per device.

v0:
```python
import functools

import jax
import jax.numpy as jnp
from jax import lax
from jax.experimental import pallas as pl
from jax.experimental.pallas import tpu as pltpu
from jax.sharding import PartitionSpec as P

ROWS_DEV = 64
BLOCK = 128
DEPTH = 16
PLANES = 3 * DEPTH
SURF = 3 * ROWS_DEV
STRIP = 72

DAMPING = 0.9
TIME_STEP = 0.1
PENALTY = 10.0

F32 = jnp.float32
BF16 = jnp.bfloat16
VMEM = pl.BlockSpec(memory_space=pltpu.VMEM)
SMEM = pl.BlockSpec(memory_space=pltpu.SMEM)
ANY = pl.BlockSpec(memory_space=pl.ANY)


def iota(shape, dim):
    return lax.broadcasted_iota(jnp.int32, shape, dim)


def roll(x, by, dim):
    return pltpu.roll(x, by % x.shape[dim], dim)


def call(kernel, out_shape, in_specs, out_specs, scratch, args, flops, bytes_accessed):
    return pl.pallas_call(
        kernel,
        out_shape=out_shape,
        in_specs=in_specs,
        out_specs=out_specs,
        scratch_shapes=scratch,
        compiler_params=pltpu.CompilerParams(vmem_limit_bytes=40 * 2**20),
        cost_estimate=pl.CostEstimate(
            flops=flops, bytes_accessed=bytes_accessed, transcendentals=0
        ),
    )(*args)


def out(rows):
    return jax.ShapeDtypeStruct((rows, BLOCK), F32)


def stress(low, high, modulus):
    g = []
    for c in range(3):
        depth = high[c][0] - low[c][0]
        rows = high[c][1] + low[c][1]
        cols = high[c][2] + low[c][2]
        line = [depth, rows, cols]
        line[c] = line[c] + 4.0
        g.append(line)
    cof = [
        [
            g[(c + 1) % 3][(d + 1) % 3] * g[(c + 2) % 3][(d + 2) % 3]
            - g[(c + 1) % 3][(d + 2) % 3] * g[(c + 2) % 3][(d + 1) % 3]
            for d in range(3)
        ]
        for c in range(3)
    ]
    det = g[0][0] * cof[0][0] + g[0][1] * cof[0][1] + g[0][2] * cof[0][2]
    linear = modulus * (0.25 * TIME_STEP * 0.25)
    bulk = modulus * (det * (0.25 * TIME_STEP / 512.0) - 0.25 * TIME_STEP * 3.0 / 16.0)
    return [[linear * g[c][d] + bulk * cof[c][d] for d in range(3)] for c in range(3)]


def dead_lane(tile):
    return lax.axis_size("gy") * BLOCK // 2 + BLOCK // 2 - 1 - tile * BLOCK


def forces_kernel(patched, *refs):
    if patched:
        u_hbm, v_hbm, shear_hbm, comb, v_out, u, v, shear, z, mask, sems = refs
    else:
        u_hbm, v_hbm, shear_hbm, v_out, u, v, shear, z, mask, sems = refs
    copies = [
        pltpu.make_async_copy(u_hbm, u.at[:, 0:ROWS_DEV, :], sems.at[0]),
        pltpu.make_async_copy(v_hbm, v, sems.at[1]),
        pltpu.make_async_copy(shear_hbm, shear, sems.at[2]),
    ]
    for copy in copies:
        copy.start()
    zero = jnp.zeros((PLANES, 8, BLOCK), F32)
    u[:, ROWS_DEV:STRIP, :] = zero
    z[:, 0:8, :] = zero
    lanes = iota((ROWS_DEV, BLOCK), 1)
    rows = iota((ROWS_DEV, BLOCK), 0)
    keep = (lanes < BLOCK - 1) & (rows < ROWS_DEV - 1) & (lanes != dead_lane(lax.axis_index("gy")))
    mask[...] = keep.astype(F32)
    for copy in copies:
        copy.wait()
    if patched:
        for c in range(3):
            at = pl.ds(c * ROWS_DEV, ROWS_DEV)
            u[c * DEPTH, 0:ROWS_DEV, :] += TIME_STEP * TIME_STEP * comb[at, :]
            v[c * DEPTH, :, :] += TIME_STEP * comb[at, :]

    def chunk(i, _):
        r0 = pl.multiple_of(i * 8, 8)
        here = pl.ds(r0, 8)
        exists = mask[here, :]

        def face(k):
            result = []
            for c in range(3):
                a = u[c * DEPTH + k, here, :]
                b = u[c * DEPTH + k, pl.ds(r0 + 1, 8), :]
                p = a + b
                q = b - a
                p_next = roll(p, -1, 1)
                q_next = roll(q, -1, 1)
                result.append((p + p_next, q + q_next, p_next - p))
            return result

        low = face(0)
        before = None
        for k in range(DEPTH):
            if k < DEPTH - 1:
                high = face(k + 1)
                now = stress(low, high, shear[k, here, :] * exists)
                low = high
            else:
                now = None
            for c in range(3):
                if before is None:
                    d, e, g = now[c]
                elif now is None:
                    d, e, g = -before[c][0], before[c][1], before[c][2]
                else:
                    d = now[c][0] - before[c][0]
                    e = now[c][1] + before[c][1]
                    g = now[c][2] + before[c][2]
                dg = (d + g) + roll(d - g, 1, 1)
                ee = e + roll(e, 1, 1)
                plane = c * DEPTH + k
                z[plane, pl.ds(r0 + 8, 8), :] = dg - ee
                total = (dg + ee) + z[plane, pl.ds(r0 + 7, 8), :]
                v_out[plane, here, :] = DAMPING * v[plane, here, :] + total
            before = now
        return 0

    lax.fori_loop(0, ROWS_DEV // 8, chunk, 0)


def interior_forces(u, v, shear, comb=None):
    args = [x.reshape(-1, ROWS_DEV, BLOCK) for x in (u, v, shear)]
    specs = [ANY, ANY, ANY]
    if comb is not None:
        args.append(comb)
        specs.append(VMEM)
    return call(
        functools.partial(forces_kernel, comb is not None),
        jax.ShapeDtypeStruct((PLANES, ROWS_DEV, BLOCK), F32),
        specs,
        VMEM,
        [
            pltpu.VMEM((PLANES, STRIP, BLOCK), F32),
            pltpu.VMEM((PLANES, ROWS_DEV, BLOCK), F32),
            pltpu.VMEM((DEPTH - 1, ROWS_DEV, BLOCK), F32),
            pltpu.VMEM((PLANES, STRIP, BLOCK), F32),
            pltpu.VMEM((ROWS_DEV, BLOCK), F32),
            pltpu.SemaphoreType.DMA((3,)),
        ],
        args,
        30_000_000,
        6_000_000,
    ).reshape(PLANES * ROWS_DEV, BLOCK)


def pack_kernel(u, shear, surface, first, last, sems):
    copies = []
    for c in range(3):
        copies.append(
            pltpu.make_async_copy(
                u.at[c * DEPTH], surface.at[pl.ds(c * ROWS_DEV, ROWS_DEV), :], sems.at[c]
            )
        )
    copies.append(pltpu.make_async_copy(u.at[:, 0, :], first.at[0:PLANES, :], sems.at[3]))
    copies.append(
        pltpu.make_async_copy(u.at[:, ROWS_DEV - 1, :], last.at[0:PLANES, :], sems.at[4])
    )
    copies.append(
        pltpu.make_async_copy(
            shear.at[:, ROWS_DEV - 1, :], last.at[PLANES : PLANES + DEPTH - 1, :], sems.at[5]
        )
    )
    for copy in copies:
        copy.start()
    first[PLANES : PLANES + DEPTH, :] = jnp.zeros((DEPTH, BLOCK), F32)
    last[PLANES + DEPTH - 1 : PLANES + DEPTH, :] = jnp.zeros((1, BLOCK), F32)
    for copy in copies:
        copy.wait()


def pack(u, shear):
    return call(
        pack_kernel,
        (out(SURF), out(64), out(64)),
        [ANY, ANY],
        (VMEM, VMEM, VMEM),
        [pltpu.SemaphoreType.DMA((6,))],
        (u.reshape(-1, ROWS_DEV, BLOCK), shear.reshape(-1, ROWS_DEV, BLOCK)),
        1000,
        400_000,
    )


def put_column(strip, plane, position):
    lanes = iota(plane.shape, 1)
    return jnp.where(lanes // 2 == position, pltpu.roll(plane, 2 * position + 1, 1), strip)


def strip_kernel(u, shear, strip):
    def layer(k, held):
        for c in range(3):
            held = put_column(held, u[c * DEPTH + k, :, :], c * DEPTH + k)
        return held

    def moduli(k, held):
        return put_column(held, shear[k, :, :], PLANES + k)

    held = lax.fori_loop(0, DEPTH, layer, jnp.zeros((ROWS_DEV, BLOCK), F32))
    held = lax.fori_loop(0, DEPTH - 1, moduli, held)
    strip[0:ROWS_DEV, :] = held
    strip[ROWS_DEV:STRIP, :] = jnp.zeros((STRIP - ROWS_DEV, BLOCK), F32)


def strips(u, shear):
    return call(
        strip_kernel,
        out(STRIP),
        [VMEM, VMEM],
        VMEM,
        [],
        (u.reshape(-1, ROWS_DEV, BLOCK), shear.reshape(-1, ROWS_DEV, BLOCK)),
        1_000_000,
        2_000_000,
    )


def ends_of_row(line):
    sub = iota((64, BLOCK), 0)
    lanes = iota((64, BLOCK), 1)
    start = jnp.broadcast_to(line[:, 0:1], (64, BLOCK))
    end = jnp.broadcast_to(line[:, BLOCK - 1 : BLOCK], (64, BLOCK))
    both = jnp.where(lanes % 2 == 1, start, end)
    return jnp.sum(jnp.where(lanes // 2 == sub, both, 0.0), axis=0, keepdims=True)


def message_kernel(surface, above, below, strip, message):
    message[0:SURF, :] = surface[...]
    message[SURF : SURF + STRIP, :] = strip[...]
    message[SURF + ROWS_DEV : SURF + ROWS_DEV + 1, :] = ends_of_row(below[...])
    message[SURF + STRIP - 1 : SURF + STRIP, :] = ends_of_row(above[...])


def message(surface, above, below, strip):
    return call(
        message_kernel,
        out(SURF + STRIP),
        [VMEM] * 4,
        VMEM,
        [],
        (surface, above, below, strip),
        100_000,
        300_000,
    )


def row_ring(low_row, high_row, moduli, upper):
    faces = []
    for c in range(3):
        a = low_row[c * DEPTH : (c + 1) * DEPTH]
        b = high_row[c * DEPTH : (c + 1) * DEPTH]
        p = a + b
        q = b - a
        p_next = roll(p, -1, 1)
        q_next = roll(q, -1, 1)
        faces.append((p + p_next, q + q_next, p_next - p))
    above = [tuple(roll(x, -1, 0) for x in face) for face in faces]
    s = stress(faces, above, moduli)
    result = []
    for c in range(3):
        d = s[c][0] - roll(s[c][0], 1, 0)
        e = s[c][1] + roll(s[c][1], 1, 0)
        g = s[c][2] + roll(s[c][2], 1, 0)
        dg = (d + g) + roll(d - g, 1, 1)
        ee = e + roll(e, 1, 1)
        result.append(dg - ee if upper else dg + ee)
    return result


def row_rings(first, last, above, below, own_moduli, moduli_above):
    gx = lax.axis_index("gx")
    lanes = iota((DEPTH, BLOCK), 1)
    sub = iota((DEPTH, BLOCK), 0)
    keep = (
        (lanes < BLOCK - 1)
        & (sub < DEPTH - 1)
        & (lanes != dead_lane(lax.axis_index("gy")))
    )
    top_moduli = jnp.where(keep & (gx > 0), moduli_above, 0.0)
    bottom_moduli = jnp.where(keep & (gx < lax.axis_size("gx") - 1), own_moduli, 0.0)
    top = row_ring(above, first, top_moduli, True)
    bottom = row_ring(last, below, bottom_moduli, False)
    return top, bottom


def column_ring(own, from_left, from_right, moduli):
    gx = lax.axis_index("gx")
    gy = lax.axis_index("gy")
    shape = (STRIP, BLOCK)
    lanes = iota(shape, 1)
    sub = iota(shape, 0)
    odd = lanes % 2 == 1
    halo = jnp.where(odd, roll(from_left, 1, 1), roll(from_right, -1, 1))
    near = jnp.where(odd, halo, own)
    far = jnp.where(odd, own, halo)
    s = near + far
    d = far - near
    s_next = roll(s, -1, 0)
    d_next = roll(d, -1, 0)
    face = (s + s_next, s_next - s, d + d_next)
    low = [tuple(roll(x, -32 * c, 1) if c else x for x in face) for c in range(3)]
    high = [tuple(roll(x, -2, 1) for x in each) for each in low]
    keep = (
        (lanes < 2 * DEPTH - 2)
        & ((sub < ROWS_DEV) | (sub == STRIP - 1))
        & ((sub != STRIP - 1) | (gx > 0))
        & ((sub != ROWS_DEV - 1) | (gx < lax.axis_size("gx") - 1))
        & (jnp.logical_not(odd) | (gy > 0))
        & (odd | (gy < lax.axis_size("gy") - 1))
    )
    held = near if moduli is None else moduli
    m = jnp.where(keep, roll(held, -96, 1), 0.0)
    q = stress(low, high, m)
    total = None
    for c in range(3):
        dd = q[c][0] - roll(q[c][0], 2, 1)
        ee = q[c][1] + roll(q[c][1], 2, 1)
        gg = q[c][2] + roll(q[c][2], 2, 1)
        dg = dd + jnp.where(odd, -gg, gg)
        f = (dg + ee) + roll(dg - ee, 1, 0)
        f = roll(f, 32 * c, 1) if c else f
        total = f if total is None else total + f
    return total[0:ROWS_DEV], near


def from_strip(strip, position):
    lanes = iota((ROWS_DEV, BLOCK), 1)
    moved = pltpu.roll(strip, BLOCK - 1 - 2 * position, 1)
    return jnp.where((lanes == 0) | (lanes == BLOCK - 1), moved, 0.0)


def parts(x):
    high = x.astype(BF16)
    low = (x - high.astype(F32)).astype(BF16)
    return high, low


def contact(surface, near, normals, gap, mortar, owner, blocks, live, lhs, prod):
    tile = lax.axis_index("gy")
    count = lax.axis_size("gy")
    partner = lax.rem(tile + count // 2, count)
    which = lax.rem(owner - partner + 1 + count, count)
    index = jnp.broadcast_to(which * ROWS_DEV + blocks, (ROWS_DEV, 256))
    onehot = jnp.where(index == iota((ROWS_DEV, 256), 1), 1.0, 0.0).astype(BF16)[:, :SURF]
    columns = []
    for half in range(2):
        for c in range(3):
            columns.append(jnp.concatenate([parts(near[e][c])[half] for e in range(3)], axis=0))
    table = jnp.concatenate(columns, axis=1)
    masters = jnp.dot(onehot, table, preferred_element_type=F32)
    lhs[...] = jnp.zeros(lhs.shape, F32)
    for j in range(6):
        lhs[pl.ds(j, ROWS_DEV, stride=8), :] = masters[:, j * BLOCK : (j + 1) * BLOCK]

    def project(r, _):
        at = pl.ds(pl.multiple_of(r * 8, 8), 8)
        block = mortar[pl.ds(pl.multiple_of(r * BLOCK, BLOCK), BLOCK), :]
        prod[at, :] = lax.dot_general(
            lhs[at, :].astype(BF16), block, (((1,), (1,)), ((), ())), preferred_element_type=F32
        )
        return 0

    lax.fori_loop(0, ROWS_DEV, project, 0, unroll=16)
    opening = gap
    for c in range(3):
        projected = (
            prod[pl.ds(c, ROWS_DEV, stride=8), :] + prod[pl.ds(c + 3, ROWS_DEV, stride=8), :]
        )
        opening = opening + normals[c] * (surface[c] - projected)
    alive = iota((ROWS_DEV, BLOCK), 0) < live
    pressure = jnp.where(alive, PENALTY * jnp.maximum(-opening, 0.0), 0.0)
    slave = [pressure * normals[c] for c in range(3)]
    for c in range(3):
        high, low = parts(slave[c])
        lhs[pl.ds(c, ROWS_DEV, stride=8), :] = high.astype(F32)
        lhs[pl.ds(c + 3, ROWS_DEV, stride=8), :] = low.astype(F32)

    def react(r, _):
        at = pl.ds(pl.multiple_of(r * 8, 8), 8)
        block = mortar[pl.ds(pl.multiple_of(r * BLOCK, BLOCK), BLOCK), :]
        prod[at, :] = jnp.dot(lhs[at, :].astype(BF16), block, preferred_element_type=F32)
        return 0

    lax.fori_loop(0, ROWS_DEV, react, 0, unroll=16)
    raw = [
        -(prod[pl.ds(c, ROWS_DEV, stride=8), :] + prod[pl.ds(c + 3, ROWS_DEV, stride=8), :])
        for c in range(3)
    ]
    return slave, raw


def place_table(owner, blocks):
    place = jnp.broadcast_to((owner * ROWS_DEV + blocks).astype(F32), (ROWS_DEV, BLOCK))
    diagonal = iota((ROWS_DEV, BLOCK), 0) == iota((ROWS_DEV, BLOCK), 1)
    line = jnp.sum(jnp.where(diagonal, place, 0.0), axis=0, keepdims=True)
    return jnp.where(iota((1, BLOCK), 1) < ROWS_DEV, line, -1.0)


def collected(raws):
    count = lax.axis_size("gy")
    partner = lax.rem(lax.axis_index("gy") + count // 2, count)
    wanted = (iota((ROWS_DEV, BLOCK), 0) + partner * ROWS_DEV).astype(F32)
    onehot = jnp.concatenate(
        [
            jnp.where(wanted == jnp.broadcast_to(table, (ROWS_DEV, BLOCK)), 1.0, 0.0).astype(BF16)[
                :, :ROWS_DEV
            ]
            for _, table in raws
        ],
        axis=1,
    )
    columns = []
    for half in range(2):
        for c in range(3):
            columns.append(jnp.concatenate([parts(raw[c])[half] for raw, _ in raws], axis=0))
    result = jnp.dot(onehot, jnp.concatenate(columns, axis=1), preferred_element_type=F32)
    return [
        result[:, c * BLOCK : (c + 1) * BLOCK] + result[:, (c + 3) * BLOCK : (c + 4) * BLOCK]
        for c in range(3)
    ]


def three(ref, start=0):
    return [ref[start + c * ROWS_DEV : start + (c + 1) * ROWS_DEV, :] for c in range(3)]


RAW = SURF + 8


def first_contact_kernel(
    surface, sent, left, right, above, below, first, last, v_hbm, normals, gap, mortar_hbm, owner,
    blocks, live, raw_out, u_out, v_out, ring_out, rows_out, mortar, v, lhs, prod, sems,
):
    load = pltpu.make_async_copy(mortar_hbm, mortar, sems.at[0])
    load.start()
    load_v = [
        pltpu.make_async_copy(
            v_hbm.at[c * DEPTH], v.at[pl.ds(c * ROWS_DEV, ROWS_DEV), :], sems.at[1 + c]
        )
        for c in range(3)
    ]
    for each in load_v:
        each.start()
    at = pl.ds(SURF, STRIP)
    ring, _ = column_ring(sent[at, :], left[at, :], right[at, :], None)
    ring_out[...] = ring
    top, bottom = row_rings(
        first[0:PLANES, :], last[0:PLANES, :], above[0:PLANES, :], below[0:PLANES, :],
        last[PLANES:64, :], above[PLANES:64, :],
    )
    for c in range(3):
        rows_out[c * DEPTH : (c + 1) * DEPTH, :] = top[c]
        rows_out[PLANES + c * DEPTH : PLANES + (c + 1) * DEPTH, :] = bottom[c]
    load.wait()
    for each in load_v:
        each.wait()
    slave, raw = contact(
        three(surface), [three(left), three(sent), three(right)], three(normals), gap[...], mortar,
        owner[...], blocks[...], live[0, 0], lhs, prod,
    )
    raw_out[SURF:RAW, :] = jnp.broadcast_to(place_table(owner[...], blocks[...]), (8, BLOCK))
    sub = iota((ROWS_DEV, BLOCK), 0)
    for c in range(3):
        here = slice(c * ROWS_DEV, (c + 1) * ROWS_DEV)
        raw_out[here, :] = raw[c]
        new = v[here, :] + from_strip(ring, c * DEPTH) + TIME_STEP * slave[c]
        new = new + jnp.where(sub == 0, jnp.broadcast_to(top[c][0:1], sub.shape), 0.0)
        new = new + jnp.where(
            sub == ROWS_DEV - 1, jnp.broadcast_to(bottom[c][0:1], sub.shape), 0.0
        )
        v_out[here, :] = new
        u_out[here, :] = surface[here, :] + TIME_STEP * new


CONTACT_SCRATCH = [
    pltpu.VMEM((ROWS_DEV * 8, BLOCK), F32),
    pltpu.VMEM((ROWS_DEV * 8, BLOCK), F32),
]


def first_contact(*args):
    return call(
        first_contact_kernel,
        (out(RAW), out(SURF), out(SURF), out(ROWS_DEV), out(2 * PLANES)),
        [VMEM] * 8 + [ANY, VMEM, VMEM, ANY, VMEM, VMEM, SMEM],
        (VMEM,) * 5,
        [pltpu.VMEM((ROWS_DEV * BLOCK, BLOCK), BF16), pltpu.VMEM((SURF, BLOCK), F32)]
        + CONTACT_SCRATCH
        + [pltpu.SemaphoreType.DMA((4,))],
        args,
        4_000_000,
        4_000_000,
    )


def update_kernel(
    u, v, ring, rows, surface, surface_v, u_out, v_out, strip, first, last
):
    strength = ring[...]
    sub = iota((ROWS_DEV, BLOCK), 0)
    for c in range(3):
        u_out[c * DEPTH, :, :] = surface[c * ROWS_DEV : (c + 1) * ROWS_DEV, :]
        v_out[c * DEPTH, :, :] = surface_v[c * ROWS_DEV : (c + 1) * ROWS_DEV, :]

    def layer(k, held):
        for c in range(3):
            plane = c * DEPTH + k
            new = v[plane, :, :] + from_strip(strength, plane)
            new = new + jnp.where(sub == 0, jnp.broadcast_to(rows[pl.ds(plane, 1), :], sub.shape), 0.0)
            new = new + jnp.where(
                sub == ROWS_DEV - 1,
                jnp.broadcast_to(rows[pl.ds(PLANES + plane, 1), :], sub.shape),
                0.0,
            )
            moved = u[plane, :, :] + TIME_STEP * new
            v_out[plane, :, :] = new
            u_out[plane, :, :] = moved
            first[pl.ds(plane, 1), :] = moved[0:1]
            last[pl.ds(plane, 1), :] = moved[ROWS_DEV - 1 : ROWS_DEV]
            held = put_column(held, moved, plane)
        return held

    zero = jnp.zeros((ROWS_DEV, BLOCK), F32)
    strip[0:ROWS_DEV, :] = lax.fori_loop(1, DEPTH, layer, zero)
    strip[ROWS_DEV:STRIP, :] = jnp.zeros((STRIP - ROWS_DEV, BLOCK), F32)
    for ref in (first, last):
        for c in range(3):
            ref[c * DEPTH : c * DEPTH + 1, :] = jnp.zeros((1, BLOCK), F32)
        ref[PLANES:64, :] = jnp.zeros((64 - PLANES, BLOCK), F32)


def update(u, v, ring, rows, surface, surface_v):
    planes = jax.ShapeDtypeStruct((PLANES, ROWS_DEV, BLOCK), F32)
    return call(
        update_kernel,
        (planes, planes, out(STRIP), out(64), out(64)),
        [VMEM] * 6,
        (VMEM,) * 5,
        [],
        (u.reshape(-1, ROWS_DEV, BLOCK), v.reshape(-1, ROWS_DEV, BLOCK), ring, rows, surface, surface_v),
        10_000_000,
        6_000_000,
    )


def collect_kernel(partial, own, left, right, comb_out, u_out):
    comb = collected([(three(x), x[SURF : SURF + 1, :]) for x in (left, own, right)])
    for c in range(3):
        here = slice(c * ROWS_DEV, (c + 1) * ROWS_DEV)
        comb_out[here, :] = comb[c]
        u_out[here, :] = partial[here, :] + TIME_STEP * TIME_STEP * comb[c]


def collect(*args):
    return call(
        collect_kernel, (out(SURF), out(SURF)), [VMEM] * 4, (VMEM,) * 2, [], args, 1_000_000, 600_000
    )


def second_contact_kernel(
    partial, comb, center, left, right, strip, normals, gap, mortar_hbm, owner, blocks, live,
    raw_out, slave_out, mortar, lhs, prod, sems,
):
    load = pltpu.make_async_copy(mortar_hbm, mortar, sems.at[0])
    load.start()
    surface = [
        p + TIME_STEP * TIME_STEP * x for p, x in zip(three(partial), three(comb), strict=True)
    ]
    held = strip[0:ROWS_DEV, :]
    for c in range(3):
        held = put_column(held, surface[c], c * DEPTH)
    raw_out[RAW : RAW + ROWS_DEV, :] = held
    raw_out[RAW + ROWS_DEV : RAW + STRIP, :] = jnp.zeros((STRIP - ROWS_DEV, BLOCK), F32)
    load.wait()
    slave, raw = contact(
        surface, [three(left), three(center), three(right)], three(normals), gap[...], mortar,
        owner[...], blocks[...], live[0, 0], lhs, prod,
    )
    raw_out[SURF:RAW, :] = jnp.broadcast_to(place_table(owner[...], blocks[...]), (8, BLOCK))
    for c in range(3):
        here = slice(c * ROWS_DEV, (c + 1) * ROWS_DEV)
        raw_out[here, :] = raw[c]
        slave_out[here, :] = slave[c]


def second_contact(*args):
    return call(
        second_contact_kernel,
        (out(RAW + STRIP), out(SURF)),
        [VMEM] * 8 + [ANY, VMEM, VMEM, SMEM],
        (VMEM,) * 2,
        [pltpu.VMEM((ROWS_DEV * BLOCK, BLOCK), BF16)] + CONTACT_SCRATCH + [pltpu.SemaphoreType.DMA((1,))],
        args,
        4_000_000,
        4_000_000,
    )


def last_collect_kernel(
    own, left, right, first, last, partial, comb_own, comb_out, first_out, last_out
):
    comb = collected([(three(x), x[SURF : SURF + 1, :]) for x in (left, own, right)])
    for c in range(3):
        comb_out[c * ROWS_DEV : (c + 1) * ROWS_DEV, :] = comb[c]
    lanes = iota((8, BLOCK), 1)
    for ref, source, row in ((first_out, first, 0), (last_out, last, ROWS_DEV - 1)):
        ref[0:64, :] = source[...]
        for c in range(3):
            at = c * ROWS_DEV + row
            ref[c * DEPTH : c * DEPTH + 1, :] = (
                partial[at : at + 1, :] + TIME_STEP * TIME_STEP * comb_own[at : at + 1, :]
            )
        at = RAW + row // 8 * 8
        ref[64:72, :] = jnp.where(
            lanes % 2 == 1, roll(left[at : at + 8, :], 1, 1), roll(right[at : at + 8, :], -1, 1)
        )


def last_collect(*args):
    return call(
        last_collect_kernel,
        (out(SURF), out(STRIP), out(STRIP)),
        [VMEM] * 7,
        (VMEM,) * 3,
        [],
        args,
        1_000_000,
        800_000,
    )


def last_update_kernel(
    u, v, slave, comb_own, comb, sent, left, right, first, last, above, below,
    old_sent, old_left, old_above, old_last, u_out, v_out,
):
    at = pl.ds(RAW, STRIP)
    sub8 = iota((8, BLOCK), 0)
    lanes8 = iota((8, BLOCK), 1)
    top_corner = above[64 + 7 : 64 + 8, :]
    bottom_corner = below[64:65, :]

    def with_corners(strip, low, high):
        end = jnp.where(
            sub8 == 0,
            jnp.broadcast_to(low, sub8.shape),
            jnp.where(sub8 == 7, jnp.broadcast_to(high, sub8.shape), 0.0),
        )
        return jnp.concatenate([strip[0:ROWS_DEV], end], axis=0)

    own = with_corners(sent[at, :], ends_of_row(below[0:64, :]), ends_of_row(above[0:64, :]))
    odd8 = iota((1, BLOCK), 1) % 2 == 1
    corner_left = roll(jnp.broadcast_to(bottom_corner, (8, BLOCK)), -1, 1)[0:1]
    from_left = with_corners(
        left[at, :], corner_left, roll(jnp.broadcast_to(top_corner, (8, BLOCK)), -1, 1)[0:1]
    )
    from_right = with_corners(
        right[at, :],
        roll(jnp.broadcast_to(bottom_corner, (8, BLOCK)), 1, 1)[0:1],
        roll(jnp.broadcast_to(top_corner, (8, BLOCK)), 1, 1)[0:1],
    )
    old = pl.ds(SURF, STRIP)
    odd = iota((STRIP, BLOCK), 1) % 2 == 1
    moduli = jnp.where(odd, roll(old_left[old, :], 1, 1), old_sent[old, :])
    ring, _ = column_ring(own, from_left, from_right, moduli)
    top, bottom = row_rings(
        first[0:PLANES, :], last[0:PLANES, :], above[0:PLANES, :], below[0:PLANES, :],
        old_last[PLANES:64, :], old_above[PLANES:64, :],
    )
    sub = iota((ROWS_DEV, BLOCK), 0)
    for k in range(DEPTH):
        for c in range(3):
            plane = c * DEPTH + k
            new = v[plane, :, :] + from_strip(ring, plane)
            new = new + jnp.where(
                sub == 0, jnp.broadcast_to(top[c][k : k + 1], sub.shape), 0.0
            )
            new = new + jnp.where(
                sub == ROWS_DEV - 1, jnp.broadcast_to(bottom[c][k : k + 1], sub.shape), 0.0
            )
            old_u = u[plane, :, :]
            if k == 0:
                here = slice(c * ROWS_DEV, (c + 1) * ROWS_DEV)
                new = new + TIME_STEP * (slave[here, :] + comb[here, :])
                old_u = old_u + TIME_STEP * TIME_STEP * comb_own[here, :]
            v_out[plane, :, :] = new
            u_out[plane, :, :] = old_u + TIME_STEP * new


def last_update(*args):
    planes = jax.ShapeDtypeStruct((PLANES, ROWS_DEV, BLOCK), F32)
    return call(
        last_update_kernel,
        (planes, planes),
        [VMEM] * 16,
        (VMEM,) * 2,
        [],
        args,
        10_000_000,
        6_000_000,
    )


def moved(x, axis, by):
    count = lax.axis_size(axis)
    return lax.ppermute(x, axis, [(i, (i + by) % count) for i in range(count)])


def local(displacement, velocity, shear, normals, gap_zero, mortar, owner, blocks, live_rows):
    half = lax.axis_size("gy") // 2
    flat_normals = normals.reshape(SURF, BLOCK)
    flat_mortar = mortar.reshape(ROWS_DEV * BLOCK, BLOCK)
    pairing = (flat_normals, gap_zero, flat_mortar, owner, blocks, live_rows)

    surface, first, last = pack(displacement, shear)
    opposite = moved(surface, "gy", half)
    above = moved(last, "gx", 1)
    below = moved(first, "gx", -1)
    strip = strips(displacement, shear)

    sent = message(opposite, above, below, strip)
    left = moved(sent, "gy", 1)
    right = moved(sent, "gy", -1)
    forced = interior_forces(displacement, velocity, shear)

    raw, part_u, part_v, ring, rows = first_contact(
        surface, sent, left, right, above, below, first, last,
        forced.reshape(PLANES, ROWS_DEV, BLOCK), *pairing,
    )
    part_opposite = moved(part_u, "gy", half)
    raw_left = moved(raw, "gy", 1)
    raw_right = moved(raw, "gy", -1)
    u, v, strip, first2, last2 = update(displacement, forced, ring, rows, part_u, part_v)

    comb, center = collect(part_opposite, raw, raw_left, raw_right)
    left2 = moved(center, "gy", 1)
    right2 = moved(center, "gy", -1)
    comb_own = moved(comb, "gy", half)

    raw, slave = second_contact(part_u, comb_own, center, left2, right2, strip, *pairing)
    raw_left = moved(raw, "gy", 1)
    raw_right = moved(raw, "gy", -1)
    forced = interior_forces(u, v, shear, comb_own)

    comb, first2, last2 = last_collect(raw, raw_left, raw_right, first2, last2, part_u, comb_own)
    comb_last = moved(comb, "gy", half)
    above2 = moved(last2, "gx", 1)
    below2 = moved(first2, "gx", -1)
    u, v = last_update(
        u, forced.reshape(PLANES, ROWS_DEV, BLOCK), slave, comb_own, comb_last, raw, raw_left,
        raw_right, first2, last2, above2, below2, sent, left, above, last,
    )
    shape = displacement.shape
    return u.reshape(shape), v.reshape(shape)


def solution(mesh):
    wide = P(None, None, "gx", "gy")
    in_specs = (
        wide,
        wide,
        P(None, "gx", "gy"),
        P(None, "gx", "gy"),
        P("gx", "gy"),
        P("gx", "gy", None, None),
        P("gx", "gy"),
        P("gx", "gy"),
        P("gx", "gy"),
    )
    return jax.shard_map(
        local, mesh=mesh, in_specs=in_specs, out_specs=(wide, wide), check_vma=False
    )
```

profile of v0, /device:TPU:0, one launch (start us, length us, event | category | flops | bytes accessed | tf_op | source)
XLA Modules:
  0.0 76.1 jit_solution(15798376649642202107)
XLA Ops:
  0.6 1.4 %copy-done = f32[3,16,64,128]{3,2,1,0:T(8,128)S(1)} copy-done((f32[3,16,64,128]{3,2,1,0:T(8,128)S(1)}, f32[3,16,64,128]{3,2,1,0:T(8,128)}, u32[]{:S(2)}) %copy-start) | copy-done | bytes 1572888
  2.0 1.0 %copy-done.3 = f32[15,64,128]{2,1,0:T(8,128)S(1)} copy-done((f32[15,64,128]{2,1,0:T(8,128)S(1)}, f32[15,64,128]{2,1,0:T(8,128)}, u32[]{:S(2)}) %copy-start.3) | copy-done | bytes 491544
  3.1 0.2 shard_map.105
  3.3 4.0 %collective-permute-start = (f32[192,128]{1,0:T(8,128)S(1)}, f32[192,128]{1,0:T(8,128)S(1)}, u32[]{:S(2)}, u32[]{:S(2)}) collective-permute-start(f32[192,128]{1,0:T(8,128)S(1)} %get-tuple-element.24.surface), channel_id=1, source_target_pairs={{0,8},{1,9},{2,10},{3,11},{4,12},{5,13},{6,14},{7,15},{8,0},{9,1},... | collective-permute-start | bytes 294920 | tf_op jit(solution)/shard_map/ppermute | solution.py:738
  7.4 5.5 %collective-permute-start.2 = (f32[64,128]{1,0:T(8,128)S(1)}, f32[64,128]{1,0:T(8,128)S(1)}, u32[]{:S(2)}, u32[]{:S(2)}) collective-permute-start(f32[64,128]{1,0:T(8,128)S(1)} %get-tuple-element.26.first), channel_id=1, source_target_pairs={{0,112},{16,0},{32,16},{48,32},{64,48},{80,64},{96,80},{112,96},{1... | collective-permute-start | bytes 98312 | tf_op jit(solution)/shard_map/ppermute | solution.py:738
  12.9 2.6 %shard_map.106.strip = f32[72,128]{1,0:T(8,128)S(1)} custom-call(f32[48,64,128]{2,1,0:T(8,128)S(1)} %bitcast.7, f32[15,64,128]{2,1,0:T(8,128)S(1)} %copy-done.3), custom_call_target="tpu_custom_call" | custom-call | flops 1000000 | bytes 2000000 | tf_op jit(solution)/shard_map/pallas_call | solution.py:37
  15.5 4.9 %collective-permute-done.1.above.old_above = f32[64,128]{1,0:T(8,128)S(1)} collective-permute-done((f32[64,128]{1,0:T(8,128)S(1)}, f32[64,128]{1,0:T(8,128)S(1)}, u32[]{:S(2)}, u32[]{:S(2)}) %collective-permute-start.1) | collective-permute-done | bytes 32800 | tf_op jit(solution)/shard_map/ppermute | solution.py:738
  20.4 0.1 shard_map.107.sent.old_sent
  20.6 0.5 collective-permute-start.3
  21.8 0.1 copy.11.owner
  21.8 0.1 copy.12.blocks
  22.0 1.4 %copy-done.5 = f32[3,16,64,128]{3,2,1,0:T(8,128)S(1)} copy-done((f32[3,16,64,128]{3,2,1,0:T(8,128)S(1)}, f32[3,16,64,128]{3,2,1,0:T(8,128)}, u32[]{:S(2)}) %copy-start.5) | copy-done | bytes 1572888
  23.4 6.0 %shard_map.104.v_hbm.v = f32[48,64,128]{2,1,0:T(8,128)S(1)} custom-call(f32[48,64,128]{2,1,0:T(8,128)S(1)} %bitcast.8, f32[48,64,128]{2,1,0:T(8,128)S(1)} %bitcast.12, f32[15,64,128]{2,1,0:T(8,128)S(1)} %copy-done.4), custom_call_target="tpu_custom_call" | custom-call | flops 30000000 | bytes 6000000 | tf_op jit(solution)/shard_map/pallas_call | solution.py:37
  29.4 3.9 %shard_map.108 = (f32[200,128]{1,0:T(8,128)S(1)}, f32[192,128]{1,0:T(8,128)S(1)}, f32[192,128]{1,0:T(8,128)S(1)}, f32[64,128]{1,0:T(8,128)S(1)}, f32[96,128]{1,0:T(8,128)S(1)}) custom-call(f32[192,128]{1,0:T(8,128)S(1)} %get-tuple-element.24.surface, f32[264,128]{1,0:T(8,128)S(1)} %shard_map.107.sent.old_sent, ...), custom_call_target="tpu_custom_call" | custom-call | flops 4000000 | bytes 4000000 | tf_op jit(solution)/shard_map/pallas_call | solution.py:37
  33.3 3.5 %collective-permute-start.7 = (f32[200,128]{1,0:T(8,128)S(1)}, f32[200,128]{1,0:T(8,128)S(1)}, u32[]{:S(2)}, u32[]{:S(2)}) collective-permute-start(f32[200,128]{1,0:T(8,128)S(1)} %get-tuple-element.33.own), channel_id=1, source_target_pairs={{0,15},{1,0},{2,1},{3,2},{4,3},{5,4},{6,5},{7,6},{8,7},{9,8},{10,9... | collective-permute-start | bytes 307208 | tf_op jit(solution)/shard_map/ppermute | solution.py:738
  36.8 7.1 %collective-permute-done.5.partial = f32[192,128]{1,0:T(8,128)S(1)} collective-permute-done((f32[192,128]{1,0:T(8,128)S(1)}, f32[192,128]{1,0:T(8,128)S(1)}, u32[]{:S(2)}, u32[]{:S(2)}) %collective-permute-start.5) | collective-permute-done | bytes 98336 | tf_op jit(solution)/shard_map/ppermute | solution.py:738
  44.0 0.2 shard_map.110
  44.3 0.1 collective-permute-start.8
  44.4 1.7 %collective-permute-start.10 = (f32[192,128]{1,0:T(8,128)S(1)}, f32[192,128]{1,0:T(8,128)S(1)}, u32[]{:S(2)}, u32[]{:S(2)}) collective-permute-start(f32[192,128]{1,0:T(8,128)S(1)} %get-tuple-element.35.center), channel_id=1, source_target_pairs={{0,15},{1,0},{2,1},{3,2},{4,3},{5,4},{6,5},{7,6},{8,7},{9,8},{10,9... | collective-permute-start | bytes 294920 | tf_op jit(solution)/shard_map/ppermute | solution.py:738
  46.1 2.6 %shard_map.109 = (f32[48,64,128]{2,1,0:T(8,128)S(1)}, f32[48,64,128]{2,1,0:T(8,128)S(1)}, f32[72,128]{1,0:T(8,128)S(1)}, f32[64,128]{1,0:T(8,128)S(1)}, f32[64,128]{1,0:T(8,128)S(1)}) custom-call(f32[48,64,128]{2,1,0:T(8,128)S(1)} %bitcast.9, f32[48,64,128]{2,1,0:T(8,128)S(1)} %shard_map.104.v_hbm.v, f32[64,128]{1,0:T(8,128)S(1)} %get-tuple-element.27.ring, ...), custom_call_target="tpu_custom_call" | custom-call | flops 10000000 | bytes 6000000 | tf_op jit(solution)/shard_map/pallas_call | solution.py:37
  48.7 3.2 %collective-permute-done.8.refs_3_.comb.comb_own = f32[192,128]{1,0:T(8,128)S(1)} collective-permute-done((f32[192,128]{1,0:T(8,128)S(1)}, f32[192,128]{1,0:T(8,128)S(1)}, u32[]{:S(2)}, u32[]{:S(2)}) %collective-permute-start.8) | collective-permute-done | bytes 98336 | tf_op jit(solution)/shard_map/ppermute | solution.py:738
  51.9 0.7 collective-permute-done.9.left
  52.6 3.2 %shard_map.112 = (f32[272,128]{1,0:T(8,128)S(1)}, f32[192,128]{1,0:T(8,128)S(1)}) custom-call(f32[192,128]{1,0:T(8,128)S(1)} %get-tuple-element.29.surface.partial, f32[192,128]{1,0:T(8,128)S(1)} %collective-permute-done.8.refs_3_.comb.comb_own, f32[192,128]{1,0:T(8,128)S(1)} %get-tuple-element.35.center, f32[192,128]{1,0:T(8,128)S(1)} %collective-permute-done.9.left, ...), custom_call_target="tpu_custom_call" | custom-call | flops 4000000 | bytes 4000000 | tf_op jit(solution)/shard_map/pallas_call | solution.py:37
  55.8 0.8 %collective-permute-start.12 = (f32[272,128]{1,0:T(8,128)S(1)}, f32[272,128]{1,0:T(8,128)S(1)}, u32[]{:S(2)}, u32[]{:S(2)}) collective-permute-start(f32[272,128]{1,0:T(8,128)S(1)} %get-tuple-element.38.own.sent), channel_id=1, source_target_pairs={{0,15},{1,0},{2,1},{3,2},{4,3},{5,4},{6,5},{7,6},{8,7},{9,8},{10,9... | collective-permute-start | bytes 417800 | tf_op jit(solution)/shard_map/ppermute | solution.py:738
  56.6 3.1 %collective-permute-done.12.right = f32[272,128]{1,0:T(8,128)S(1)} collective-permute-done((f32[272,128]{1,0:T(8,128)S(1)}, f32[272,128]{1,0:T(8,128)S(1)}, u32[]{:S(2)}, u32[]{:S(2)}) %collective-permute-start.12) | collective-permute-done | bytes 139296 | tf_op jit(solution)/shard_map/ppermute | solution.py:738
  59.8 3.4 %collective-permute-done.11.left = f32[272,128]{1,0:T(8,128)S(1)} collective-permute-done((f32[272,128]{1,0:T(8,128)S(1)}, f32[272,128]{1,0:T(8,128)S(1)}, u32[]{:S(2)}, u32[]{:S(2)}) %collective-permute-start.11) | collective-permute-done | bytes 139296 | tf_op jit(solution)/shard_map/ppermute | solution.py:738
  63.2 0.2 shard_map.113
  63.4 0.1 collective-permute-start.13
  63.5 0.8 %collective-permute-start.15 = (f32[72,128]{1,0:T(8,128)S(1)}, f32[72,128]{1,0:T(8,128)S(1)}, u32[]{:S(2)}, u32[]{:S(2)}) collective-permute-start(f32[72,128]{1,0:T(8,128)S(1)} %get-tuple-element.42.first), channel_id=1, source_target_pairs={{0,112},{16,0},{32,16},{48,32},{64,48},{80,64},{96,80},{112,96},{1... | collective-permute-start | bytes 110600 | tf_op jit(solution)/shard_map/ppermute | solution.py:738
  64.4 2.8 %collective-permute-start.14 = (f32[72,128]{1,0:T(8,128)S(1)}, f32[72,128]{1,0:T(8,128)S(1)}, u32[]{:S(2)}, u32[]{:S(2)}) collective-permute-start(f32[72,128]{1,0:T(8,128)S(1)} %get-tuple-element.43.last), channel_id=1, source_target_pairs={{0,16},{16,32},{32,48},{48,64},{64,80},{80,96},{96,112},{112,0},{1... | collective-permute-start | bytes 110600 | tf_op jit(solution)/shard_map/ppermute | solution.py:738
  67.1 6.0 %shard_map.111.v = f32[48,64,128]{2,1,0:T(8,128)S(1)} custom-call(f32[48,64,128]{2,1,0:T(8,128)S(1)} %get-tuple-element.31.refs_0_.u, f32[48,64,128]{2,1,0:T(8,128)S(1)} %get-tuple-element.32.refs_1_, f32[15,64,128]{2,1,0:T(8,128)S(1)} %copy-done.4, f32[192,128]{1,0:T(8,128)S(1)} %collective-permute-done.8.refs_3_.comb.comb_own), custom_call_target="tpu_custom_call" | custom-call | flops 30000000 | bytes 6000000 | tf_op jit(solution)/shard_map/pallas_call | solution.py:37
  73.2 3.0 %shard_map.114 = (f32[48,64,128]{2,1,0:T(8,128)}, f32[48,64,128]{2,1,0:T(8,128)}) custom-call(f32[48,64,128]{2,1,0:T(8,128)S(1)} %get-tuple-element.31.refs_0_.u, f32[48,64,128]{2,1,0:T(8,128)S(1)} %shard_map.111.v, f32[192,128]{1,0:T(8,128)S(1)} %get-tuple-element.37.slave, f32[192,128]{1,0:T(8,128)S(1)} %collective-permute-done.8.refs_3_.comb.comb_own, ...), custom_call_target="tpu_custom_call" | custom-call | flops 10000000 | bytes 6000000 | tf_op jit(solution)/shard_map/pallas_call | solution.py:37
  (33 shorter events, 0.2 us)
Async XLA Ops:
  0.6 1.4 %copy-start = (f32[3,16,64,128]{3,2,1,0:T(8,128)S(1)}, f32[3,16,64,128]{3,2,1,0:T(8,128)}, u32[]{:S(2)}) copy-start(f32[3,16,64,128]{3,2,1,0:T(8,128)} %param.9) | copy-start | bytes 4718596
  2.0 1.0 %copy-start.3 = (f32[15,64,128]{2,1,0:T(8,128)S(1)}, f32[15,64,128]{2,1,0:T(8,128)}, u32[]{:S(2)}) copy-start(f32[15,64,128]{2,1,0:T(8,128)} %refs_2_.3) | copy-start | bytes 1474564
  3.3 18.4 %copy-start.8 = (s32[64,1]{0,1:T(1,128)S(1)}, s32[64,1]{0,1:T(1,128)}, u32[]{:S(2)}) copy-start(s32[64,1]{0,1:T(1,128)} %param.15) | copy-start | bytes 772
  3.3 18.5 %copy-start.9 = (s32[64,1]{0,1:T(1,128)S(1)}, s32[64,1]{0,1:T(1,128)}, u32[]{:S(2)}) copy-start(s32[64,1]{0,1:T(1,128)} %param.16) | copy-start | bytes 772
  3.3 18.6 %copy-start.1 = (f32[3,16,64,128]{3,2,1,0:T(8,128)S(1)}, f32[3,16,64,128]{3,2,1,0:T(8,128)}, u32[]{:S(2)}) copy-start(f32[3,16,64,128]{3,2,1,0:T(8,128)} %param.9) | copy-start | bytes 4718596
  3.3 18.6 %copy-start.4 = (f32[15,64,128]{2,1,0:T(8,128)S(1)}, f32[15,64,128]{2,1,0:T(8,128)}, u32[]{:S(2)}) copy-start(f32[15,64,128]{2,1,0:T(8,128)} %refs_2_.3) | copy-start | bytes 1474564
  3.3 17.0 %collective-permute-start = (f32[192,128]{1,0:T(8,128)S(1)}, f32[192,128]{1,0:T(8,128)S(1)}, u32[]{:S(2)}, u32[]{:S(2)}) collective-permute-start(f32[192,128]{1,0:T(8,128)S(1)} %get-tuple-element.24.surface), channel_id=1, source_target_pairs={{0,8},{1,9},{2,10},{3,11},{4,12},{5,13},{6,14},{7,15},{8,0},{9,1},... | collective-permute-start | bytes 294920 | tf_op jit(solution)/shard_map/ppermute | solution.py:738
  7.4 8.1 %collective-permute-start.2 = (f32[64,128]{1,0:T(8,128)S(1)}, f32[64,128]{1,0:T(8,128)S(1)}, u32[]{:S(2)}, u32[]{:S(2)}) collective-permute-start(f32[64,128]{1,0:T(8,128)S(1)} %get-tuple-element.26.first), channel_id=1, source_target_pairs={{0,112},{16,0},{32,16},{48,32},{64,48},{80,64},{96,80},{112,96},{1... | collective-permute-start | bytes 98312 | tf_op jit(solution)/shard_map/ppermute | solution.py:738
  12.9 7.5 %collective-permute-start.1 = (f32[64,128]{1,0:T(8,128)S(1)}, f32[64,128]{1,0:T(8,128)S(1)}, u32[]{:S(2)}, u32[]{:S(2)}) collective-permute-start(f32[64,128]{1,0:T(8,128)S(1)} %get-tuple-element.25.last.old_last), channel_id=1, source_target_pairs={{0,16},{16,32},{32,48},{48,64},{64,80},{80,96},{96,112},{112,0},{1... | collective-permute-start | bytes 98312 | tf_op jit(solution)/shard_map/ppermute | solution.py:738
  20.5 8.8 %collective-permute-start.4 = (f32[264,128]{1,0:T(8,128)S(1)}, f32[264,128]{1,0:T(8,128)S(1)}, u32[]{:S(2)}, u32[]{:S(2)}) collective-permute-start(f32[264,128]{1,0:T(8,128)S(1)} %shard_map.107.sent.old_sent), channel_id=1, source_target_pairs={{0,15},{1,0},{2,1},{3,2},{4,3},{5,4},{6,5},{7,6},{8,7},{9,8},{10,9... | collective-permute-start | bytes 405512 | tf_op jit(solution)/shard_map/ppermute | solution.py:738
  20.6 8.8 %collective-permute-start.3 = (f32[264,128]{1,0:T(8,128)S(1)}, f32[264,128]{1,0:T(8,128)S(1)}, u32[]{:S(2)}, u32[]{:S(2)}) collective-permute-start(f32[264,128]{1,0:T(8,128)S(1)} %shard_map.107.sent.old_sent), channel_id=1, source_target_pairs={{0,1},{1,2},{2,3},{3,4},{4,5},{5,6},{6,7},{7,8},{8,9},{9,10},{10,1... | collective-permute-start | bytes 405512 | tf_op jit(solution)/shard_map/ppermute | solution.py:738
  22.0 1.4 %copy-start.5 = (f32[3,16,64,128]{3,2,1,0:T(8,128)S(1)}, f32[3,16,64,128]{3,2,1,0:T(8,128)}, u32[]{:S(2)}) copy-start(f32[3,16,64,128]{3,2,1,0:T(8,128)} %param.10) | copy-start | bytes 4718596
  23.4 6.0 %copy-start.2 = (bf16[64,1,128,128]{3,2,1,0:T(8,128)(2,1)S(1)}, bf16[64,1,128,128]{3,2,1,0:T(8,128)(2,1)}, u32[]{:S(2)}) copy-start(bf16[64,1,128,128]{3,2,1,0:T(8,128)(2,1)} %param.14) | copy-start | bytes 6291460
  23.4 6.0 %copy-start.6 = (f32[3,64,128]{2,1,0:T(8,128)S(1)}, f32[3,64,128]{2,1,0:T(8,128)}, u32[]{:S(2)}) copy-start(f32[3,64,128]{2,1,0:T(8,128)} %param.12) | copy-start | bytes 294916
  23.4 6.0 %copy-start.7 = (f32[64,128]{1,0:T(8,128)S(1)}, f32[64,128]{1,0:T(8,128)}, u32[]{:S(2)}) copy-start(f32[64,128]{1,0:T(8,128)} %gap.3) | copy-start | bytes 98308
  33.3 10.7 %collective-permute-start.7 = (f32[200,128]{1,0:T(8,128)S(1)}, f32[200,128]{1,0:T(8,128)S(1)}, u32[]{:S(2)}, u32[]{:S(2)}) collective-permute-start(f32[200,128]{1,0:T(8,128)S(1)} %get-tuple-element.33.own), channel_id=1, source_target_pairs={{0,15},{1,0},{2,1},{3,2},{4,3},{5,4},{6,5},{7,6},{8,7},{9,8},{10,9... | collective-permute-start | bytes 307208 | tf_op jit(solution)/shard_map/ppermute | solution.py:738
  36.8 7.2 %collective-permute-start.6 = (f32[200,128]{1,0:T(8,128)S(1)}, f32[200,128]{1,0:T(8,128)S(1)}, u32[]{:S(2)}, u32[]{:S(2)}) collective-permute-start(f32[200,128]{1,0:T(8,128)S(1)} %get-tuple-element.33.own), channel_id=1, source_target_pairs={{0,1},{1,2},{2,3},{3,4},{4,5},{5,6},{6,7},{7,8},{8,9},{9,10},{10,1... | collective-permute-start | bytes 307208 | tf_op jit(solution)/shard_map/ppermute | solution.py:738
  36.8 7.1 %collective-permute-start.5 = (f32[192,128]{1,0:T(8,128)S(1)}, f32[192,128]{1,0:T(8,128)S(1)}, u32[]{:S(2)}, u32[]{:S(2)}) collective-permute-start(f32[192,128]{1,0:T(8,128)S(1)} %get-tuple-element.29.surface.partial), channel_id=1, source_target_pairs={{0,8},{1,9},{2,10},{3,11},{4,12},{5,13},{6,14},{7,15},{8,0},{9,1},... | collective-permute-start | bytes 294920 | tf_op jit(solution)/shard_map/ppermute | solution.py:738
  44.3 7.6 %collective-permute-start.8 = (f32[192,128]{1,0:T(8,128)S(1)}, f32[192,128]{1,0:T(8,128)S(1)}, u32[]{:S(2)}, u32[]{:S(2)}) collective-permute-start(f32[192,128]{1,0:T(8,128)S(1)} %get-tuple-element.34), channel_id=1, source_target_pairs={{0,8},{1,9},{2,10},{3,11},{4,12},{5,13},{6,14},{7,15},{8,0},{9,1},... | collective-permute-start | bytes 294920 | tf_op jit(solution)/shard_map/ppermute | solution.py:738
  44.4 7.5 %collective-permute-start.10 = (f32[192,128]{1,0:T(8,128)S(1)}, f32[192,128]{1,0:T(8,128)S(1)}, u32[]{:S(2)}, u32[]{:S(2)}) collective-permute-start(f32[192,128]{1,0:T(8,128)S(1)} %get-tuple-element.35.center), channel_id=1, source_target_pairs={{0,15},{1,0},{2,1},{3,2},{4,3},{5,4},{6,5},{7,6},{8,7},{9,8},{10,9... | collective-permute-start | bytes 294920 | tf_op jit(solution)/shard_map/ppermute | solution.py:738
  46.1 6.5 %collective-permute-start.9 = (f32[192,128]{1,0:T(8,128)S(1)}, f32[192,128]{1,0:T(8,128)S(1)}, u32[]{:S(2)}, u32[]{:S(2)}) collective-permute-start(f32[192,128]{1,0:T(8,128)S(1)} %get-tuple-element.35.center), channel_id=1, source_target_pairs={{0,1},{1,2},{2,3},{3,4},{4,5},{5,6},{6,7},{7,8},{8,9},{9,10},{10,1... | collective-permute-start | bytes 294920 | tf_op jit(solution)/shard_map/ppermute | solution.py:738
  55.8 4.0 %collective-permute-start.12 = (f32[272,128]{1,0:T(8,128)S(1)}, f32[272,128]{1,0:T(8,128)S(1)}, u32[]{:S(2)}, u32[]{:S(2)}) collective-permute-start(f32[272,128]{1,0:T(8,128)S(1)} %get-tuple-element.38.own.sent), channel_id=1, source_target_pairs={{0,15},{1,0},{2,1},{3,2},{4,3},{5,4},{6,5},{7,6},{8,7},{9,8},{10,9... | collective-permute-start | bytes 417800 | tf_op jit(solution)/shard_map/ppermute | solution.py:738
  56.6 6.6 %collective-permute-start.11 = (f32[272,128]{1,0:T(8,128)S(1)}, f32[272,128]{1,0:T(8,128)S(1)}, u32[]{:S(2)}, u32[]{:S(2)}) collective-permute-start(f32[272,128]{1,0:T(8,128)S(1)} %get-tuple-element.38.own.sent), channel_id=1, source_target_pairs={{0,1},{1,2},{2,3},{3,4},{4,5},{5,6},{6,7},{7,8},{8,9},{9,10},{10,1... | collective-permute-start | bytes 417800 | tf_op jit(solution)/shard_map/ppermute | solution.py:738
  63.4 9.7 %collective-permute-start.13 = (f32[192,128]{1,0:T(8,128)S(1)}, f32[192,128]{1,0:T(8,128)S(1)}, u32[]{:S(2)}, u32[]{:S(2)}) collective-permute-start(f32[192,128]{1,0:T(8,128)S(1)} %get-tuple-element.41), channel_id=1, source_target_pairs={{0,8},{1,9},{2,10},{3,11},{4,12},{5,13},{6,14},{7,15},{8,0},{9,1},... | collective-permute-start | bytes 294920 | tf_op jit(solution)/shard_map/ppermute | solution.py:738
  63.5 9.6 %collective-permute-start.15 = (f32[72,128]{1,0:T(8,128)S(1)}, f32[72,128]{1,0:T(8,128)S(1)}, u32[]{:S(2)}, u32[]{:S(2)}) collective-permute-start(f32[72,128]{1,0:T(8,128)S(1)} %get-tuple-element.42.first), channel_id=1, source_target_pairs={{0,112},{16,0},{32,16},{48,32},{64,48},{80,64},{96,80},{112,96},{1... | collective-permute-start | bytes 110600 | tf_op jit(solution)/shard_map/ppermute | solution.py:738
  64.4 8.8 %collective-permute-start.14 = (f32[72,128]{1,0:T(8,128)S(1)}, f32[72,128]{1,0:T(8,128)S(1)}, u32[]{:S(2)}, u32[]{:S(2)}) collective-permute-start(f32[72,128]{1,0:T(8,128)S(1)} %get-tuple-element.43.last), channel_id=1, source_target_pairs={{0,16},{16,32},{32,48},{48,64},{64,80},{80,96},{96,112},{112,0},{1... | collective-permute-start | bytes 110600 | tf_op jit(solution)/shard_map/ppermute | solution.py:738
where the time goes:
time: 76.4 us; the launch traced here: 76.1 us
  Pallas kernels  28.1 us (37%)
  waiting for transfers between devices  22.6 us (30%)
  starting transfers between devices  19.9 us (26%)
  local copies, waits for them, and re-layouts  4.06 us (5%)
  between operations  1.5 us (2%)
    pallas_call x11, Pallas kernels, call(): pl.pallas_call(kernel, out_shape=out_shape, in_specs=in_specs, out_specs=...  28.1 us
    ppermute x16, waiting for transfers between devices, moved(): return lax.ppermute(x, axis, [(i, (i + by) % count) for i in range(count)])  22.6 us
    ppermute x16, starting transfers between devices, moved(): return lax.ppermute(x, axis, [(i, (i + by) % count) for i in range(count)])  19.9 us
    unnamed x22, local copies, waits for them, and re-layouts  4.06 us
  transfers between devices with their start and end apart: 16, of which 7 were waited for; matrix products, arithmetic and copies ran while one was open for 0% of the time, Pallas kernels for 23%

commit v1 on v0

--- a/solution.py
+++ b/solution.py
@@ -33,14 +33,14 @@
     return pltpu.roll(x, by % x.shape[dim], dim)
 
 
-def call(kernel, out_shape, in_specs, out_specs, scratch, args, flops, bytes_accessed):
+def call(kernel, out_shape, in_specs, out_specs, scratch, args, flops, bytes_accessed, limit=16):
     return pl.pallas_call(
         kernel,
         out_shape=out_shape,
         in_specs=in_specs,
         out_specs=out_specs,
         scratch_shapes=scratch,
-        compiler_params=pltpu.CompilerParams(vmem_limit_bytes=40 * 2**20),
+        compiler_params=pltpu.CompilerParams(vmem_limit_bytes=limit * 2**20),
         cost_estimate=pl.CostEstimate(
             flops=flops, bytes_accessed=bytes_accessed, transcendentals=0
         ),
@@ -74,36 +74,26 @@
     return [[linear * g[c][d] + bulk * cof[c][d] for d in range(3)] for c in range(3)]
 
 
-def dead_lane(tile):
-    return lax.axis_size("gy") * BLOCK // 2 + BLOCK // 2 - 1 - tile * BLOCK
-
-
-def forces_kernel(patched, *refs):
-    if patched:
-        u_hbm, v_hbm, shear_hbm, comb, v_out, u, v, shear, z, mask, sems = refs
+def forces_kernel(layers, later, *refs):
+    start, end = layers
+    count = end - start
+    first_face, last_face = max(start - 1, 0), min(end, DEPTH - 1)
+    u, shear, *refs = refs
+    if later:
+        v, comb, *refs = refs
+    if later and start == 0:
+        v_out, z, mask, comb_home = refs
+        comb_home[:, ROWS_DEV:STRIP, :] = jnp.zeros((3, STRIP - ROWS_DEV, BLOCK), F32)
+        for c in range(3):
+            comb_home[c, 0:ROWS_DEV, :] = comb[c * ROWS_DEV : (c + 1) * ROWS_DEV, :]
+        comb = comb_home
     else:
-        u_hbm, v_hbm, shear_hbm, v_out, u, v, shear, z, mask, sems = refs
-    copies = [
-        pltpu.make_async_copy(u_hbm, u.at[:, 0:ROWS_DEV, :], sems.at[0]),
-        pltpu.make_async_copy(v_hbm, v, sems.at[1]),
-        pltpu.make_async_copy(shear_hbm, shear, sems.at[2]),
-    ]
-    for copy in copies:
-        copy.start()
-    zero = jnp.zeros((PLANES, 8, BLOCK), F32)
-    u[:, ROWS_DEV:STRIP, :] = zero
-    z[:, 0:8, :] = zero
+        v_out, z, mask = refs
+    z[:, 0:8, :] = jnp.zeros((3 * count, 8, BLOCK), F32)
     lanes = iota((ROWS_DEV, BLOCK), 1)
     rows = iota((ROWS_DEV, BLOCK), 0)
-    keep = (lanes < BLOCK - 1) & (rows < ROWS_DEV - 1) & (lanes != dead_lane(lax.axis_index("gy")))
+    keep = (lanes < BLOCK - 1) & (rows < ROWS_DEV - 1)
     mask[...] = keep.astype(F32)
-    for copy in copies:
-        copy.wait()
-    if patched:
-        for c in range(3):
-            at = pl.ds(c * ROWS_DEV, ROWS_DEV)
-            u[c * DEPTH, 0:ROWS_DEV, :] += TIME_STEP * TIME_STEP * comb[at, :]
-            v[c * DEPTH, :, :] += TIME_STEP * comb[at, :]
 
     def chunk(i, _):
         r0 = pl.multiple_of(i * 8, 8)
@@ -115,6 +105,9 @@
             for c in range(3):
                 a = u[c * DEPTH + k, here, :]
                 b = u[c * DEPTH + k, pl.ds(r0 + 1, 8), :]
+                if later and k == 0:
+                    a = a + TIME_STEP * TIME_STEP * comb[c, here, :]
+                    b = b + TIME_STEP * TIME_STEP * comb[c, pl.ds(r0 + 1, 8), :]
                 p = a + b
                 q = b - a
                 p_next = roll(p, -1, 1)
@@ -122,94 +115,92 @@
                 result.append((p + p_next, q + q_next, p_next - p))
             return result
 
-        low = face(0)
+        low = face(first_face)
         before = None
-        for k in range(DEPTH):
+        for k in range(first_face, end):
             if k < DEPTH - 1:
                 high = face(k + 1)
                 now = stress(low, high, shear[k, here, :] * exists)
                 low = high
             else:
                 now = None
-            for c in range(3):
-                if before is None:
-                    d, e, g = now[c]
-                elif now is None:
-                    d, e, g = -before[c][0], before[c][1], before[c][2]
-                else:
-                    d = now[c][0] - before[c][0]
-                    e = now[c][1] + before[c][1]
-                    g = now[c][2] + before[c][2]
-                dg = (d + g) + roll(d - g, 1, 1)
-                ee = e + roll(e, 1, 1)
-                plane = c * DEPTH + k
-                z[plane, pl.ds(r0 + 8, 8), :] = dg - ee
-                total = (dg + ee) + z[plane, pl.ds(r0 + 7, 8), :]
-                v_out[plane, here, :] = DAMPING * v[plane, here, :] + total
+            if k >= start:
+                for c in range(3):
+                    if before is None:
+                        d, e, g = now[c]
+                    elif now is None:
+                        d, e, g = -before[c][0], before[c][1], before[c][2]
+                    else:
+                        d = now[c][0] - before[c][0]
+                        e = now[c][1] + before[c][1]
+                        g = now[c][2] + before[c][2]
+                    dg = (d + g) + roll(d - g, 1, 1)
+                    ee = e + roll(e, 1, 1)
+                    plane = c * count + k - start
+                    z[plane, pl.ds(r0 + 8, 8), :] = dg - ee
+                    total = (dg + ee) + z[plane, pl.ds(r0 + 7, 8), :]
+                    if later:
+                        total = total + DAMPING * v[c * DEPTH + k, here, :]
+                        if k == 0:
+                            total = total + DAMPING * TIME_STEP * comb[c, here, :]
+                    v_out[plane, here, :] = total
             before = now
         return 0
 
     lax.fori_loop(0, ROWS_DEV // 8, chunk, 0)
 
 
-def interior_forces(u, v, shear, comb=None):
-    args = [x.reshape(-1, ROWS_DEV, BLOCK) for x in (u, v, shear)]
-    specs = [ANY, ANY, ANY]
-    if comb is not None:
-        args.append(comb)
-        specs.append(VMEM)
-    return call(
-        functools.partial(forces_kernel, comb is not None),
-        jax.ShapeDtypeStruct((PLANES, ROWS_DEV, BLOCK), F32),
-        specs,
+HALVES = ((0, DEPTH // 2), (DEPTH // 2, DEPTH))
+
+
+def planes(count, rows=ROWS_DEV):
+    return jax.ShapeDtypeStruct((count, rows, BLOCK), F32)
+
+
+def inner_forces(layers, u, shear, v=None, comb=None):
+    start, end = layers
+    count = end - start
+    args = [u, shear]
+    scratch = [
+        pltpu.VMEM((3 * count, STRIP, BLOCK), F32),
+        pltpu.VMEM((ROWS_DEV, BLOCK), F32),
+    ]
+    if v is not None:
+        args += [v, comb]
+        if start == 0:
+            scratch.append(pltpu.VMEM((3, STRIP, BLOCK), F32))
+    return call(
+        functools.partial(forces_kernel, layers, v is not None),
+        planes(3 * count),
+        [VMEM] * len(args),
         VMEM,
-        [
-            pltpu.VMEM((PLANES, STRIP, BLOCK), F32),
-            pltpu.VMEM((PLANES, ROWS_DEV, BLOCK), F32),
-            pltpu.VMEM((DEPTH - 1, ROWS_DEV, BLOCK), F32),
-            pltpu.VMEM((PLANES, STRIP, BLOCK), F32),
-            pltpu.VMEM((ROWS_DEV, BLOCK), F32),
-            pltpu.SemaphoreType.DMA((3,)),
-        ],
+        scratch,
         args,
-        30_000_000,
-        6_000_000,
-    ).reshape(PLANES * ROWS_DEV, BLOCK)
-
-
-def pack_kernel(u, shear, surface, first, last, sems):
-    copies = []
-    for c in range(3):
-        copies.append(
-            pltpu.make_async_copy(
-                u.at[c * DEPTH], surface.at[pl.ds(c * ROWS_DEV, ROWS_DEV), :], sems.at[c]
-            )
-        )
-    copies.append(pltpu.make_async_copy(u.at[:, 0, :], first.at[0:PLANES, :], sems.at[3]))
-    copies.append(
-        pltpu.make_async_copy(u.at[:, ROWS_DEV - 1, :], last.at[0:PLANES, :], sems.at[4])
-    )
-    copies.append(
-        pltpu.make_async_copy(
-            shear.at[:, ROWS_DEV - 1, :], last.at[PLANES : PLANES + DEPTH - 1, :], sems.at[5]
-        )
-    )
-    for copy in copies:
-        copy.start()
-    first[PLANES : PLANES + DEPTH, :] = jnp.zeros((DEPTH, BLOCK), F32)
-    last[PLANES + DEPTH - 1 : PLANES + DEPTH, :] = jnp.zeros((1, BLOCK), F32)
-    for copy in copies:
-        copy.wait()
-
-
-def pack(u, shear):
+        15_000_000,
+        3_000_000,
+    )
+
+
+def pack_kernel(u, shear, surface, first, last):
+    first[PLANES:64, :] = jnp.zeros((64 - PLANES, BLOCK), F32)
+    last[63:64, :] = jnp.zeros((1, BLOCK), F32)
+    for c in range(3):
+        surface[c * ROWS_DEV : (c + 1) * ROWS_DEV, :] = u[c * DEPTH, 0:ROWS_DEV, :]
+    for plane in range(PLANES):
+        first[plane : plane + 1, :] = u[plane, 0:1, :]
+        last[plane : plane + 1, :] = u[plane, ROWS_DEV - 1 : ROWS_DEV, :]
+    for k in range(DEPTH - 1):
+        last[PLANES + k : PLANES + k + 1, :] = shear[k, :, :]
+
+
+def pack(u, shear_row):
     return call(
         pack_kernel,
         (out(SURF), out(64), out(64)),
-        [ANY, ANY],
-        (VMEM, VMEM, VMEM),
-        [pltpu.SemaphoreType.DMA((6,))],
-        (u.reshape(-1, ROWS_DEV, BLOCK), shear.reshape(-1, ROWS_DEV, BLOCK)),
+        [VMEM, VMEM],
+        (VMEM,) * 3,
+        [],
+        (u, shear_row),
         1000,
         400_000,
     )
@@ -223,7 +214,7 @@
 def strip_kernel(u, shear, strip):
     def layer(k, held):
         for c in range(3):
-            held = put_column(held, u[c * DEPTH + k, :, :], c * DEPTH + k)
+            held = put_column(held, u[c * DEPTH + k, 0:ROWS_DEV, :], c * DEPTH + k)
         return held
 
     def moduli(k, held):
@@ -242,7 +233,7 @@
         [VMEM, VMEM],
         VMEM,
         [],
-        (u.reshape(-1, ROWS_DEV, BLOCK), shear.reshape(-1, ROWS_DEV, BLOCK)),
+        (u, shear),
         1_000_000,
         2_000_000,
     )
@@ -304,16 +295,17 @@
     gx = lax.axis_index("gx")
     lanes = iota((DEPTH, BLOCK), 1)
     sub = iota((DEPTH, BLOCK), 0)
-    keep = (
-        (lanes < BLOCK - 1)
-        & (sub < DEPTH - 1)
-        & (lanes != dead_lane(lax.axis_index("gy")))
-    )
+    keep = (lanes < BLOCK - 1) & (sub < DEPTH - 1)
     top_moduli = jnp.where(keep & (gx > 0), moduli_above, 0.0)
     bottom_moduli = jnp.where(keep & (gx < lax.axis_size("gx") - 1), own_moduli, 0.0)
     top = row_ring(above, first, top_moduli, True)
     bottom = row_ring(last, below, bottom_moduli, False)
     return top, bottom
+
+
+def by_side(across, within):
+    even = lax.rem(lax.axis_index("gy"), 2) == 0
+    return jnp.where(even, across, within), jnp.where(even, within, across)
 
 
 def column_ring(own, from_left, from_right, moduli):
@@ -353,7 +345,7 @@
         f = (dg + ee) + roll(dg - ee, 1, 0)
         f = roll(f, 32 * c, 1) if c else f
         total = f if total is None else total + f
-    return total[0:ROWS_DEV], near
+    return total[0:ROWS_DEV]
 
 
 def from_strip(strip, position):
@@ -373,6 +365,7 @@
     count = lax.axis_size("gy")
     partner = lax.rem(tile + count // 2, count)
     which = lax.rem(owner - partner + 1 + count, count)
+    which = jnp.where(lax.rem(tile, 2) == 0, which, 2 - which)
     index = jnp.broadcast_to(which * ROWS_DEV + blocks, (ROWS_DEV, 256))
     onehot = jnp.where(index == iota((ROWS_DEV, 256), 1), 1.0, 0.0).astype(BF16)[:, :SURF]
     columns = []
@@ -461,21 +454,12 @@
 
 
 def first_contact_kernel(
-    surface, sent, left, right, above, below, first, last, v_hbm, normals, gap, mortar_hbm, owner,
-    blocks, live, raw_out, u_out, v_out, ring_out, rows_out, mortar, v, lhs, prod, sems,
+    surface, sent, across, within, above, below, first, last, low, surface_v, normals, gap, mortar,
+    owner, blocks, live, raw_out, u_out, v_out, ring_out, rows_out, lhs, prod,
 ):
-    load = pltpu.make_async_copy(mortar_hbm, mortar, sems.at[0])
-    load.start()
-    load_v = [
-        pltpu.make_async_copy(
-            v_hbm.at[c * DEPTH], v.at[pl.ds(c * ROWS_DEV, ROWS_DEV), :], sems.at[1 + c]
-        )
-        for c in range(3)
-    ]
-    for each in load_v:
-        each.start()
     at = pl.ds(SURF, STRIP)
-    ring, _ = column_ring(sent[at, :], left[at, :], right[at, :], None)
+    left, right = by_side(across[at, :], within[at, :])
+    ring = column_ring(sent[at, :], left, right, None)
     ring_out[...] = ring
     top, bottom = row_rings(
         first[0:PLANES, :], last[0:PLANES, :], above[0:PLANES, :], below[0:PLANES, :],
@@ -484,11 +468,8 @@
     for c in range(3):
         rows_out[c * DEPTH : (c + 1) * DEPTH, :] = top[c]
         rows_out[PLANES + c * DEPTH : PLANES + (c + 1) * DEPTH, :] = bottom[c]
-    load.wait()
-    for each in load_v:
-        each.wait()
     slave, raw = contact(
-        three(surface), [three(left), three(sent), three(right)], three(normals), gap[...], mortar,
+        three(surface), [three(across), three(sent), three(within)], three(normals), gap[...], mortar,
         owner[...], blocks[...], live[0, 0], lhs, prod,
     )
     raw_out[SURF:RAW, :] = jnp.broadcast_to(place_table(owner[...], blocks[...]), (8, BLOCK))
@@ -496,7 +477,8 @@
     for c in range(3):
         here = slice(c * ROWS_DEV, (c + 1) * ROWS_DEV)
         raw_out[here, :] = raw[c]
-        new = v[here, :] + from_strip(ring, c * DEPTH) + TIME_STEP * slave[c]
+        new = DAMPING * surface_v[here, :] + low[c * (DEPTH // 2), :, :] + TIME_STEP * slave[c]
+        new = new + from_strip(ring, c * DEPTH)
         new = new + jnp.where(sub == 0, jnp.broadcast_to(top[c][0:1], sub.shape), 0.0)
         new = new + jnp.where(
             sub == ROWS_DEV - 1, jnp.broadcast_to(bottom[c][0:1], sub.shape), 0.0
@@ -515,11 +497,9 @@
     return call(
         first_contact_kernel,
         (out(RAW), out(SURF), out(SURF), out(ROWS_DEV), out(2 * PLANES)),
-        [VMEM] * 8 + [ANY, VMEM, VMEM, ANY, VMEM, VMEM, SMEM],
+        [VMEM] * 15 + [SMEM],
         (VMEM,) * 5,
-        [pltpu.VMEM((ROWS_DEV * BLOCK, BLOCK), BF16), pltpu.VMEM((SURF, BLOCK), F32)]
-        + CONTACT_SCRATCH
-        + [pltpu.SemaphoreType.DMA((4,))],
+        CONTACT_SCRATCH,
         args,
         4_000_000,
         4_000_000,
@@ -527,34 +507,39 @@
 
 
 def update_kernel(
-    u, v, ring, rows, surface, surface_v, u_out, v_out, strip, first, last
+    u, v, low, high, ring, rows, surface, surface_v, u_out, v_out, strip, first, last
 ):
     strength = ring[...]
     sub = iota((ROWS_DEV, BLOCK), 0)
-    for c in range(3):
-        u_out[c * DEPTH, :, :] = surface[c * ROWS_DEV : (c + 1) * ROWS_DEV, :]
+    u_out[:, ROWS_DEV:STRIP, :] = jnp.zeros((PLANES, STRIP - ROWS_DEV, BLOCK), F32)
+    for c in range(3):
+        u_out[c * DEPTH, 0:ROWS_DEV, :] = surface[c * ROWS_DEV : (c + 1) * ROWS_DEV, :]
         v_out[c * DEPTH, :, :] = surface_v[c * ROWS_DEV : (c + 1) * ROWS_DEV, :]
 
-    def layer(k, held):
+    half = DEPTH // 2
+
+    def layer(forces, start, k, held):
         for c in range(3):
             plane = c * DEPTH + k
-            new = v[plane, :, :] + from_strip(strength, plane)
+            new = v[plane, :, :] + forces[c * half + k - start, :, :]
+            new = new + from_strip(strength, plane)
             new = new + jnp.where(sub == 0, jnp.broadcast_to(rows[pl.ds(plane, 1), :], sub.shape), 0.0)
             new = new + jnp.where(
                 sub == ROWS_DEV - 1,
                 jnp.broadcast_to(rows[pl.ds(PLANES + plane, 1), :], sub.shape),
                 0.0,
             )
-            moved = u[plane, :, :] + TIME_STEP * new
+            moved = u[plane, 0:ROWS_DEV, :] + TIME_STEP * new
             v_out[plane, :, :] = new
-            u_out[plane, :, :] = moved
+            u_out[plane, 0:ROWS_DEV, :] = moved
             first[pl.ds(plane, 1), :] = moved[0:1]
             last[pl.ds(plane, 1), :] = moved[ROWS_DEV - 1 : ROWS_DEV]
             held = put_column(held, moved, plane)
         return held
 
     zero = jnp.zeros((ROWS_DEV, BLOCK), F32)
-    strip[0:ROWS_DEV, :] = lax.fori_loop(1, DEPTH, layer, zero)
+    zero = lax.fori_loop(1, half, functools.partial(layer, low, 0), zero)
+    strip[0:ROWS_DEV, :] = lax.fori_loop(half, DEPTH, functools.partial(layer, high, half), zero)
     strip[ROWS_DEV:STRIP, :] = jnp.zeros((STRIP - ROWS_DEV, BLOCK), F32)
     for ref in (first, last):
         for c in range(3):
@@ -562,15 +547,14 @@
         ref[PLANES:64, :] = jnp.zeros((64 - PLANES, BLOCK), F32)
 
 
-def update(u, v, ring, rows, surface, surface_v):
-    planes = jax.ShapeDtypeStruct((PLANES, ROWS_DEV, BLOCK), F32)
+def update(u, v, low, high, ring, rows, surface, surface_v):
     return call(
         update_kernel,
-        (planes, planes, out(STRIP), out(64), out(64)),
-        [VMEM] * 6,
+        (planes(PLANES, STRIP), planes(PLANES), out(STRIP), out(64), out(64)),
+        [VMEM] * 8,
         (VMEM,) * 5,
         [],
-        (u.reshape(-1, ROWS_DEV, BLOCK), v.reshape(-1, ROWS_DEV, BLOCK), ring, rows, surface, surface_v),
+        (u, v, low, high, ring, rows, surface, surface_v),
         10_000_000,
         6_000_000,
     )
@@ -591,11 +575,9 @@
 
 
 def second_contact_kernel(
-    partial, comb, center, left, right, strip, normals, gap, mortar_hbm, owner, blocks, live,
-    raw_out, slave_out, mortar, lhs, prod, sems,
+    partial, comb, center, across, within, strip, normals, gap, mortar, owner, blocks, live,
+    raw_out, slave_out, lhs, prod,
 ):
-    load = pltpu.make_async_copy(mortar_hbm, mortar, sems.at[0])
-    load.start()
     surface = [
         p + TIME_STEP * TIME_STEP * x for p, x in zip(three(partial), three(comb), strict=True)
     ]
@@ -604,9 +586,8 @@
         held = put_column(held, surface[c], c * DEPTH)
     raw_out[RAW : RAW + ROWS_DEV, :] = held
     raw_out[RAW + ROWS_DEV : RAW + STRIP, :] = jnp.zeros((STRIP - ROWS_DEV, BLOCK), F32)
-    load.wait()
     slave, raw = contact(
-        surface, [three(left), three(center), three(right)], three(normals), gap[...], mortar,
+        surface, [three(across), three(center), three(within)], three(normals), gap[...], mortar,
         owner[...], blocks[...], live[0, 0], lhs, prod,
     )
     raw_out[SURF:RAW, :] = jnp.broadcast_to(place_table(owner[...], blocks[...]), (8, BLOCK))
@@ -620,9 +601,9 @@
     return call(
         second_contact_kernel,
         (out(RAW + STRIP), out(SURF)),
-        [VMEM] * 8 + [ANY, VMEM, VMEM, SMEM],
+        [VMEM] * 11 + [SMEM],
         (VMEM,) * 2,
-        [pltpu.VMEM((ROWS_DEV * BLOCK, BLOCK), BF16)] + CONTACT_SCRATCH + [pltpu.SemaphoreType.DMA((1,))],
+        CONTACT_SCRATCH,
         args,
         4_000_000,
         4_000_000,
@@ -630,9 +611,9 @@
 
 
 def last_collect_kernel(
-    own, left, right, first, last, partial, comb_own, comb_out, first_out, last_out
+    own, across, within, first, last, partial, comb_own, comb_out, first_out, last_out
 ):
-    comb = collected([(three(x), x[SURF : SURF + 1, :]) for x in (left, own, right)])
+    comb = collected([(three(x), x[SURF : SURF + 1, :]) for x in (across, own, within)])
     for c in range(3):
         comb_out[c * ROWS_DEV : (c + 1) * ROWS_DEV, :] = comb[c]
     lanes = iota((8, BLOCK), 1)
@@ -644,9 +625,8 @@
                 partial[at : at + 1, :] + TIME_STEP * TIME_STEP * comb_own[at : at + 1, :]
             )
         at = RAW + row // 8 * 8
-        ref[64:72, :] = jnp.where(
-            lanes % 2 == 1, roll(left[at : at + 8, :], 1, 1), roll(right[at : at + 8, :], -1, 1)
-        )
+        left, right = by_side(across[at : at + 8, :], within[at : at + 8, :])
+        ref[64:72, :] = jnp.where(lanes % 2 == 1, roll(left, 1, 1), roll(right, -1, 1))
 
 
 def last_collect(*args):
@@ -662,15 +642,15 @@
     )
 
 
+GROUP = 4
+
+
 def last_update_kernel(
-    u, v, slave, comb_own, comb, sent, left, right, first, last, above, below,
-    old_sent, old_left, old_above, old_last, u_out, v_out,
+    u, v_low, v_high, slave, comb_own, comb, sent, across, within, first, last, above, below,
+    old_sent, old_across, old_within, old_above, old_last, u_hbm, v_hbm, u_out, v_out, sems,
 ):
     at = pl.ds(RAW, STRIP)
     sub8 = iota((8, BLOCK), 0)
-    lanes8 = iota((8, BLOCK), 1)
-    top_corner = above[64 + 7 : 64 + 8, :]
-    bottom_corner = below[64:65, :]
 
     def with_corners(strip, low, high):
         end = jnp.where(
@@ -680,53 +660,69 @@
         )
         return jnp.concatenate([strip[0:ROWS_DEV], end], axis=0)
 
+    def shifted(row, by):
+        return roll(jnp.broadcast_to(row, sub8.shape), by, 1)[0:1]
+
     own = with_corners(sent[at, :], ends_of_row(below[0:64, :]), ends_of_row(above[0:64, :]))
-    odd8 = iota((1, BLOCK), 1) % 2 == 1
-    corner_left = roll(jnp.broadcast_to(bottom_corner, (8, BLOCK)), -1, 1)[0:1]
-    from_left = with_corners(
-        left[at, :], corner_left, roll(jnp.broadcast_to(top_corner, (8, BLOCK)), -1, 1)[0:1]
-    )
-    from_right = with_corners(
-        right[at, :],
-        roll(jnp.broadcast_to(bottom_corner, (8, BLOCK)), 1, 1)[0:1],
-        roll(jnp.broadcast_to(top_corner, (8, BLOCK)), 1, 1)[0:1],
-    )
+    low_corner = below[64:65, :]
+    high_corner = above[STRIP - 1 : STRIP, :]
+    left, right = by_side(across[at, :], within[at, :])
+    left = with_corners(left, shifted(low_corner, -1), shifted(high_corner, -1))
+    right = with_corners(right, shifted(low_corner, 1), shifted(high_corner, 1))
     old = pl.ds(SURF, STRIP)
     odd = iota((STRIP, BLOCK), 1) % 2 == 1
-    moduli = jnp.where(odd, roll(old_left[old, :], 1, 1), old_sent[old, :])
-    ring, _ = column_ring(own, from_left, from_right, moduli)
+    old_left, _ = by_side(old_across[old, :], old_within[old, :])
+    moduli = jnp.where(odd, roll(old_left, 1, 1), old_sent[old, :])
+    ring = column_ring(own, left, right, moduli)
     top, bottom = row_rings(
         first[0:PLANES, :], last[0:PLANES, :], above[0:PLANES, :], below[0:PLANES, :],
         old_last[PLANES:64, :], old_above[PLANES:64, :],
     )
     sub = iota((ROWS_DEV, BLOCK), 0)
+    half = DEPTH // 2
+    copies = []
     for k in range(DEPTH):
         for c in range(3):
             plane = c * DEPTH + k
-            new = v[plane, :, :] + from_strip(ring, plane)
+            v = v_low[c * half + k, :, :] if k < half else v_high[c * half + k - half, :, :]
+            new = v + from_strip(ring, plane)
             new = new + jnp.where(
                 sub == 0, jnp.broadcast_to(top[c][k : k + 1], sub.shape), 0.0
             )
             new = new + jnp.where(
                 sub == ROWS_DEV - 1, jnp.broadcast_to(bottom[c][k : k + 1], sub.shape), 0.0
             )
-            old_u = u[plane, :, :]
+            old_u = u[plane, 0:ROWS_DEV, :]
             if k == 0:
                 here = slice(c * ROWS_DEV, (c + 1) * ROWS_DEV)
                 new = new + TIME_STEP * (slave[here, :] + comb[here, :])
                 old_u = old_u + TIME_STEP * TIME_STEP * comb_own[here, :]
             v_out[plane, :, :] = new
             u_out[plane, :, :] = old_u + TIME_STEP * new
+        if k % GROUP == GROUP - 1:
+            for c in range(3):
+                group = pl.ds(c * DEPTH + k + 1 - GROUP, GROUP)
+                for source, target in ((u_out, u_hbm), (v_out, v_hbm)):
+                    copy = pltpu.make_async_copy(
+                        source.at[group], target.at[group], sems.at[len(copies)]
+                    )
+                    copy.start()
+                    copies.append(copy)
+    for copy in copies:
+        copy.wait()
 
 
 def last_update(*args):
-    planes = jax.ShapeDtypeStruct((PLANES, ROWS_DEV, BLOCK), F32)
     return call(
         last_update_kernel,
-        (planes, planes),
-        [VMEM] * 16,
-        (VMEM,) * 2,
-        [],
+        (planes(PLANES), planes(PLANES)),
+        [VMEM] * 18,
+        (ANY,) * 2,
+        [
+            pltpu.VMEM((PLANES, ROWS_DEV, BLOCK), F32),
+            pltpu.VMEM((PLANES, ROWS_DEV, BLOCK), F32),
+            pltpu.SemaphoreType.DMA((6 * DEPTH // GROUP,)),
+        ],
         args,
         10_000_000,
         6_000_000,
@@ -736,6 +732,12 @@
 def moved(x, axis, by):
     count = lax.axis_size(axis)
     return lax.ppermute(x, axis, [(i, (i + by) % count) for i in range(count)])
+
+
+def exchanged(x, odd):
+    count = lax.axis_size("gy")
+    pairs = [(i, ((i + odd) ^ 1) - odd) for i in range(count)]
+    return lax.ppermute(x, "gy", [(i, j % count) for i, j in pairs])
 
 
 def local(displacement, velocity, shear, normals, gap_zero, mortar, owner, blocks, live_rows):
@@ -744,45 +746,64 @@
     flat_mortar = mortar.reshape(ROWS_DEV * BLOCK, BLOCK)
     pairing = (flat_normals, gap_zero, flat_mortar, owner, blocks, live_rows)
 
-    surface, first, last = pack(displacement, shear)
+    shape = displacement.shape
+    rows = lax.axis_index("gx") * ROWS_DEV + jnp.arange(ROWS_DEV, dtype=jnp.int32)
+    cols = lax.axis_index("gy") * BLOCK + jnp.arange(BLOCK, dtype=jnp.int32)
+    rows_all = lax.axis_size("gx") * ROWS_DEV
+    cols_all = lax.axis_size("gy") * BLOCK
+    valid = (rows < rows_all - 1)[:, None] & (
+        (cols < cols_all - 1) & (cols != cols_all // 2 + BLOCK // 2 - 1)
+    )[None, :]
+    displacement = jnp.pad(
+        displacement.reshape(PLANES, ROWS_DEV, BLOCK), ((0, 0), (0, STRIP - ROWS_DEV), (0, 0))
+    )
+    shear = jnp.where(valid, shear, 0.0)
+    surface, first, last = pack(displacement, shear[:, ROWS_DEV - 1 :, :])
     opposite = moved(surface, "gy", half)
     above = moved(last, "gx", 1)
     below = moved(first, "gx", -1)
     strip = strips(displacement, shear)
 
     sent = message(opposite, above, below, strip)
-    left = moved(sent, "gy", 1)
-    right = moved(sent, "gy", -1)
-    forced = interior_forces(displacement, velocity, shear)
+    across = exchanged(sent, 1)
+    within = exchanged(sent, 0)
+    low = inner_forces(HALVES[0], displacement, shear)
 
     raw, part_u, part_v, ring, rows = first_contact(
-        surface, sent, left, right, above, below, first, last,
-        forced.reshape(PLANES, ROWS_DEV, BLOCK), *pairing,
+        surface, sent, across, within, above, below, first, last, low,
+        velocity[:, 0].reshape(SURF, BLOCK), *pairing,
     )
     part_opposite = moved(part_u, "gy", half)
-    raw_left = moved(raw, "gy", 1)
-    raw_right = moved(raw, "gy", -1)
-    u, v, strip, first2, last2 = update(displacement, forced, ring, rows, part_u, part_v)
-
-    comb, center = collect(part_opposite, raw, raw_left, raw_right)
-    left2 = moved(center, "gy", 1)
-    right2 = moved(center, "gy", -1)
+    raw_across = exchanged(raw, 1)
+    raw_within = exchanged(raw, 0)
+    high = inner_forces(HALVES[1], displacement, shear)
+    raw, high = lax.optimization_barrier((raw, high))
+
+    comb, center = collect(part_opposite, raw, raw_across, raw_within)
     comb_own = moved(comb, "gy", half)
-
-    raw, slave = second_contact(part_u, comb_own, center, left2, right2, strip, *pairing)
-    raw_left = moved(raw, "gy", 1)
-    raw_right = moved(raw, "gy", -1)
-    forced = interior_forces(u, v, shear, comb_own)
-
-    comb, first2, last2 = last_collect(raw, raw_left, raw_right, first2, last2, part_u, comb_own)
+    across2 = exchanged(center, 1)
+    within2 = exchanged(center, 0)
+    raw, velocity = lax.optimization_barrier((raw, velocity))
+    damped = DAMPING * velocity.reshape(PLANES, ROWS_DEV, BLOCK)
+    u, v, strip, first2, last2 = update(displacement, damped, low, high, ring, rows, part_u, part_v)
+
+    raw, slave = second_contact(part_u, comb_own, center, across2, within2, strip, *pairing)
+    raw_across = exchanged(raw, 1)
+    raw_within = exchanged(raw, 0)
+    high = inner_forces(HALVES[1], u, shear, v, comb_own)
+    raw, high = lax.optimization_barrier((raw, high))
+
+    comb, first2, last2 = last_collect(
+        raw, raw_across, raw_within, first2, last2, part_u, comb_own
+    )
     comb_last = moved(comb, "gy", half)
     above2 = moved(last2, "gx", 1)
     below2 = moved(first2, "gx", -1)
+    low = inner_forces(HALVES[0], u, shear, v, comb_own)
     u, v = last_update(
-        u, forced.reshape(PLANES, ROWS_DEV, BLOCK), slave, comb_own, comb_last, raw, raw_left,
-        raw_right, first2, last2, above2, below2, sent, left, above, last,
-    )
-    shape = displacement.shape
+        u, low, high, slave, comb_own, comb_last, raw, raw_across, raw_within, first2, last2,
+        above2, below2, sent, across, within, above, last,
+    )
     return u.reshape(shape), v.reshape(shape)
 
 

time: 76.4 us -> 64.7 us (0.85)
  waiting for transfers between devices: 22.6 us -> 12.4 us
  Pallas kernels: 28.1 us -> 24.9 us
  starting transfers between devices: 19.9 us -> 21.4 us
  other arithmetic: 0 us -> 1.4 us
  local copies, waits for them, and re-layouts: 4.06 us -> 2.68 us
    ppermute x16 -> x8, waiting for transfers between devices: 22.6 us -> 8.36 us  [moved(): return lax.ppermute(x, axis, [(i, (i + by) % count) for i in range(count)])]
    ppermute x0 -> x8, starting transfers between devices: none -> 5.27 us  [exchanged(): return lax.ppermute(x, 'gy', [(i, j % count) for i, j in pairs])]
    ppermute x0 -> x8, waiting for transfers between devices: none -> 4.07 us  [exchanged(): return lax.ppermute(x, 'gy', [(i, j % count) for i, j in pairs])]
    unnamed x22 -> x14, local copies, waits for them, and re-layouts: 4.06 us -> 0.22 us
    ppermute x16 -> x8, starting transfers between devices: 19.9 us -> 16.1 us  [moved(): return lax.ppermute(x, axis, [(i, (i + by) % count) for i in range(count)])]
    pallas_call x11 -> x13, Pallas kernels: 28.1 us -> 24.9 us  [call(): pl.pallas_call(kernel, out_shape=out_shape, in_specs=in_specs, out_specs=...]
    pad x0 -> x1, local copies, waits for them, and re-layouts: none -> 1.54 us  [local(): jnp.pad(displacement.reshape(PLANES, ROWS_DEV, BLOCK), ((0, 0), (0, STRIP...]
    select_n x0 -> x1, other arithmetic: none -> 1.07 us  [local(): shear = jnp.where(valid, shear, 0.0)]
  transfers between devices with their start and end apart: 16 -> 16, of which waited for: 7 -> 6; matrix products, arithmetic and copies ran while one was open for 0% -> 2% of each run, Pallas kernels for 23% -> 23%
where the time goes in v1:
time: 64.7 us; the launch traced here: 64.4 us
  Pallas kernels  24.9 us (38%)
  starting transfers between devices  21.4 us (33%)
  waiting for transfers between devices  12.4 us (19%)
  local copies, waits for them, and re-layouts  2.68 us (4%)
  between operations  1.63 us (3%)
  other arithmetic  1.4 us (2%)
    pallas_call x13, Pallas kernels, call(): pl.pallas_call(kernel, out_shape=out_shape, in_specs=in_specs, out_specs=...  24.9 us
    ppermute x8, starting transfers between devices, moved(): return lax.ppermute(x, axis, [(i, (i + by) % count) for i in range(count)])  16.1 us
    ppermute x8, waiting for transfers between devices, moved(): return lax.ppermute(x, axis, [(i, (i + by) % count) for i in range(count)])  8.36 us
    ppermute x8, starting transfers between devices, exchanged(): return lax.ppermute(x, 'gy', [(i, j % count) for i, j in pairs])  5.27 us
    ppermute x8, waiting for transfers between devices, exchanged(): return lax.ppermute(x, 'gy', [(i, j % count) for i, j in pairs])  4.07 us
    pad x1, local copies, waits for them, and re-layouts, local(): jnp.pad(displacement.reshape(PLANES, ROWS_DEV, BLOCK), ((0, 0), (0, STRIP...  1.54 us
  transfers between devices with their start and end apart: 16, of which 6 were waited for; matrix products, arithmetic and copies ran while one was open for 2% of the time, Pallas kernels for 23%

profile of v1, /device:TPU:0, one launch (start us, length us, event | category | flops | bytes accessed | tf_op | source)
XLA Modules:
  0.0 64.4 jit_solution(12405987990222303998)
XLA Ops:
  0.7 1.1 %broadcast_select_fusion.shear.refs_1_ = f32[15,64,128]{2,1,0:T(8,128)S(1)} fusion(f32[15,64,128]{2,1,0:T(8,128)} %param.11, pred[64,128]{1,0:T(8,128)(4,1)S(1)} %broadcast_and_fusion), kind=kLoop, calls=%fused_computation.1 | loop fusion | flops 122880 | bytes 991232 | tf_op jit(solution)/shard_map/jit(_where)/select_n | solution.py:760
  1.8 1.5 %pad.4.u.refs_0_ = f32[48,72,128]{2,1,0:T(8,128)S(1)} pad(f32[48,64,128]{2,1,0:T(8,128)} %bitcast.13, f32[]{:T(128)} %constant.10.clone.1), padding=0_0x0_8x0_0 | pad | bytes 3342340 | tf_op jit(solution)/shard_map/jit(_pad)/pad | solution.py:757
  3.5 4.0 %collective-permute-start = (f32[192,128]{1,0:T(8,128)S(1)}, f32[192,128]{1,0:T(8,128)S(1)}, u32[]{:S(2)}, u32[]{:S(2)}) collective-permute-start(f32[192,128]{1,0:T(8,128)S(1)} %get-tuple-element.29.surface), channel_id=1, source_target_pairs={{0,8},{1,9},{2,10},{3,11},{4,12},{5,13},{6,14},{7,15},{8,0},{9,1},... | collective-permute-start | bytes 294920 | tf_op jit(solution)/shard_map/ppermute | solution.py:734
  7.5 3.0 %collective-permute-start.1 = (f32[64,128]{1,0:T(8,128)S(1)}, f32[64,128]{1,0:T(8,128)S(1)}, u32[]{:S(2)}, u32[]{:S(2)}) collective-permute-start(f32[64,128]{1,0:T(8,128)S(1)} %get-tuple-element.30.last.old_last), channel_id=1, source_target_pairs={{0,16},{16,32},{32,48},{48,64},{64,80},{80,96},{96,112},{112,0},{1... | collective-permute-start | bytes 98312 | tf_op jit(solution)/shard_map/ppermute | solution.py:734
  10.5 2.6 %collective-permute-start.2 = (f32[64,128]{1,0:T(8,128)S(1)}, f32[64,128]{1,0:T(8,128)S(1)}, u32[]{:S(2)}, u32[]{:S(2)}) collective-permute-start(f32[64,128]{1,0:T(8,128)S(1)} %get-tuple-element.31.first), channel_id=1, source_target_pairs={{0,112},{16,0},{32,16},{48,32},{64,48},{80,64},{96,80},{112,96},{1... | collective-permute-start | bytes 98312 | tf_op jit(solution)/shard_map/ppermute | solution.py:734
  13.1 2.6 %shard_map.105.strip = f32[72,128]{1,0:T(8,128)S(1)} custom-call(f32[48,72,128]{2,1,0:T(8,128)S(1)} %pad.4.u.refs_0_, f32[15,64,128]{2,1,0:T(8,128)S(1)} %broadcast_select_fusion.shear.refs_1_), custom_call_target="tpu_custom_call" | custom-call | flops 1000000 | bytes 2000000 | tf_op jit(solution)/shard_map/pallas_call | solution.py:37
  15.8 0.2 collective-permute-done.2.below
  16.1 0.2 collective-permute-start.3
  16.2 1.4 %collective-permute-start.4 = (f32[264,128]{1,0:T(8,128)S(1)}, f32[264,128]{1,0:T(8,128)S(1)}, u32[]{:S(2)}, u32[]{:S(2)}) collective-permute-start(f32[264,128]{1,0:T(8,128)S(1)} %shard_map.106.sent.old_sent), channel_id=1, source_target_pairs={{0,1},{1,0},{2,3},{3,2},{4,5},{5,4},{6,7},{7,6},{8,9},{9,8},{10,11... | collective-permute-start | bytes 405512 | tf_op jit(solution)/shard_map/ppermute | solution.py:740
  17.6 0.9 %slice.7 = f32[3,1,64,128]{3,2,1,0:T(8,128)S(1)} slice(f32[3,16,64,128]{3,2,1,0:T(8,128)} %param.10), slice={[0:3], [0:1], [0:64], [0:128]} | slice | bytes 196608 | tf_op jit(solution)/shard_map/slice | solution.py:774
  19.5 2.4 %shard_map.107.low = f32[24,64,128]{2,1,0:T(8,128)S(1)} custom-call(f32[48,72,128]{2,1,0:T(8,128)S(1)} %pad.4.u.refs_0_, f32[15,64,128]{2,1,0:T(8,128)S(1)} %broadcast_select_fusion.shear.refs_1_), custom_call_target="tpu_custom_call" | custom-call | flops 15000000 | bytes 3000000 | tf_op jit(solution)/shard_map/pallas_call | solution.py:37
  21.9 0.8 %collective-permute-done.3.across.old_across = f32[264,128]{1,0:T(8,128)S(1)} collective-permute-done((f32[264,128]{1,0:T(8,128)S(1)}, f32[264,128]{1,0:T(8,128)S(1)}, u32[]{:S(2)}, u32[]{:S(2)}) %collective-permute-start.3) | collective-permute-done | bytes 135200 | tf_op jit(solution)/shard_map/ppermute | solution.py:740
  22.7 3.4 %shard_map.108 = (f32[200,128]{1,0:T(8,128)S(1)}, f32[192,128]{1,0:T(8,128)S(1)}, f32[192,128]{1,0:T(8,128)S(1)}, f32[64,128]{1,0:T(8,128)S(1)}, f32[96,128]{1,0:T(8,128)S(1)}) custom-call(f32[192,128]{1,0:T(8,128)S(1)} %get-tuple-element.29.surface, f32[264,128]{1,0:T(8,128)S(1)} %shard_map.106.sent.old_sent, ...), custom_call_target="tpu_custom_call" | custom-call | flops 4000000 | bytes 4000000 | tf_op jit(solution)/shard_map/pallas_call | solution.py:37
  26.1 1.8 %collective-permute-start.6 = (f32[200,128]{1,0:T(8,128)S(1)}, f32[200,128]{1,0:T(8,128)S(1)}, u32[]{:S(2)}, u32[]{:S(2)}) collective-permute-start(f32[200,128]{1,0:T(8,128)S(1)} %get-tuple-element.33.own), channel_id=1, source_target_pairs={{0,15},{1,2},{2,1},{3,4},{4,3},{5,6},{6,5},{7,8},{8,7},{9,10},{10,... | collective-permute-start | bytes 307208 | tf_op jit(solution)/shard_map/ppermute | solution.py:740
  27.9 0.2 collective-permute-start.5
  28.1 2.5 %shard_map.109.high = f32[24,64,128]{2,1,0:T(8,128)S(1)} custom-call(f32[48,72,128]{2,1,0:T(8,128)S(1)} %pad.4.u.refs_0_, f32[15,64,128]{2,1,0:T(8,128)S(1)} %broadcast_select_fusion.shear.refs_1_), custom_call_target="tpu_custom_call" | custom-call | flops 15000000 | bytes 3000000 | tf_op jit(solution)/shard_map/pallas_call | solution.py:37
  30.6 4.0 %collective-permute-done.5.partial = f32[192,128]{1,0:T(8,128)S(1)} collective-permute-done((f32[192,128]{1,0:T(8,128)S(1)}, f32[192,128]{1,0:T(8,128)S(1)}, u32[]{:S(2)}, u32[]{:S(2)}) %collective-permute-start.5) | collective-permute-done | bytes 98336 | tf_op jit(solution)/shard_map/ppermute | solution.py:734
  34.6 0.2 shard_map.111
  34.9 0.9 %collective-permute-start.9 = (f32[192,128]{1,0:T(8,128)S(1)}, f32[192,128]{1,0:T(8,128)S(1)}, u32[]{:S(2)}, u32[]{:S(2)}) collective-permute-start(f32[192,128]{1,0:T(8,128)S(1)} %get-tuple-element.43.center), channel_id=1, source_target_pairs={{0,15},{1,2},{2,1},{3,4},{4,3},{5,6},{6,5},{7,8},{8,7},{9,10},{10,... | collective-permute-start | bytes 294920 | tf_op jit(solution)/shard_map/ppermute | solution.py:740
  35.8 0.4 collective-permute-start.8
  36.2 0.2 broadcast_multiply_fusion
  36.5 2.6 %shard_map.110 = (f32[48,72,128]{2,1,0:T(8,128)S(1)}, f32[48,64,128]{2,1,0:T(8,128)S(1)}, f32[72,128]{1,0:T(8,128)S(1)}, f32[64,128]{1,0:T(8,128)S(1)}, f32[64,128]{1,0:T(8,128)S(1)}) custom-call(f32[48,72,128]{2,1,0:T(8,128)S(1)} %pad.4.u.refs_0_, f32[48,64,128]{2,1,0:T(8,128)S(1)} %bitcast.9, f32[24,64,128]{2,1,0:T(8,128)S(1)} %shard_map.107.low, ...), custom_call_target="tpu_custom_call" | custom-call | flops 10000000 | bytes 6000000 | tf_op jit(solution)/shard_map/pallas_call | solution.py:37
  39.1 4.1 %collective-permute-done.8.refs_3_.comb.comb_own = f32[192,128]{1,0:T(8,128)S(1)} collective-permute-done((f32[192,128]{1,0:T(8,128)S(1)}, f32[192,128]{1,0:T(8,128)S(1)}, u32[]{:S(2)}, u32[]{:S(2)}) %collective-permute-start.8) | collective-permute-done | bytes 98336 | tf_op jit(solution)/shard_map/ppermute | solution.py:734
  43.2 2.9 %shard_map.113 = (f32[272,128]{1,0:T(8,128)S(1)}, f32[192,128]{1,0:T(8,128)S(1)}) custom-call(f32[192,128]{1,0:T(8,128)S(1)} %get-tuple-element.38.surface.partial, f32[192,128]{1,0:T(8,128)S(1)} %collective-permute-done.8.refs_3_.comb.comb_own, f32[192,128]{1,0:T(8,128)S(1)} %get-tuple-element.43.center, f32[192,128]{1,0:T(8,128)S(1)} %collective-permute-done.9.across, ...), custom_call_target="tpu_custom_call" | custom-call | flops 4000000 | bytes 4000000 | tf_op jit(solution)/shard_map/pallas_call | solution.py:37
  46.1 1.0 %collective-permute-start.11 = (f32[272,128]{1,0:T(8,128)S(1)}, f32[272,128]{1,0:T(8,128)S(1)}, u32[]{:S(2)}, u32[]{:S(2)}) collective-permute-start(f32[272,128]{1,0:T(8,128)S(1)} %get-tuple-element.48.own.sent), channel_id=1, source_target_pairs={{0,15},{1,2},{2,1},{3,4},{4,3},{5,6},{6,5},{7,8},{8,7},{9,10},{10,... | collective-permute-start | bytes 417800 | tf_op jit(solution)/shard_map/ppermute | solution.py:740
  47.2 2.5 %shard_map.114.v_high = f32[24,64,128]{2,1,0:T(8,128)S(1)} custom-call(f32[48,72,128]{2,1,0:T(8,128)S(1)} %get-tuple-element.40.refs_0_.u, f32[15,64,128]{2,1,0:T(8,128)S(1)} %broadcast_select_fusion.shear.refs_1_, f32[48,64,128]{2,1,0:T(8,128)S(1)} %get-tuple-element.41.refs_2_, f32[192,128]{1,0:T(8,128)S(1)} %collective-permute-done.8.refs_3_.comb.comb_own), custom_call_target="tpu_custom_call" | custom-call | flops 15000000 | bytes 3000000 | tf_op jit(solution)/shard_map/pallas_call | solution.py:37
  49.7 3.3 %collective-permute-done.11.across = f32[272,128]{1,0:T(8,128)S(1)} collective-permute-done((f32[272,128]{1,0:T(8,128)S(1)}, f32[272,128]{1,0:T(8,128)S(1)}, u32[]{:S(2)}, u32[]{:S(2)}) %collective-permute-start.11) | collective-permute-done | bytes 139296 | tf_op jit(solution)/shard_map/ppermute | solution.py:740
  53.0 0.2 shard_map.115
  53.3 2.9 %collective-permute-start.14 = (f32[72,128]{1,0:T(8,128)S(1)}, f32[72,128]{1,0:T(8,128)S(1)}, u32[]{:S(2)}, u32[]{:S(2)}) collective-permute-start(f32[72,128]{1,0:T(8,128)S(1)} %get-tuple-element.53.last), channel_id=1, source_target_pairs={{0,16},{16,32},{32,48},{48,64},{64,80},{80,96},{96,112},{112,0},{1... | collective-permute-start | bytes 110600 | tf_op jit(solution)/shard_map/ppermute | solution.py:734
  56.1 2.8 %collective-permute-start.15 = (f32[72,128]{1,0:T(8,128)S(1)}, f32[72,128]{1,0:T(8,128)S(1)}, u32[]{:S(2)}, u32[]{:S(2)}) collective-permute-start(f32[72,128]{1,0:T(8,128)S(1)} %get-tuple-element.52.first), channel_id=1, source_target_pairs={{0,112},{16,0},{32,16},{48,32},{64,48},{80,64},{96,80},{112,96},{1... | collective-permute-start | bytes 110600 | tf_op jit(solution)/shard_map/ppermute | solution.py:734
  59.0 2.5 %shard_map.112.v_low = f32[24,64,128]{2,1,0:T(8,128)S(1)} custom-call(f32[48,72,128]{2,1,0:T(8,128)S(1)} %get-tuple-element.40.refs_0_.u, f32[15,64,128]{2,1,0:T(8,128)S(1)} %broadcast_select_fusion.shear.refs_1_, f32[48,64,128]{2,1,0:T(8,128)S(1)} %get-tuple-element.41.refs_2_, f32[192,128]{1,0:T(8,128)S(1)} %collective-permute-done.8.refs_3_.comb.comb_own), custom_call_target="tpu_custom_call" | custom-call | flops 15000000 | bytes 3000000 | tf_op jit(solution)/shard_map/pallas_call | solution.py:37
  61.6 2.8 %shard_map.116 = (f32[48,64,128]{2,1,0:T(8,128)}, f32[48,64,128]{2,1,0:T(8,128)}) custom-call(f32[48,72,128]{2,1,0:T(8,128)S(1)} %get-tuple-element.40.refs_0_.u, f32[24,64,128]{2,1,0:T(8,128)S(1)} %shard_map.112.v_low, f32[24,64,128]{2,1,0:T(8,128)S(1)} %shard_map.114.v_high, f32[192,128]{1,0:T(8,128)S(1)} %get-tuple-element.47.slave, ...), custom_call_target="tpu_custom_call" | custom-call | flops 10000000 | bytes 6000000 | tf_op jit(solution)/shard_map/pallas_call | solution.py:37
  (35 shorter events, 0.7 us)
Async XLA Ops:
  3.4 15.1 %copy-start.4 = (s32[64,1]{0,1:T(1,128)S(1)}, s32[64,1]{0,1:T(1,128)}, u32[]{:S(2)}) copy-start(s32[64,1]{0,1:T(1,128)} %param.15) | copy-start | bytes 772
  3.5 15.2 %copy-start.5 = (s32[64,1]{0,1:T(1,128)S(1)}, s32[64,1]{0,1:T(1,128)}, u32[]{:S(2)}) copy-start(s32[64,1]{0,1:T(1,128)} %param.16) | copy-start | bytes 772
  3.5 12.5 %collective-permute-start = (f32[192,128]{1,0:T(8,128)S(1)}, f32[192,128]{1,0:T(8,128)S(1)}, u32[]{:S(2)}, u32[]{:S(2)}) collective-permute-start(f32[192,128]{1,0:T(8,128)S(1)} %get-tuple-element.29.surface), channel_id=1, source_target_pairs={{0,8},{1,9},{2,10},{3,11},{4,12},{5,13},{6,14},{7,15},{8,0},{9,1},... | collective-permute-start | bytes 294920 | tf_op jit(solution)/shard_map/ppermute | solution.py:734
  7.5 8.3 %collective-permute-start.1 = (f32[64,128]{1,0:T(8,128)S(1)}, f32[64,128]{1,0:T(8,128)S(1)}, u32[]{:S(2)}, u32[]{:S(2)}) collective-permute-start(f32[64,128]{1,0:T(8,128)S(1)} %get-tuple-element.30.last.old_last), channel_id=1, source_target_pairs={{0,16},{16,32},{32,48},{48,64},{64,80},{80,96},{96,112},{112,0},{1... | collective-permute-start | bytes 98312 | tf_op jit(solution)/shard_map/ppermute | solution.py:734
  10.5 5.4 %collective-permute-start.2 = (f32[64,128]{1,0:T(8,128)S(1)}, f32[64,128]{1,0:T(8,128)S(1)}, u32[]{:S(2)}, u32[]{:S(2)}) collective-permute-start(f32[64,128]{1,0:T(8,128)S(1)} %get-tuple-element.31.first), channel_id=1, source_target_pairs={{0,112},{16,0},{32,16},{48,32},{64,48},{80,64},{96,80},{112,96},{1... | collective-permute-start | bytes 98312 | tf_op jit(solution)/shard_map/ppermute | solution.py:734
  16.1 6.6 %collective-permute-start.3 = (f32[264,128]{1,0:T(8,128)S(1)}, f32[264,128]{1,0:T(8,128)S(1)}, u32[]{:S(2)}, u32[]{:S(2)}) collective-permute-start(f32[264,128]{1,0:T(8,128)S(1)} %shard_map.106.sent.old_sent), channel_id=1, source_target_pairs={{0,15},{1,2},{2,1},{3,4},{4,3},{5,6},{6,5},{7,8},{8,7},{9,10},{10,... | collective-permute-start | bytes 405512 | tf_op jit(solution)/shard_map/ppermute | solution.py:740
  16.2 6.5 %collective-permute-start.4 = (f32[264,128]{1,0:T(8,128)S(1)}, f32[264,128]{1,0:T(8,128)S(1)}, u32[]{:S(2)}, u32[]{:S(2)}) collective-permute-start(f32[264,128]{1,0:T(8,128)S(1)} %shard_map.106.sent.old_sent), channel_id=1, source_target_pairs={{0,1},{1,0},{2,3},{3,2},{4,5},{5,4},{6,7},{7,6},{8,9},{9,8},{10,11... | collective-permute-start | bytes 405512 | tf_op jit(solution)/shard_map/ppermute | solution.py:740
  18.5 4.2 %copy-start.1 = (f32[3,64,128]{2,1,0:T(8,128)S(1)}, f32[3,64,128]{2,1,0:T(8,128)}, u32[]{:S(2)}) copy-start(f32[3,64,128]{2,1,0:T(8,128)} %param.12) | copy-start | bytes 294916
  18.5 4.2 %copy-start.2 = (f32[64,128]{1,0:T(8,128)S(1)}, f32[64,128]{1,0:T(8,128)}, u32[]{:S(2)}) copy-start(f32[64,128]{1,0:T(8,128)} %gap.3) | copy-start | bytes 98308
  18.7 4.0 %copy-start = (bf16[64,1,128,128]{3,2,1,0:T(8,128)(2,1)S(1)}, bf16[64,1,128,128]{3,2,1,0:T(8,128)(2,1)}, u32[]{:S(2)}) copy-start(bf16[64,1,128,128]{3,2,1,0:T(8,128)(2,1)} %param.14) | copy-start | bytes 6291460
  26.1 8.5 %collective-permute-start.6 = (f32[200,128]{1,0:T(8,128)S(1)}, f32[200,128]{1,0:T(8,128)S(1)}, u32[]{:S(2)}, u32[]{:S(2)}) collective-permute-start(f32[200,128]{1,0:T(8,128)S(1)} %get-tuple-element.33.own), channel_id=1, source_target_pairs={{0,15},{1,2},{2,1},{3,4},{4,3},{5,6},{6,5},{7,8},{8,7},{9,10},{10,... | collective-permute-start | bytes 307208 | tf_op jit(solution)/shard_map/ppermute | solution.py:740
  27.9 6.7 %collective-permute-start.7 = (f32[200,128]{1,0:T(8,128)S(1)}, f32[200,128]{1,0:T(8,128)S(1)}, u32[]{:S(2)}, u32[]{:S(2)}) collective-permute-start(f32[200,128]{1,0:T(8,128)S(1)} %get-tuple-element.33.own), channel_id=1, source_target_pairs={{0,1},{1,0},{2,3},{3,2},{4,5},{5,4},{6,7},{7,6},{8,9},{9,8},{10,11... | collective-permute-start | bytes 307208 | tf_op jit(solution)/shard_map/ppermute | solution.py:740
  27.9 8.4 %copy-start.3 = (f32[3,16,64,128]{3,2,1,0:T(8,128)S(1)}, f32[3,16,64,128]{3,2,1,0:T(8,128)}, u32[]{:S(2)}) copy-start(f32[3,16,64,128]{3,2,1,0:T(8,128)} %param.10) | copy-start | bytes 4718596
  27.9 6.7 %collective-permute-start.5 = (f32[192,128]{1,0:T(8,128)S(1)}, f32[192,128]{1,0:T(8,128)S(1)}, u32[]{:S(2)}, u32[]{:S(2)}) collective-permute-start(f32[192,128]{1,0:T(8,128)S(1)} %get-tuple-element.38.surface.partial), channel_id=1, source_target_pairs={{0,8},{1,9},{2,10},{3,11},{4,12},{5,13},{6,14},{7,15},{8,0},{9,1},... | collective-permute-start | bytes 294920 | tf_op jit(solution)/shard_map/ppermute | solution.py:734
  34.9 8.3 %collective-permute-start.9 = (f32[192,128]{1,0:T(8,128)S(1)}, f32[192,128]{1,0:T(8,128)S(1)}, u32[]{:S(2)}, u32[]{:S(2)}) collective-permute-start(f32[192,128]{1,0:T(8,128)S(1)} %get-tuple-element.43.center), channel_id=1, source_target_pairs={{0,15},{1,2},{2,1},{3,4},{4,3},{5,6},{6,5},{7,8},{8,7},{9,10},{10,... | collective-permute-start | bytes 294920 | tf_op jit(solution)/shard_map/ppermute | solution.py:740
  35.8 7.4 %collective-permute-start.10 = (f32[192,128]{1,0:T(8,128)S(1)}, f32[192,128]{1,0:T(8,128)S(1)}, u32[]{:S(2)}, u32[]{:S(2)}) collective-permute-start(f32[192,128]{1,0:T(8,128)S(1)} %get-tuple-element.43.center), channel_id=1, source_target_pairs={{0,1},{1,0},{2,3},{3,2},{4,5},{5,4},{6,7},{7,6},{8,9},{9,8},{10,11... | collective-permute-start | bytes 294920 | tf_op jit(solution)/shard_map/ppermute | solution.py:740
  35.8 7.4 %collective-permute-start.8 = (f32[192,128]{1,0:T(8,128)S(1)}, f32[192,128]{1,0:T(8,128)S(1)}, u32[]{:S(2)}, u32[]{:S(2)}) collective-permute-start(f32[192,128]{1,0:T(8,128)S(1)} %get-tuple-element.42), channel_id=1, source_target_pairs={{0,8},{1,9},{2,10},{3,11},{4,12},{5,13},{6,14},{7,15},{8,0},{9,1},... | collective-permute-start | bytes 294920 | tf_op jit(solution)/shard_map/ppermute | solution.py:734
  46.1 6.8 %collective-permute-start.11 = (f32[272,128]{1,0:T(8,128)S(1)}, f32[272,128]{1,0:T(8,128)S(1)}, u32[]{:S(2)}, u32[]{:S(2)}) collective-permute-start(f32[272,128]{1,0:T(8,128)S(1)} %get-tuple-element.48.own.sent), channel_id=1, source_target_pairs={{0,15},{1,2},{2,1},{3,4},{4,3},{5,6},{6,5},{7,8},{8,7},{9,10},{10,... | collective-permute-start | bytes 417800 | tf_op jit(solution)/shard_map/ppermute | solution.py:740
  47.2 5.8 %collective-permute-start.12 = (f32[272,128]{1,0:T(8,128)S(1)}, f32[272,128]{1,0:T(8,128)S(1)}, u32[]{:S(2)}, u32[]{:S(2)}) collective-permute-start(f32[272,128]{1,0:T(8,128)S(1)} %get-tuple-element.48.own.sent), channel_id=1, source_target_pairs={{0,1},{1,0},{2,3},{3,2},{4,5},{5,4},{6,7},{7,6},{8,9},{9,8},{10,11... | collective-permute-start | bytes 417800 | tf_op jit(solution)/shard_map/ppermute | solution.py:740
  53.2 8.4 %collective-permute-start.13 = (f32[192,128]{1,0:T(8,128)S(1)}, f32[192,128]{1,0:T(8,128)S(1)}, u32[]{:S(2)}, u32[]{:S(2)}) collective-permute-start(f32[192,128]{1,0:T(8,128)S(1)} %get-tuple-element.51), channel_id=1, source_target_pairs={{0,8},{1,9},{2,10},{3,11},{4,12},{5,13},{6,14},{7,15},{8,0},{9,1},... | collective-permute-start | bytes 294920 | tf_op jit(solution)/shard_map/ppermute | solution.py:734
  53.3 8.2 %collective-permute-start.14 = (f32[72,128]{1,0:T(8,128)S(1)}, f32[72,128]{1,0:T(8,128)S(1)}, u32[]{:S(2)}, u32[]{:S(2)}) collective-permute-start(f32[72,128]{1,0:T(8,128)S(1)} %get-tuple-element.53.last), channel_id=1, source_target_pairs={{0,16},{16,32},{32,48},{48,64},{64,80},{80,96},{96,112},{112,0},{1... | collective-permute-start | bytes 110600 | tf_op jit(solution)/shard_map/ppermute | solution.py:734
  56.1 5.5 %collective-permute-start.15 = (f32[72,128]{1,0:T(8,128)S(1)}, f32[72,128]{1,0:T(8,128)S(1)}, u32[]{:S(2)}, u32[]{:S(2)}) collective-permute-start(f32[72,128]{1,0:T(8,128)S(1)} %get-tuple-element.52.first), channel_id=1, source_target_pairs={{0,112},{16,0},{32,16},{48,32},{64,48},{80,64},{96,80},{112,96},{1... | collective-permute-start | bytes 110600 | tf_op jit(solution)/shard_map/ppermute | solution.py:734

commit v2 on v1

--- a/solution.py
+++ b/solution.py
@@ -13,6 +13,7 @@
 PLANES = 3 * DEPTH
 SURF = 3 * ROWS_DEV
 STRIP = 72
+LIVE = 2**16
 
 DAMPING = 0.9
 TIME_STEP = 0.1
@@ -21,7 +22,6 @@
 F32 = jnp.float32
 BF16 = jnp.bfloat16
 VMEM = pl.BlockSpec(memory_space=pltpu.VMEM)
-SMEM = pl.BlockSpec(memory_space=pltpu.SMEM)
 ANY = pl.BlockSpec(memory_space=pl.ANY)
 
 
@@ -42,7 +42,7 @@
         scratch_shapes=scratch,
         compiler_params=pltpu.CompilerParams(vmem_limit_bytes=limit * 2**20),
         cost_estimate=pl.CostEstimate(
-            flops=flops, bytes_accessed=bytes_accessed, transcendentals=0
+            flops=1000, bytes_accessed=1000, transcendentals=0
         ),
     )(*args)
 
@@ -150,7 +150,8 @@
     lax.fori_loop(0, ROWS_DEV // 8, chunk, 0)
 
 
-HALVES = ((0, DEPTH // 2), (DEPTH // 2, DEPTH))
+FIRST_LOW = 11
+SECOND_LOW = 5
 
 
 def planes(count, rows=ROWS_DEV):
@@ -212,16 +213,11 @@
 
 
 def strip_kernel(u, shear, strip):
-    def layer(k, held):
-        for c in range(3):
-            held = put_column(held, u[c * DEPTH + k, 0:ROWS_DEV, :], c * DEPTH + k)
-        return held
-
-    def moduli(k, held):
-        return put_column(held, shear[k, :, :], PLANES + k)
-
-    held = lax.fori_loop(0, DEPTH, layer, jnp.zeros((ROWS_DEV, BLOCK), F32))
-    held = lax.fori_loop(0, DEPTH - 1, moduli, held)
+    held = jnp.zeros((ROWS_DEV, BLOCK), F32)
+    for plane in range(PLANES):
+        held = put_column(held, u[plane, 0:ROWS_DEV, :], plane)
+    for k in range(DEPTH - 1):
+        held = put_column(held, shear[k, :, :], PLANES + k)
     strip[0:ROWS_DEV, :] = held
     strip[ROWS_DEV:STRIP, :] = jnp.zeros((STRIP - ROWS_DEV, BLOCK), F32)
 
@@ -295,7 +291,9 @@
     gx = lax.axis_index("gx")
     lanes = iota((DEPTH, BLOCK), 1)
     sub = iota((DEPTH, BLOCK), 0)
-    keep = (lanes < BLOCK - 1) & (sub < DEPTH - 1)
+    cols_all = lax.axis_size("gy") * BLOCK
+    column = lanes + lax.axis_index("gy") * BLOCK
+    keep = (lanes < BLOCK - 1) & (sub < DEPTH - 1) & (column != cols_all // 2 + BLOCK // 2 - 1)
     top_moduli = jnp.where(keep & (gx > 0), moduli_above, 0.0)
     bottom_moduli = jnp.where(keep & (gx < lax.axis_size("gx") - 1), own_moduli, 0.0)
     top = row_ring(above, first, top_moduli, True)
@@ -308,14 +306,19 @@
     return jnp.where(even, across, within), jnp.where(even, within, across)
 
 
-def column_ring(own, from_left, from_right, moduli):
+def halo_of(across, within):
+    left, right = by_side(across, within)
+    odd = iota(left.shape, 1) % 2 == 1
+    return jnp.where(odd, roll(left, 1, 1), roll(right, -1, 1))
+
+
+def column_ring(own, halo, moduli):
     gx = lax.axis_index("gx")
     gy = lax.axis_index("gy")
     shape = (STRIP, BLOCK)
     lanes = iota(shape, 1)
     sub = iota(shape, 0)
     odd = lanes % 2 == 1
-    halo = jnp.where(odd, roll(from_left, 1, 1), roll(from_right, -1, 1))
     near = jnp.where(odd, halo, own)
     far = jnp.where(odd, own, halo)
     s = near + far
@@ -360,13 +363,15 @@
     return high, low
 
 
-def contact(surface, near, normals, gap, mortar, owner, blocks, live, lhs, prod):
+def contact(surface, near, normals, gap, mortar, coded, lhs, prod):
     tile = lax.axis_index("gy")
     count = lax.axis_size("gy")
     partner = lax.rem(tile + count // 2, count)
+    place, alive = coded & (LIVE - 1), jnp.broadcast_to(coded >= LIVE, (ROWS_DEV, BLOCK))
+    owner = lax.shift_right_logical(place, 6)
     which = lax.rem(owner - partner + 1 + count, count)
     which = jnp.where(lax.rem(tile, 2) == 0, which, 2 - which)
-    index = jnp.broadcast_to(which * ROWS_DEV + blocks, (ROWS_DEV, 256))
+    index = jnp.broadcast_to(which * ROWS_DEV + (place & (ROWS_DEV - 1)), (ROWS_DEV, 256))
     onehot = jnp.where(index == iota((ROWS_DEV, 256), 1), 1.0, 0.0).astype(BF16)[:, :SURF]
     columns = []
     for half in range(2):
@@ -378,22 +383,18 @@
     for j in range(6):
         lhs[pl.ds(j, ROWS_DEV, stride=8), :] = masters[:, j * BLOCK : (j + 1) * BLOCK]
 
-    def project(r, _):
-        at = pl.ds(pl.multiple_of(r * 8, 8), 8)
-        block = mortar[pl.ds(pl.multiple_of(r * BLOCK, BLOCK), BLOCK), :]
+    for r in range(ROWS_DEV):
+        at = slice(r * 8, (r + 1) * 8)
+        block = mortar[r * BLOCK : (r + 1) * BLOCK, :]
         prod[at, :] = lax.dot_general(
             lhs[at, :].astype(BF16), block, (((1,), (1,)), ((), ())), preferred_element_type=F32
         )
-        return 0
-
-    lax.fori_loop(0, ROWS_DEV, project, 0, unroll=16)
     opening = gap
     for c in range(3):
         projected = (
             prod[pl.ds(c, ROWS_DEV, stride=8), :] + prod[pl.ds(c + 3, ROWS_DEV, stride=8), :]
         )
         opening = opening + normals[c] * (surface[c] - projected)
-    alive = iota((ROWS_DEV, BLOCK), 0) < live
     pressure = jnp.where(alive, PENALTY * jnp.maximum(-opening, 0.0), 0.0)
     slave = [pressure * normals[c] for c in range(3)]
     for c in range(3):
@@ -401,22 +402,22 @@
         lhs[pl.ds(c, ROWS_DEV, stride=8), :] = high.astype(F32)
         lhs[pl.ds(c + 3, ROWS_DEV, stride=8), :] = low.astype(F32)
 
-    def react(r, _):
-        at = pl.ds(pl.multiple_of(r * 8, 8), 8)
-        block = mortar[pl.ds(pl.multiple_of(r * BLOCK, BLOCK), BLOCK), :]
+    return slave
+
+
+def reactions(lhs, mortar, prod):
+    for r in range(ROWS_DEV):
+        at = slice(r * 8, (r + 1) * 8)
+        block = mortar[r * BLOCK : (r + 1) * BLOCK, :]
         prod[at, :] = jnp.dot(lhs[at, :].astype(BF16), block, preferred_element_type=F32)
-        return 0
-
-    lax.fori_loop(0, ROWS_DEV, react, 0, unroll=16)
-    raw = [
+    return [
         -(prod[pl.ds(c, ROWS_DEV, stride=8), :] + prod[pl.ds(c + 3, ROWS_DEV, stride=8), :])
         for c in range(3)
     ]
-    return slave, raw
-
-
-def place_table(owner, blocks):
-    place = jnp.broadcast_to((owner * ROWS_DEV + blocks).astype(F32), (ROWS_DEV, BLOCK))
+
+
+def place_table(place):
+    place = jnp.broadcast_to(place.astype(F32), (ROWS_DEV, BLOCK))
     diagonal = iota((ROWS_DEV, BLOCK), 0) == iota((ROWS_DEV, BLOCK), 1)
     line = jnp.sum(jnp.where(diagonal, place, 0.0), axis=0, keepdims=True)
     return jnp.where(iota((1, BLOCK), 1) < ROWS_DEV, line, -1.0)
@@ -455,11 +456,10 @@
 
 def first_contact_kernel(
     surface, sent, across, within, above, below, first, last, low, surface_v, normals, gap, mortar,
-    owner, blocks, live, raw_out, u_out, v_out, ring_out, rows_out, lhs, prod,
+    place, lhs, u_out, v_out, ring_out, rows_out, prod,
 ):
     at = pl.ds(SURF, STRIP)
-    left, right = by_side(across[at, :], within[at, :])
-    ring = column_ring(sent[at, :], left, right, None)
+    ring = column_ring(sent[at, :], halo_of(across[at, :], within[at, :]), None)
     ring_out[...] = ring
     top, bottom = row_rings(
         first[0:PLANES, :], last[0:PLANES, :], above[0:PLANES, :], below[0:PLANES, :],
@@ -468,16 +468,14 @@
     for c in range(3):
         rows_out[c * DEPTH : (c + 1) * DEPTH, :] = top[c]
         rows_out[PLANES + c * DEPTH : PLANES + (c + 1) * DEPTH, :] = bottom[c]
-    slave, raw = contact(
+    slave = contact(
         three(surface), [three(across), three(sent), three(within)], three(normals), gap[...], mortar,
-        owner[...], blocks[...], live[0, 0], lhs, prod,
-    )
-    raw_out[SURF:RAW, :] = jnp.broadcast_to(place_table(owner[...], blocks[...]), (8, BLOCK))
+        place[...], lhs, prod,
+    )
     sub = iota((ROWS_DEV, BLOCK), 0)
     for c in range(3):
         here = slice(c * ROWS_DEV, (c + 1) * ROWS_DEV)
-        raw_out[here, :] = raw[c]
-        new = DAMPING * surface_v[here, :] + low[c * (DEPTH // 2), :, :] + TIME_STEP * slave[c]
+        new = surface_v[here, :] + low[c * FIRST_LOW, :, :] + TIME_STEP * slave[c]
         new = new + from_strip(ring, c * DEPTH)
         new = new + jnp.where(sub == 0, jnp.broadcast_to(top[c][0:1], sub.shape), 0.0)
         new = new + jnp.where(
@@ -487,19 +485,33 @@
         u_out[here, :] = surface[here, :] + TIME_STEP * new
 
 
-CONTACT_SCRATCH = [
-    pltpu.VMEM((ROWS_DEV * 8, BLOCK), F32),
-    pltpu.VMEM((ROWS_DEV * 8, BLOCK), F32),
-]
+def reaction_kernel(lhs, mortar, place, raw_out, prod):
+    raw = reactions(lhs, mortar, prod)
+    raw_out[SURF:RAW, :] = jnp.broadcast_to(place_table(place[...] & (LIVE - 1)), (8, BLOCK))
+    for c in range(3):
+        raw_out[c * ROWS_DEV : (c + 1) * ROWS_DEV, :] = raw[c]
+
+
+def reaction(*args):
+    return call(
+        reaction_kernel,
+        out(RAW),
+        [VMEM] * 3,
+        VMEM,
+        [pltpu.VMEM((ROWS_DEV * 8, BLOCK), F32)],
+        args,
+        2_000_000,
+        2_000_000,
+    )
 
 
 def first_contact(*args):
     return call(
         first_contact_kernel,
-        (out(RAW), out(SURF), out(SURF), out(ROWS_DEV), out(2 * PLANES)),
-        [VMEM] * 15 + [SMEM],
+        (out(ROWS_DEV * 8), out(SURF), out(SURF), out(ROWS_DEV), out(2 * PLANES)),
+        [VMEM] * 14,
         (VMEM,) * 5,
-        CONTACT_SCRATCH,
+        [pltpu.VMEM((ROWS_DEV * 8, BLOCK), F32)],
         args,
         4_000_000,
         4_000_000,
@@ -516,30 +528,32 @@
         u_out[c * DEPTH, 0:ROWS_DEV, :] = surface[c * ROWS_DEV : (c + 1) * ROWS_DEV, :]
         v_out[c * DEPTH, :, :] = surface_v[c * ROWS_DEV : (c + 1) * ROWS_DEV, :]
 
-    half = DEPTH // 2
-
-    def layer(forces, start, k, held):
+    for k in range(1, DEPTH):
         for c in range(3):
             plane = c * DEPTH + k
-            new = v[plane, :, :] + forces[c * half + k - start, :, :]
-            new = new + from_strip(strength, plane)
-            new = new + jnp.where(sub == 0, jnp.broadcast_to(rows[pl.ds(plane, 1), :], sub.shape), 0.0)
+            if k < FIRST_LOW:
+                forces = low[c * FIRST_LOW + k, :, :]
+            else:
+                forces = high[c * (DEPTH - FIRST_LOW) + k - FIRST_LOW, :, :]
+            new = v[plane, :, :] + forces + from_strip(strength, plane)
+            new = new + jnp.where(
+                sub == 0, jnp.broadcast_to(rows[plane : plane + 1, :], sub.shape), 0.0
+            )
             new = new + jnp.where(
                 sub == ROWS_DEV - 1,
-                jnp.broadcast_to(rows[pl.ds(PLANES + plane, 1), :], sub.shape),
+                jnp.broadcast_to(rows[PLANES + plane : PLANES + plane + 1, :], sub.shape),
                 0.0,
             )
             moved = u[plane, 0:ROWS_DEV, :] + TIME_STEP * new
             v_out[plane, :, :] = new
             u_out[plane, 0:ROWS_DEV, :] = moved
-            first[pl.ds(plane, 1), :] = moved[0:1]
-            last[pl.ds(plane, 1), :] = moved[ROWS_DEV - 1 : ROWS_DEV]
-            held = put_column(held, moved, plane)
-        return held
-
-    zero = jnp.zeros((ROWS_DEV, BLOCK), F32)
-    zero = lax.fori_loop(1, half, functools.partial(layer, low, 0), zero)
-    strip[0:ROWS_DEV, :] = lax.fori_loop(half, DEPTH, functools.partial(layer, high, half), zero)
+            first[plane : plane + 1, :] = moved[0:1]
+            last[plane : plane + 1, :] = moved[ROWS_DEV - 1 : ROWS_DEV]
+    held = jnp.zeros((ROWS_DEV, BLOCK), F32)
+    for k in range(1, DEPTH):
+        for c in range(3):
+            held = put_column(held, u_out[c * DEPTH + k, 0:ROWS_DEV, :], c * DEPTH + k)
+    strip[0:ROWS_DEV, :] = held
     strip[ROWS_DEV:STRIP, :] = jnp.zeros((STRIP - ROWS_DEV, BLOCK), F32)
     for ref in (first, last):
         for c in range(3):
@@ -574,9 +588,23 @@
     )
 
 
+def outer_rows_kernel(first, last, center, first_out, last_out):
+    for ref, source, row in ((first_out, first, 0), (last_out, last, ROWS_DEV - 1)):
+        ref[...] = source[...]
+        for c in range(3):
+            at = c * ROWS_DEV + row
+            ref[c * DEPTH : c * DEPTH + 1, :] = center[at : at + 1, :]
+
+
+def outer_rows(*args):
+    return call(
+        outer_rows_kernel, (out(64), out(64)), [VMEM] * 3, (VMEM,) * 2, [], args, 1000, 300_000
+    )
+
+
 def second_contact_kernel(
-    partial, comb, center, across, within, strip, normals, gap, mortar, owner, blocks, live,
-    raw_out, slave_out, lhs, prod,
+    partial, comb, center, across, within, strip, normals, gap, mortar, place, raw_out,
+    strip_out, slave_out, lhs, prod,
 ):
     surface = [
         p + TIME_STEP * TIME_STEP * x for p, x in zip(three(partial), three(comb), strict=True)
@@ -584,13 +612,13 @@
     held = strip[0:ROWS_DEV, :]
     for c in range(3):
         held = put_column(held, surface[c], c * DEPTH)
-    raw_out[RAW : RAW + ROWS_DEV, :] = held
-    raw_out[RAW + ROWS_DEV : RAW + STRIP, :] = jnp.zeros((STRIP - ROWS_DEV, BLOCK), F32)
-    slave, raw = contact(
+    strip_out[...] = held
+    slave = contact(
         surface, [three(across), three(center), three(within)], three(normals), gap[...], mortar,
-        owner[...], blocks[...], live[0, 0], lhs, prod,
-    )
-    raw_out[SURF:RAW, :] = jnp.broadcast_to(place_table(owner[...], blocks[...]), (8, BLOCK))
+        place[...], lhs, prod,
+    )
+    raw = reactions(lhs, mortar, prod)
+    raw_out[SURF:RAW, :] = jnp.broadcast_to(place_table(place[...] & (LIVE - 1)), (8, BLOCK))
     for c in range(3):
         here = slice(c * ROWS_DEV, (c + 1) * ROWS_DEV)
         raw_out[here, :] = raw[c]
@@ -600,92 +628,164 @@
 def second_contact(*args):
     return call(
         second_contact_kernel,
-        (out(RAW + STRIP), out(SURF)),
-        [VMEM] * 11 + [SMEM],
-        (VMEM,) * 2,
-        CONTACT_SCRATCH,
+        (out(RAW), out(ROWS_DEV), out(SURF)),
+        [VMEM] * 10,
+        (VMEM,) * 3,
+        [pltpu.VMEM((ROWS_DEV * 8, BLOCK), F32), pltpu.VMEM((ROWS_DEV * 8, BLOCK), F32)],
         args,
         4_000_000,
         4_000_000,
     )
 
 
-def last_collect_kernel(
-    own, across, within, first, last, partial, comb_own, comb_out, first_out, last_out
+def second_message_kernel(raw, strip, above, below, message):
+    message[0:RAW, :] = raw[...]
+    message[RAW : RAW + ROWS_DEV, :] = strip[...]
+    message[RAW + ROWS_DEV : RAW + STRIP, :] = jnp.zeros((STRIP - ROWS_DEV, BLOCK), F32)
+    message[RAW + ROWS_DEV : RAW + ROWS_DEV + 1, :] = ends_of_row(below[...])
+    message[RAW + STRIP - 1 : RAW + STRIP, :] = ends_of_row(above[...])
+
+
+def second_message(*args):
+    return call(
+        second_message_kernel, out(RAW + STRIP), [VMEM] * 4, VMEM, [], args, 100_000, 300_000
+    )
+
+
+def last_collect_kernel(own, across, within, above, below, comb_out):
+    comb = collected([(three(x), x[SURF : SURF + 1, :]) for x in (across, own, within)])
+    for c in range(3):
+        comb_out[c * ROWS_DEV : (c + 1) * ROWS_DEV, :] = comb[c]
+        comb_out[SURF + c : SURF + c + 1, :] = below[c * DEPTH : c * DEPTH + 1, :]
+        comb_out[SURF + 3 + c : SURF + 4 + c, :] = above[c * DEPTH : c * DEPTH + 1, :]
+    at = pl.ds(RAW + ROWS_DEV, 8)
+    corners = halo_of(across[at, :], within[at, :])
+    comb_out[SURF + 6 : SURF + 7, :] = corners[0:1]
+    comb_out[SURF + 7 : SURF + 8, :] = corners[7:8]
+
+
+def last_collect(*args):
+    return call(
+        last_collect_kernel, out(RAW), [VMEM] * 5, VMEM, [], args, 1_000_000, 800_000
+    )
+
+
+def strips_around(sent, across, within, above, below):
+    at = pl.ds(RAW, STRIP)
+    strip_row = iota((STRIP, BLOCK), 0)
+    own = sent[at, :]
+    for row, line in ((ROWS_DEV, below), (STRIP - 1, above)):
+        own = jnp.where(
+            strip_row == row, jnp.broadcast_to(ends_of_row(line), (STRIP, BLOCK)), own
+        )
+    return own, halo_of(across[at, :], within[at, :])
+
+
+def old_moduli(sent, across, within):
+    at = pl.ds(SURF, STRIP)
+    odd = iota((STRIP, BLOCK), 1) % 2 == 1
+    return jnp.where(odd, halo_of(across[at, :], within[at, :]), sent[at, :])
+
+
+FIRST_FINAL = 2
+
+
+def last_update_kernel(
+    u, v_low, v_high, sent, across, within, first, last, above, below, old_sent, old_across,
+    old_within, old_above, old_last, u_hbm, v_hbm, u_out, v_out, sems,
 ):
-    comb = collected([(three(x), x[SURF : SURF + 1, :]) for x in (across, own, within)])
-    for c in range(3):
-        comb_out[c * ROWS_DEV : (c + 1) * ROWS_DEV, :] = comb[c]
-    lanes = iota((8, BLOCK), 1)
-    for ref, source, row in ((first_out, first, 0), (last_out, last, ROWS_DEV - 1)):
-        ref[0:64, :] = source[...]
-        for c in range(3):
-            at = c * ROWS_DEV + row
-            ref[c * DEPTH : c * DEPTH + 1, :] = (
-                partial[at : at + 1, :] + TIME_STEP * TIME_STEP * comb_own[at : at + 1, :]
-            )
-        at = RAW + row // 8 * 8
-        left, right = by_side(across[at : at + 8, :], within[at : at + 8, :])
-        ref[64:72, :] = jnp.where(lanes % 2 == 1, roll(left, 1, 1), roll(right, -1, 1))
-
-
-def last_collect(*args):
-    return call(
-        last_collect_kernel,
-        (out(SURF), out(STRIP), out(STRIP)),
-        [VMEM] * 7,
-        (VMEM,) * 3,
-        [],
-        args,
-        1_000_000,
-        800_000,
-    )
-
-
-GROUP = 4
-
-
-def last_update_kernel(
-    u, v_low, v_high, slave, comb_own, comb, sent, across, within, first, last, above, below,
-    old_sent, old_across, old_within, old_above, old_last, u_hbm, v_hbm, u_out, v_out, sems,
-):
-    at = pl.ds(RAW, STRIP)
-    sub8 = iota((8, BLOCK), 0)
-
-    def with_corners(strip, low, high):
-        end = jnp.where(
-            sub8 == 0,
-            jnp.broadcast_to(low, sub8.shape),
-            jnp.where(sub8 == 7, jnp.broadcast_to(high, sub8.shape), 0.0),
-        )
-        return jnp.concatenate([strip[0:ROWS_DEV], end], axis=0)
-
-    def shifted(row, by):
-        return roll(jnp.broadcast_to(row, sub8.shape), by, 1)[0:1]
-
-    own = with_corners(sent[at, :], ends_of_row(below[0:64, :]), ends_of_row(above[0:64, :]))
-    low_corner = below[64:65, :]
-    high_corner = above[STRIP - 1 : STRIP, :]
-    left, right = by_side(across[at, :], within[at, :])
-    left = with_corners(left, shifted(low_corner, -1), shifted(high_corner, -1))
-    right = with_corners(right, shifted(low_corner, 1), shifted(high_corner, 1))
-    old = pl.ds(SURF, STRIP)
-    odd = iota((STRIP, BLOCK), 1) % 2 == 1
-    old_left, _ = by_side(old_across[old, :], old_within[old, :])
-    moduli = jnp.where(odd, roll(old_left, 1, 1), old_sent[old, :])
-    ring = column_ring(own, left, right, moduli)
+    own, halo = strips_around(sent, across, within, above[...], below[...])
+    ring = column_ring(own, halo, old_moduli(old_sent, old_across, old_within))
     top, bottom = row_rings(
         first[0:PLANES, :], last[0:PLANES, :], above[0:PLANES, :], below[0:PLANES, :],
         old_last[PLANES:64, :], old_above[PLANES:64, :],
     )
     sub = iota((ROWS_DEV, BLOCK), 0)
-    half = DEPTH // 2
     copies = []
-    for k in range(DEPTH):
+    begin = FIRST_FINAL
+    for k in range(FIRST_FINAL, DEPTH):
         for c in range(3):
             plane = c * DEPTH + k
-            v = v_low[c * half + k, :, :] if k < half else v_high[c * half + k - half, :, :]
+            if k < SECOND_LOW:
+                v = v_low[c * SECOND_LOW + k, :, :]
+            else:
+                v = v_high[c * (DEPTH - SECOND_LOW) + k - SECOND_LOW, :, :]
             new = v + from_strip(ring, plane)
+            new = new + jnp.where(
+                sub == 0, jnp.broadcast_to(top[c][k : k + 1], sub.shape), 0.0
+            )
+            new = new + jnp.where(
+                sub == ROWS_DEV - 1, jnp.broadcast_to(bottom[c][k : k + 1], sub.shape), 0.0
+            )
+            v_out[plane, :, :] = new
+            u_out[plane, :, :] = u[plane, 0:ROWS_DEV, :] + TIME_STEP * new
+        if k in (3, 7, 11, 15):
+            for c in range(3):
+                group = pl.ds(c * DEPTH + begin, k + 1 - begin)
+                for source, target in ((u_out, u_hbm), (v_out, v_hbm)):
+                    copy = pltpu.make_async_copy(
+                        source.at[group], target.at[group], sems.at[len(copies)]
+                    )
+                    copy.start()
+                    copies.append(copy)
+            begin = k + 1
+    for copy in copies:
+        copy.wait()
+
+
+def last_update(*args):
+    return call(
+        last_update_kernel,
+        (planes(PLANES), planes(PLANES)),
+        [VMEM] * 15,
+        (ANY,) * 2,
+        [
+            pltpu.VMEM((PLANES, ROWS_DEV, BLOCK), F32),
+            pltpu.VMEM((PLANES, ROWS_DEV, BLOCK), F32),
+            pltpu.SemaphoreType.DMA((24,)),
+        ],
+        args,
+        10_000_000,
+        6_000_000,
+    )
+
+
+def last_surface_kernel(
+    u, v_low, slave, comb_own, comb, sent, across, within, first, last, above, below,
+    old_sent, old_across, old_within, old_above, old_last, u_in, v_in, u_hbm, v_hbm, u_out, v_out,
+    below_all, above_all, first_all, last_all, sems,
+):
+    for c in range(3):
+        top_row = slice(c * DEPTH, c * DEPTH + 1)
+        below_all[c * DEPTH : (c + 1) * DEPTH, :] = below[c * DEPTH : (c + 1) * DEPTH, :]
+        above_all[c * DEPTH : (c + 1) * DEPTH, :] = above[c * DEPTH : (c + 1) * DEPTH, :]
+        first_all[c * DEPTH : (c + 1) * DEPTH, :] = first[c * DEPTH : (c + 1) * DEPTH, :]
+        last_all[c * DEPTH : (c + 1) * DEPTH, :] = last[c * DEPTH : (c + 1) * DEPTH, :]
+        below_all[top_row, :] = comb[SURF + c : SURF + c + 1, :]
+        above_all[top_row, :] = comb[SURF + 3 + c : SURF + 4 + c, :]
+        for ref, row in ((first_all, 0), (last_all, ROWS_DEV - 1)):
+            at = c * ROWS_DEV + row
+            ref[top_row, :] = (
+                u[c * DEPTH, row : row + 1, :] + TIME_STEP * TIME_STEP * comb_own[at : at + 1, :]
+            )
+    for ref in (below_all, above_all):
+        ref[PLANES:64, :] = jnp.zeros((64 - PLANES, BLOCK), F32)
+    own, halo = strips_around(sent, across, within, above_all[...], below_all[...])
+    strip_row = iota((STRIP, BLOCK), 0)
+    layer_0 = iota((STRIP, BLOCK), 1) % (2 * DEPTH) < 2
+    for i, row in ((6, ROWS_DEV), (7, STRIP - 1)):
+        corner = jnp.broadcast_to(comb[SURF + i : SURF + i + 1, :], (STRIP, BLOCK))
+        halo = jnp.where(layer_0 & (strip_row == row), corner, halo)
+    ring = column_ring(own, halo, old_moduli(old_sent, old_across, old_within))
+    top, bottom = row_rings(
+        first_all[...], last_all[...], above_all[0:PLANES, :], below_all[0:PLANES, :],
+        old_last[PLANES:64, :], old_above[PLANES:64, :],
+    )
+    sub = iota((ROWS_DEV, BLOCK), 0)
+    for k in range(FIRST_FINAL):
+        for c in range(3):
+            plane = c * DEPTH + k
+            new = v_low[c * SECOND_LOW + k, :, :] + from_strip(ring, plane)
             new = new + jnp.where(
                 sub == 0, jnp.broadcast_to(top[c][k : k + 1], sub.shape), 0.0
             )
@@ -697,36 +797,42 @@
                 here = slice(c * ROWS_DEV, (c + 1) * ROWS_DEV)
                 new = new + TIME_STEP * (slave[here, :] + comb[here, :])
                 old_u = old_u + TIME_STEP * TIME_STEP * comb_own[here, :]
-            v_out[plane, :, :] = new
-            u_out[plane, :, :] = old_u + TIME_STEP * new
-        if k % GROUP == GROUP - 1:
-            for c in range(3):
-                group = pl.ds(c * DEPTH + k + 1 - GROUP, GROUP)
-                for source, target in ((u_out, u_hbm), (v_out, v_hbm)):
-                    copy = pltpu.make_async_copy(
-                        source.at[group], target.at[group], sems.at[len(copies)]
-                    )
-                    copy.start()
-                    copies.append(copy)
+            v_out[c * FIRST_FINAL + k, :, :] = new
+            u_out[c * FIRST_FINAL + k, :, :] = old_u + TIME_STEP * new
+    copies = []
+    for c in range(3):
+        source_at = pl.ds(c * FIRST_FINAL, FIRST_FINAL)
+        target_at = pl.ds(c * DEPTH, FIRST_FINAL)
+        for source, target in ((u_out, u_hbm), (v_out, v_hbm)):
+            copies.append(
+                pltpu.make_async_copy(
+                    source.at[source_at], target.at[target_at], sems.at[len(copies)]
+                )
+            )
+            copies[-1].start()
     for copy in copies:
         copy.wait()
 
 
-def last_update(*args):
-    return call(
-        last_update_kernel,
-        (planes(PLANES), planes(PLANES)),
-        [VMEM] * 18,
-        (ANY,) * 2,
-        [
-            pltpu.VMEM((PLANES, ROWS_DEV, BLOCK), F32),
-            pltpu.VMEM((PLANES, ROWS_DEV, BLOCK), F32),
-            pltpu.SemaphoreType.DMA((6 * DEPTH // GROUP,)),
+def last_surface(*args):
+    return pl.pallas_call(
+        last_surface_kernel,
+        out_shape=(planes(PLANES), planes(PLANES)),
+        in_specs=[VMEM] * 17 + [ANY] * 2,
+        out_specs=(ANY,) * 2,
+        scratch_shapes=[
+            pltpu.VMEM((3 * FIRST_FINAL, ROWS_DEV, BLOCK), F32),
+            pltpu.VMEM((3 * FIRST_FINAL, ROWS_DEV, BLOCK), F32),
+            pltpu.VMEM((64, BLOCK), F32),
+            pltpu.VMEM((64, BLOCK), F32),
+            pltpu.VMEM((PLANES, BLOCK), F32),
+            pltpu.VMEM((PLANES, BLOCK), F32),
+            pltpu.SemaphoreType.DMA((6,)),
         ],
-        args,
-        10_000_000,
-        6_000_000,
-    )
+        input_output_aliases={17: 0, 18: 1},
+        compiler_params=pltpu.CompilerParams(vmem_limit_bytes=16 * 2**20),
+        cost_estimate=pl.CostEstimate(flops=1000, bytes_accessed=1000, transcendentals=0),
+    )(*args)
 
 
 def moved(x, axis, by):
@@ -744,7 +850,9 @@
     half = lax.axis_size("gy") // 2
     flat_normals = normals.reshape(SURF, BLOCK)
     flat_mortar = mortar.reshape(ROWS_DEV * BLOCK, BLOCK)
-    pairing = (flat_normals, gap_zero, flat_mortar, owner, blocks, live_rows)
+    alive = jnp.arange(ROWS_DEV, dtype=jnp.int32)[:, None] < live_rows
+    place = owner * ROWS_DEV + blocks + jnp.where(alive, LIVE, 0)
+    pairing = (flat_normals, gap_zero, flat_mortar, place)
 
     shape = displacement.shape
     rows = lax.axis_index("gx") * ROWS_DEV + jnp.arange(ROWS_DEV, dtype=jnp.int32)
@@ -757,53 +865,61 @@
     displacement = jnp.pad(
         displacement.reshape(PLANES, ROWS_DEV, BLOCK), ((0, 0), (0, STRIP - ROWS_DEV), (0, 0))
     )
+    surface, first, last = pack(displacement, shear[:, ROWS_DEV - 1 :, :])
+    surface, shear = lax.optimization_barrier((surface, shear))
     shear = jnp.where(valid, shear, 0.0)
-    surface, first, last = pack(displacement, shear[:, ROWS_DEV - 1 :, :])
     opposite = moved(surface, "gy", half)
     above = moved(last, "gx", 1)
     below = moved(first, "gx", -1)
     strip = strips(displacement, shear)
 
+    damped = DAMPING * velocity.reshape(PLANES, ROWS_DEV, BLOCK)
+    surface_v = damped.reshape(3, DEPTH, ROWS_DEV, BLOCK)[:, 0].reshape(SURF, BLOCK)
+    strip, surface_v = lax.optimization_barrier((strip, surface_v))
     sent = message(opposite, above, below, strip)
     across = exchanged(sent, 1)
     within = exchanged(sent, 0)
-    low = inner_forces(HALVES[0], displacement, shear)
-
-    raw, part_u, part_v, ring, rows = first_contact(
+    sent, displacement = lax.optimization_barrier((sent, displacement))
+    low = inner_forces((0, FIRST_LOW), displacement, shear)
+
+    lhs, part_u, part_v, ring, rows = first_contact(
         surface, sent, across, within, above, below, first, last, low,
-        velocity[:, 0].reshape(SURF, BLOCK), *pairing,
+        surface_v, *pairing,
     )
     part_opposite = moved(part_u, "gy", half)
+    raw = reaction(lhs, flat_mortar, place)
     raw_across = exchanged(raw, 1)
     raw_within = exchanged(raw, 0)
-    high = inner_forces(HALVES[1], displacement, shear)
-    raw, high = lax.optimization_barrier((raw, high))
-
+    raw, displacement = lax.optimization_barrier((raw, displacement))
+    high = inner_forces((FIRST_LOW, DEPTH), displacement, shear)
+    u, v, strip, first2, last2 = update(displacement, damped, low, high, ring, rows, part_u, part_v)
+
+    raw, first2 = lax.optimization_barrier((raw, first2))
     comb, center = collect(part_opposite, raw, raw_across, raw_within)
     comb_own = moved(comb, "gy", half)
     across2 = exchanged(center, 1)
     within2 = exchanged(center, 0)
-    raw, velocity = lax.optimization_barrier((raw, velocity))
-    damped = DAMPING * velocity.reshape(PLANES, ROWS_DEV, BLOCK)
-    u, v, strip, first2, last2 = update(displacement, damped, low, high, ring, rows, part_u, part_v)
-
-    raw, slave = second_contact(part_u, comb_own, center, across2, within2, strip, *pairing)
-    raw_across = exchanged(raw, 1)
-    raw_within = exchanged(raw, 0)
-    high = inner_forces(HALVES[1], u, shear, v, comb_own)
-    raw, high = lax.optimization_barrier((raw, high))
-
-    comb, first2, last2 = last_collect(
-        raw, raw_across, raw_within, first2, last2, part_u, comb_own
-    )
+    first3, last3 = outer_rows(first2, last2, center)
+    above2 = moved(last3, "gx", 1)
+    below2 = moved(first3, "gx", -1)
+
+    raw, strip, slave = second_contact(part_u, comb_own, center, across2, within2, strip, *pairing)
+    sent2 = second_message(raw, strip, above2, below2)
+    across3 = exchanged(sent2, 1)
+    within3 = exchanged(sent2, 0)
+    sent2, u = lax.optimization_barrier((sent2, u))
+    high = inner_forces((SECOND_LOW, DEPTH), u, shear, v, part_u)
+    sent2, high, u = lax.optimization_barrier((sent2, high, u))
+
+    comb = last_collect(sent2, across3, within3, above2, below2)
     comb_last = moved(comb, "gy", half)
-    above2 = moved(last2, "gx", 1)
-    below2 = moved(first2, "gx", -1)
-    low = inner_forces(HALVES[0], u, shear, v, comb_own)
-    u, v = last_update(
-        u, low, high, slave, comb_own, comb_last, raw, raw_across, raw_within, first2, last2,
-        above2, below2, sent, across, within, above, last,
-    )
+    comb, u = lax.optimization_barrier((comb, u))
+    low = inner_forces((0, SECOND_LOW), u, shear, v, comb_own)
+    around = (
+        sent2, across3, within3, first2, last2, above2, below2, sent, across, within, above, last
+    )
+    final = last_update(u, low, high, *around)
+    u, v = last_surface(u, low, slave, comb_own, comb_last, *around, *final)
     return u.reshape(shape), v.reshape(shape)
 
 

time: 64.7 us -> 60.1 us (0.929)
  Pallas kernels: 24.9 us -> 20.8 us
  waiting for transfers between devices: 12.4 us -> 8.4 us
  starting transfers between devices: 21.4 us -> 24.3 us
    pallas_call x13 -> x16, Pallas kernels: 24.9 us -> 19.3 us  [call(): pl.pallas_call(kernel, out_shape=out_shape, in_specs=in_specs, out_specs=...]
    ppermute x8, waiting for transfers between devices: 8.36 us -> 4.36 us  [moved(): return lax.ppermute(x, axis, [(i, (i + by) % count) for i in range(count)])]
    ppermute x8, starting transfers between devices: 16.1 us -> 18 us  [moved(): return lax.ppermute(x, axis, [(i, (i + by) % count) for i in range(count)])]
    pallas_call x0 -> x1, Pallas kernels: none -> 1.55 us  [last_surface(): pl.pallas_call(last_surface_kernel, out_shape=(planes(PLANES), planes(PLA...]
    mul x1, other arithmetic: 0.24 us -> 1.71 us  [local(): damped = DAMPING * velocity.reshape(PLANES, ROWS_DEV, BLOCK)]
    select_n x1, other arithmetic: 1.07 us -> 0.04 us  [local(): shear = jnp.where(valid, shear, 0.0)]
    ppermute x8, starting transfers between devices: 5.27 us -> 6.29 us  [exchanged(): return lax.ppermute(x, 'gy', [(i, j % count) for i, j in pairs])]
    slice x1, local copies, waits for them, and re-layouts: 0.9 us -> 0.01 us  [local(): damped.reshape(3, DEPTH, ROWS_DEV, BLOCK)[:, 0].reshape(SURF, BLOCK)]
  transfers between devices with their start and end apart: 16 -> 16, of which waited for: 6 -> 4; matrix products, arithmetic and copies ran while one was open for 2% -> 3% of each run, Pallas kernels for 23% -> 27%
where the time goes in v2:
time: 60.1 us; the launch traced here: 59.9 us
  starting transfers between devices  24.3 us (40%)
  Pallas kernels  20.8 us (35%)
  waiting for transfers between devices  8.4 us (14%)
  local copies, waits for them, and re-layouts  2.98 us (5%)
  other arithmetic  1.85 us (3%)
  between operations  1.55 us (3%)
    pallas_call x16, Pallas kernels, call(): pl.pallas_call(kernel, out_shape=out_shape, in_specs=in_specs, out_specs=...  19.3 us
    ppermute x8, starting transfers between devices, moved(): return lax.ppermute(x, axis, [(i, (i + by) % count) for i in range(count)])  18 us
    ppermute x8, starting transfers between devices, exchanged(): return lax.ppermute(x, 'gy', [(i, j % count) for i, j in pairs])  6.29 us
    ppermute x8, waiting for transfers between devices, moved(): return lax.ppermute(x, axis, [(i, (i + by) % count) for i in range(count)])  4.36 us
    ppermute x8, waiting for transfers between devices, exchanged(): return lax.ppermute(x, 'gy', [(i, j % count) for i, j in pairs])  4.04 us
    mul x1, other arithmetic, local(): damped = DAMPING * velocity.reshape(PLANES, ROWS_DEV, BLOCK)  1.71 us
    pallas_call x1, Pallas kernels, last_surface(): pl.pallas_call(last_surface_kernel, out_shape=(planes(PLANES), planes(PLA...  1.55 us
    pad x1, local copies, waits for them, and re-layouts, local(): jnp.pad(displacement.reshape(PLANES, ROWS_DEV, BLOCK), ((0, 0), (0, STRIP...  1.54 us
  transfers between devices with their start and end apart: 16, of which 4 were waited for; matrix products, arithmetic and copies ran while one was open for 3% of the time, Pallas kernels for 27%

profile of v2, /device:TPU:0, one launch (start us, length us, event | category | flops | bytes accessed | tf_op | source)
XLA Modules:
  0.0 59.9 jit_solution(7326388290585644696)
XLA Ops:
  0.6 0.8 %slice.6.shear = f32[15,1,128]{2,1,0:T(1,128)S(1)} slice(f32[15,64,128]{2,1,0:T(8,128)} %param.11), slice={[0:15], [63:64], [0:128]} | slice | bytes 15360 | tf_op jit(solution)/shard_map/slice | solution.py:868
  1.5 1.5 %pad.4.u.refs_0_ = f32[48,72,128]{2,1,0:T(8,128)S(1)} pad(f32[48,64,128]{2,1,0:T(8,128)} %bitcast.16, f32[]{:T(128)} %constant.12.clone.1), padding=0_0x0_8x0_0 | pad | bytes 3342340 | tf_op jit(solution)/shard_map/jit(_pad)/pad | solution.py:865
  3.1 3.2 %collective-permute-start.1 = (f32[64,128]{1,0:T(8,128)S(1)}, f32[64,128]{1,0:T(8,128)S(1)}, u32[]{:S(2)}, u32[]{:S(2)}) collective-permute-start(f32[64,128]{1,0:T(8,128)S(1)} %get-tuple-element.44.last.old_last), channel_id=1, source_target_pairs={{0,16},{16,32},{32,48},{48,64},{64,80},{80,96},{96,112},{112,0},{1... | collective-permute-start | bytes 98312 | tf_op jit(solution)/shard_map/ppermute | solution.py:840
  6.2 3.9 %collective-permute-start = (f32[192,128]{1,0:T(8,128)S(1)}, f32[192,128]{1,0:T(8,128)S(1)}, u32[]{:S(2)}, u32[]{:S(2)}) collective-permute-start(f32[192,128]{1,0:T(8,128)S(1)} %get-tuple-element.43.surface), channel_id=1, source_target_pairs={{0,8},{1,9},{2,10},{3,11},{4,12},{5,13},{6,14},{7,15},{8,0},{9,1},... | collective-permute-start | bytes 294920 | tf_op jit(solution)/shard_map/ppermute | solution.py:840
  10.1 2.6 %collective-permute-start.2 = (f32[64,128]{1,0:T(8,128)S(1)}, f32[64,128]{1,0:T(8,128)S(1)}, u32[]{:S(2)}, u32[]{:S(2)}) collective-permute-start(f32[64,128]{1,0:T(8,128)S(1)} %get-tuple-element.45.first), channel_id=1, source_target_pairs={{0,112},{16,0},{32,16},{48,32},{64,48},{80,64},{96,80},{112,96},{1... | collective-permute-start | bytes 98312 | tf_op jit(solution)/shard_map/ppermute | solution.py:840
  12.8 1.7 %broadcast_multiply_fusion = f32[3,16,64,128]{3,2,1,0:T(8,128)S(1)} fusion(f32[3,16,64,128]{3,2,1,0:T(8,128)} %param.10), kind=kLoop, calls=%fused_computation | loop fusion | flops 393216 | bytes 3145728 | tf_op jit(solution)/shard_map/mul | solution.py:876
  14.7 0.6 %shard_map.105.strip = f32[72,128]{1,0:T(8,128)S(1)} custom-call(f32[48,72,128]{2,1,0:T(8,128)S(1)} %pad.4.u.refs_0_, f32[15,64,128]{2,1,0:T(8,128)S(1)} %broadcast_select_fusion.shear.refs_1_), custom_call_target="tpu_custom_call" | custom-call | flops 1000 | bytes 1000 | tf_op jit(solution)/shard_map/pallas_call | solution.py:37
  15.3 0.4 copy-done.1
  16.6 0.3 collective-permute-start.3
  17.0 1.4 %collective-permute-start.4 = (f32[264,128]{1,0:T(8,128)S(1)}, f32[264,128]{1,0:T(8,128)S(1)}, u32[]{:S(2)}, u32[]{:S(2)}) collective-permute-start(f32[264,128]{1,0:T(8,128)S(1)} %shard_map.106.sent.old_sent), channel_id=1, source_target_pairs={{0,1},{1,0},{2,3},{3,2},{4,5},{5,4},{6,7},{7,6},{8,9},{9,8},{10,11... | collective-permute-start | bytes 405512 | tf_op jit(solution)/shard_map/ppermute | solution.py:846
  18.4 3.1 %shard_map.107.low = f32[33,64,128]{2,1,0:T(8,128)S(1)} custom-call(f32[48,72,128]{2,1,0:T(8,128)S(1)} %pad.4.u.refs_0_, f32[15,64,128]{2,1,0:T(8,128)S(1)} %broadcast_select_fusion.shear.refs_1_), custom_call_target="tpu_custom_call" | custom-call | flops 1000 | bytes 1000 | tf_op jit(solution)/shard_map/pallas_call | solution.py:37
  21.5 1.8 %collective-permute-done.3.across.old_across = f32[264,128]{1,0:T(8,128)S(1)} collective-permute-done((f32[264,128]{1,0:T(8,128)S(1)}, f32[264,128]{1,0:T(8,128)S(1)}, u32[]{:S(2)}, u32[]{:S(2)}) %collective-permute-start.3) | collective-permute-done | bytes 135200 | tf_op jit(solution)/shard_map/ppermute | solution.py:846
  23.3 1.5 %shard_map.108 = (f32[512,128]{1,0:T(8,128)S(1)}, f32[192,128]{1,0:T(8,128)S(1)}, f32[192,128]{1,0:T(8,128)S(1)}, f32[64,128]{1,0:T(8,128)S(1)}, f32[96,128]{1,0:T(8,128)S(1)}) custom-call(f32[192,128]{1,0:T(8,128)S(1)} %get-tuple-element.43.surface, f32[264,128]{1,0:T(8,128)S(1)} %shard_map.106.sent.old_sent, ...), custom_call_target="tpu_custom_call" | custom-call | flops 1000 | bytes 1000 | tf_op jit(solution)/shard_map/pallas_call | solution.py:37
  24.8 0.7 %shard_map.109.own = f32[200,128]{1,0:T(8,128)S(1)} custom-call(f32[512,128]{1,0:T(8,128)S(1)} %get-tuple-element.52.lhs, bf16[8192,128]{1,0:T(8,128)(2,1)S(1)} %bitcast.10, s32[64,1]{1,0:T(8,128)S(1)} %select_add_fusion.place), custom_call_target="tpu_custom_call" | custom-call | flops 1000 | bytes 1000 | tf_op jit(solution)/shard_map/pallas_call | solution.py:37
  25.5 1.1 %collective-permute-start.6 = (f32[200,128]{1,0:T(8,128)S(1)}, f32[200,128]{1,0:T(8,128)S(1)}, u32[]{:S(2)}, u32[]{:S(2)}) collective-permute-start(f32[200,128]{1,0:T(8,128)S(1)} %shard_map.109.own), channel_id=1, source_target_pairs={{0,15},{1,2},{2,1},{3,4},{4,3},{5,6},{6,5},{7,8},{8,7},{9,10},{10,... | collective-permute-start | bytes 307208 | tf_op jit(solution)/shard_map/ppermute | solution.py:846
  26.6 0.3 collective-permute-start.5
  27.0 2.0 %shard_map.110.high = f32[15,64,128]{2,1,0:T(8,128)S(1)} custom-call(f32[48,72,128]{2,1,0:T(8,128)S(1)} %pad.4.u.refs_0_, f32[15,64,128]{2,1,0:T(8,128)S(1)} %broadcast_select_fusion.shear.refs_1_), custom_call_target="tpu_custom_call" | custom-call | flops 1000 | bytes 1000 | tf_op jit(solution)/shard_map/pallas_call | solution.py:37
  29.0 0.9 %shard_map.111 = (f32[48,72,128]{2,1,0:T(8,128)S(1)}, f32[48,64,128]{2,1,0:T(8,128)S(1)}, f32[72,128]{1,0:T(8,128)S(1)}, f32[64,128]{1,0:T(8,128)S(1)}, f32[64,128]{1,0:T(8,128)S(1)}) custom-call(f32[48,72,128]{2,1,0:T(8,128)S(1)} %pad.4.u.refs_0_, f32[48,64,128]{2,1,0:T(8,128)S(1)} %bitcast.12, f32[33,64,128]{2,1,0:T(8,128)S(1)} %shard_map.107.low, ...), custom_call_target="tpu_custom_call" | custom-call | flops 1000 | bytes 1000 | tf_op jit(solution)/shard_map/pallas_call | solution.py:37
  29.9 4.0 %collective-permute-done.5.partial = f32[192,128]{1,0:T(8,128)S(1)} collective-permute-done((f32[192,128]{1,0:T(8,128)S(1)}, f32[192,128]{1,0:T(8,128)S(1)}, u32[]{:S(2)}, u32[]{:S(2)}) %collective-permute-start.5) | collective-permute-done | bytes 98336 | tf_op jit(solution)/shard_map/ppermute | solution.py:840
  34.2 1.0 %collective-permute-start.8 = (f32[192,128]{1,0:T(8,128)S(1)}, f32[192,128]{1,0:T(8,128)S(1)}, u32[]{:S(2)}, u32[]{:S(2)}) collective-permute-start(f32[192,128]{1,0:T(8,128)S(1)} %get-tuple-element.60), channel_id=1, source_target_pairs={{0,8},{1,9},{2,10},{3,11},{4,12},{5,13},{6,14},{7,15},{8,0},{9,1},... | collective-permute-start | bytes 294920 | tf_op jit(solution)/shard_map/ppermute | solution.py:840
  35.2 1.3 %collective-permute-start.9 = (f32[192,128]{1,0:T(8,128)S(1)}, f32[192,128]{1,0:T(8,128)S(1)}, u32[]{:S(2)}, u32[]{:S(2)}) collective-permute-start(f32[192,128]{1,0:T(8,128)S(1)} %get-tuple-element.61.center), channel_id=1, source_target_pairs={{0,15},{1,2},{2,1},{3,4},{4,3},{5,6},{6,5},{7,8},{8,7},{9,10},{10,... | collective-permute-start | bytes 294920 | tf_op jit(solution)/shard_map/ppermute | solution.py:846
  36.5 1.6 %collective-permute-start.11 = (f32[64,128]{1,0:T(8,128)S(1)}, f32[64,128]{1,0:T(8,128)S(1)}, u32[]{:S(2)}, u32[]{:S(2)}) collective-permute-start(f32[64,128]{1,0:T(8,128)S(1)} %get-tuple-element.67), channel_id=1, source_target_pairs={{0,16},{16,32},{32,48},{48,64},{64,80},{80,96},{96,112},{112,0},{1... | collective-permute-start | bytes 98312 | tf_op jit(solution)/shard_map/ppermute | solution.py:840
  38.1 4.1 %collective-permute-start.12 = (f32[64,128]{1,0:T(8,128)S(1)}, f32[64,128]{1,0:T(8,128)S(1)}, u32[]{:S(2)}, u32[]{:S(2)}) collective-permute-start(f32[64,128]{1,0:T(8,128)S(1)} %get-tuple-element.68), channel_id=1, source_target_pairs={{0,112},{16,0},{32,16},{48,32},{64,48},{80,64},{96,80},{112,96},{1... | collective-permute-start | bytes 98312 | tf_op jit(solution)/shard_map/ppermute | solution.py:840
  42.2 2.0 %shard_map.113 = (f32[200,128]{1,0:T(8,128)S(1)}, f32[64,128]{1,0:T(8,128)S(1)}, f32[192,128]{1,0:T(8,128)S(1)}) custom-call(f32[192,128]{1,0:T(8,128)S(1)} %get-tuple-element.51.surface.partial.refs_3_, f32[192,128]{1,0:T(8,128)S(1)} %collective-permute-done.8.comb.refs_3_.comb_own, f32[192,128]{1,0:T(8,128)S(1)} %get-tuple-element.61.center, ...), custom_call_target="tpu_custom_call" | custom-call | flops 1000 | bytes 1000 | tf_op jit(solution)/shard_map/pallas_call | solution.py:37
  44.4 2.1 %collective-permute-start.13 = (f32[272,128]{1,0:T(8,128)S(1)}, f32[272,128]{1,0:T(8,128)S(1)}, u32[]{:S(2)}, u32[]{:S(2)}) collective-permute-start(f32[272,128]{1,0:T(8,128)S(1)} %shard_map.115.own.sent), channel_id=1, source_target_pairs={{0,15},{1,2},{2,1},{3,4},{4,3},{5,6},{6,5},{7,8},{8,7},{9,10},{10,... | collective-permute-start | bytes 417800 | tf_op jit(solution)/shard_map/ppermute | solution.py:846
  46.5 3.1 %shard_map.116.v_high = f32[33,64,128]{2,1,0:T(8,128)S(1)} custom-call(f32[48,72,128]{2,1,0:T(8,128)S(1)} %get-tuple-element.75.refs_0_.u, f32[15,64,128]{2,1,0:T(8,128)S(1)} %broadcast_select_fusion.shear.refs_1_, f32[48,64,128]{2,1,0:T(8,128)S(1)} %get-tuple-element.72.refs_2_, f32[192,128]{1,0:T(8,128)S(1)} %get-tuple-element.51.surface.partial.refs_3_), custom_call_target="tpu_custom_call" | custom-call | flops 1000 | bytes 1000 | tf_op jit(solution)/shard_map/pallas_call | solution.py:37
  49.6 2.3 %collective-permute-done.13.across = f32[272,128]{1,0:T(8,128)S(1)} collective-permute-done((f32[272,128]{1,0:T(8,128)S(1)}, f32[272,128]{1,0:T(8,128)S(1)}, u32[]{:S(2)}, u32[]{:S(2)}) %collective-permute-start.13) | collective-permute-done | bytes 139296 | tf_op jit(solution)/shard_map/ppermute | solution.py:846
  52.1 1.3 %collective-permute-start.15 = (f32[200,128]{1,0:T(8,128)S(1)}, f32[200,128]{1,0:T(8,128)S(1)}, u32[]{:S(2)}, u32[]{:S(2)}) collective-permute-start(f32[200,128]{1,0:T(8,128)S(1)} %shard_map.117), channel_id=1, source_target_pairs={{0,8},{1,9},{2,10},{3,11},{4,12},{5,13},{6,14},{7,15},{8,0},{9,1},... | collective-permute-start | bytes 307208 | tf_op jit(solution)/shard_map/ppermute | solution.py:840
  53.4 2.0 %shard_map.118.v_low = f32[15,64,128]{2,1,0:T(8,128)S(1)} custom-call(f32[48,72,128]{2,1,0:T(8,128)S(1)} %get-tuple-element.75.refs_0_.u, f32[15,64,128]{2,1,0:T(8,128)S(1)} %broadcast_select_fusion.shear.refs_1_, f32[48,64,128]{2,1,0:T(8,128)S(1)} %get-tuple-element.72.refs_2_, f32[192,128]{1,0:T(8,128)S(1)} %collective-permute-done.8.comb.refs_3_.comb_own), custom_call_target="tpu_custom_call" | custom-call | flops 1000 | bytes 1000 | tf_op jit(solution)/shard_map/pallas_call | solution.py:37
  55.4 2.6 %shard_map.119 = (f32[48,64,128]{2,1,0:T(8,128)}, f32[48,64,128]{2,1,0:T(8,128)}) custom-call(f32[48,72,128]{2,1,0:T(8,128)S(1)} %get-tuple-element.75.refs_0_.u, f32[15,64,128]{2,1,0:T(8,128)S(1)} %shard_map.118.v_low, f32[33,64,128]{2,1,0:T(8,128)S(1)} %shard_map.116.v_high, f32[272,128]{1,0:T(8,128)S(1)} %shard_map.115.own.sent, ...), custom_call_target="tpu_custom_call" | custom-call | flops 1000 | bytes 1000 | tf_op jit(solution)/shard_map/pallas_call | solution.py:37
  58.0 0.3 collective-permute-done.15.comb
  58.3 1.6 %shard_map.120 = (f32[48,64,128]{2,1,0:T(8,128)}, f32[48,64,128]{2,1,0:T(8,128)}) custom-call(f32[48,72,128]{2,1,0:T(8,128)S(1)} %get-tuple-element.75.refs_0_.u, f32[15,64,128]{2,1,0:T(8,128)S(1)} %shard_map.118.v_low, f32[192,128]{1,0:T(8,128)S(1)} %get-tuple-element.76.slave, ...), custom_call_target="tpu_custom_call", output_to_operand_aliasing={{0}: (17, {}), {1}: (18, {})} | custom-call | flops 1000 | bytes 1000 | tf_op jit(solution)/shard_map/pallas_call | solution.py:818
  (45 shorter events, 1.3 us)
Async XLA Ops:
  3.1 13.4 %collective-permute-start.1 = (f32[64,128]{1,0:T(8,128)S(1)}, f32[64,128]{1,0:T(8,128)S(1)}, u32[]{:S(2)}, u32[]{:S(2)}) collective-permute-start(f32[64,128]{1,0:T(8,128)S(1)} %get-tuple-element.44.last.old_last), channel_id=1, source_target_pairs={{0,16},{16,32},{32,48},{48,64},{64,80},{80,96},{96,112},{112,0},{1... | collective-permute-start | bytes 98312 | tf_op jit(solution)/shard_map/ppermute | solution.py:840
  6.2 10.3 %collective-permute-start = (f32[192,128]{1,0:T(8,128)S(1)}, f32[192,128]{1,0:T(8,128)S(1)}, u32[]{:S(2)}, u32[]{:S(2)}) collective-permute-start(f32[192,128]{1,0:T(8,128)S(1)} %get-tuple-element.43.surface), channel_id=1, source_target_pairs={{0,8},{1,9},{2,10},{3,11},{4,12},{5,13},{6,14},{7,15},{8,0},{9,1},... | collective-permute-start | bytes 294920 | tf_op jit(solution)/shard_map/ppermute | solution.py:840
  10.1 6.4 %collective-permute-start.2 = (f32[64,128]{1,0:T(8,128)S(1)}, f32[64,128]{1,0:T(8,128)S(1)}, u32[]{:S(2)}, u32[]{:S(2)}) collective-permute-start(f32[64,128]{1,0:T(8,128)S(1)} %get-tuple-element.45.first), channel_id=1, source_target_pairs={{0,112},{16,0},{32,16},{48,32},{64,48},{80,64},{96,80},{112,96},{1... | collective-permute-start | bytes 98312 | tf_op jit(solution)/shard_map/ppermute | solution.py:840
  12.7 1.8 %copy-start.5 = (f32[15,64,128]{2,1,0:T(8,128)S(1)}, f32[15,64,128]{2,1,0:T(8,128)}, u32[]{:S(2)}) copy-start(f32[15,64,128]{2,1,0:T(8,128)} %param.11) | copy-start | bytes 1474564
  12.8 1.9 %copy-start.7 = (s32[64,1]{0,1:T(1,128)S(1)}, s32[64,1]{0,1:T(1,128)}, u32[]{:S(2)}) copy-start(s32[64,1]{0,1:T(1,128)} %param.15) | copy-start | bytes 772
  14.5 1.1 %copy-start.1 = (f32[3,16,64,128]{3,2,1,0:T(8,128)}, f32[3,16,64,128]{3,2,1,0:T(8,128)S(1)}, u32[]{:S(2)}) copy-start(f32[3,16,64,128]{3,2,1,0:T(8,128)S(1)} %broadcast_multiply_fusion) | copy-start | bytes 4718596
  14.6 1.2 %copy-start.6 = (s32[64,1]{0,1:T(1,128)S(1)}, s32[64,1]{0,1:T(1,128)}, u32[]{:S(2)}) copy-start(s32[64,1]{0,1:T(1,128)} %param.16) | copy-start | bytes 772
  16.6 6.6 %collective-permute-start.3 = (f32[264,128]{1,0:T(8,128)S(1)}, f32[264,128]{1,0:T(8,128)S(1)}, u32[]{:S(2)}, u32[]{:S(2)}) collective-permute-start(f32[264,128]{1,0:T(8,128)S(1)} %shard_map.106.sent.old_sent), channel_id=1, source_target_pairs={{0,15},{1,2},{2,1},{3,4},{4,3},{5,6},{6,5},{7,8},{8,7},{9,10},{10,... | collective-permute-start | bytes 405512 | tf_op jit(solution)/shard_map/ppermute | solution.py:846
  17.0 6.3 %collective-permute-start.4 = (f32[264,128]{1,0:T(8,128)S(1)}, f32[264,128]{1,0:T(8,128)S(1)}, u32[]{:S(2)}, u32[]{:S(2)}) collective-permute-start(f32[264,128]{1,0:T(8,128)S(1)} %shard_map.106.sent.old_sent), channel_id=1, source_target_pairs={{0,1},{1,0},{2,3},{3,2},{4,5},{5,4},{6,7},{7,6},{8,9},{9,8},{10,11... | collective-permute-start | bytes 405512 | tf_op jit(solution)/shard_map/ppermute | solution.py:846
  18.3 4.9 %copy-start = (bf16[64,1,128,128]{3,2,1,0:T(8,128)(2,1)S(1)}, bf16[64,1,128,128]{3,2,1,0:T(8,128)(2,1)}, u32[]{:S(2)}) copy-start(bf16[64,1,128,128]{3,2,1,0:T(8,128)(2,1)} %param.14) | copy-start | bytes 6291460
  18.4 4.9 %copy-start.3 = (f32[3,64,128]{2,1,0:T(8,128)S(1)}, f32[3,64,128]{2,1,0:T(8,128)}, u32[]{:S(2)}) copy-start(f32[3,64,128]{2,1,0:T(8,128)} %param.12) | copy-start | bytes 294916
  18.4 4.9 %copy-start.4 = (f32[64,128]{1,0:T(8,128)S(1)}, f32[64,128]{1,0:T(8,128)}, u32[]{:S(2)}) copy-start(f32[64,128]{1,0:T(8,128)} %gap.3) | copy-start | bytes 98308
  25.5 3.5 %copy-start.2 = (f32[3,16,64,128]{3,2,1,0:T(8,128)S(1)}, f32[3,16,64,128]{3,2,1,0:T(8,128)}, u32[]{:S(2)}) copy-start(f32[3,16,64,128]{3,2,1,0:T(8,128)} %copy-done.1) | copy-start | bytes 4718596
  25.5 8.4 %collective-permute-start.6 = (f32[200,128]{1,0:T(8,128)S(1)}, f32[200,128]{1,0:T(8,128)S(1)}, u32[]{:S(2)}, u32[]{:S(2)}) collective-permute-start(f32[200,128]{1,0:T(8,128)S(1)} %shard_map.109.own), channel_id=1, source_target_pairs={{0,15},{1,2},{2,1},{3,4},{4,3},{5,6},{6,5},{7,8},{8,7},{9,10},{10,... | collective-permute-start | bytes 307208 | tf_op jit(solution)/shard_map/ppermute | solution.py:846
  26.6 7.3 %collective-permute-start.7 = (f32[200,128]{1,0:T(8,128)S(1)}, f32[200,128]{1,0:T(8,128)S(1)}, u32[]{:S(2)}, u32[]{:S(2)}) collective-permute-start(f32[200,128]{1,0:T(8,128)S(1)} %shard_map.109.own), channel_id=1, source_target_pairs={{0,1},{1,0},{2,3},{3,2},{4,5},{5,4},{6,7},{7,6},{8,9},{9,8},{10,11... | collective-permute-start | bytes 307208 | tf_op jit(solution)/shard_map/ppermute | solution.py:846
  26.6 7.2 %collective-permute-start.5 = (f32[192,128]{1,0:T(8,128)S(1)}, f32[192,128]{1,0:T(8,128)S(1)}, u32[]{:S(2)}, u32[]{:S(2)}) collective-permute-start(f32[192,128]{1,0:T(8,128)S(1)} %get-tuple-element.51.surface.partial.refs_3_), channel_id=1, source_target_pairs={{0,8},{1,9},{2,10},{3,11},{4,12},{5,13},{6,14},{7,15},{8,0},{9,1},... | collective-permute-start | bytes 294920 | tf_op jit(solution)/shard_map/ppermute | solution.py:840
  34.1 8.1 %collective-permute-start.10 = (f32[192,128]{1,0:T(8,128)S(1)}, f32[192,128]{1,0:T(8,128)S(1)}, u32[]{:S(2)}, u32[]{:S(2)}) collective-permute-start(f32[192,128]{1,0:T(8,128)S(1)} %get-tuple-element.61.center), channel_id=1, source_target_pairs={{0,1},{1,0},{2,3},{3,2},{4,5},{5,4},{6,7},{7,6},{8,9},{9,8},{10,11... | collective-permute-start | bytes 294920 | tf_op jit(solution)/shard_map/ppermute | solution.py:846
  34.2 8.0 %collective-permute-start.8 = (f32[192,128]{1,0:T(8,128)S(1)}, f32[192,128]{1,0:T(8,128)S(1)}, u32[]{:S(2)}, u32[]{:S(2)}) collective-permute-start(f32[192,128]{1,0:T(8,128)S(1)} %get-tuple-element.60), channel_id=1, source_target_pairs={{0,8},{1,9},{2,10},{3,11},{4,12},{5,13},{6,14},{7,15},{8,0},{9,1},... | collective-permute-start | bytes 294920 | tf_op jit(solution)/shard_map/ppermute | solution.py:840
  35.2 7.0 %collective-permute-start.9 = (f32[192,128]{1,0:T(8,128)S(1)}, f32[192,128]{1,0:T(8,128)S(1)}, u32[]{:S(2)}, u32[]{:S(2)}) collective-permute-start(f32[192,128]{1,0:T(8,128)S(1)} %get-tuple-element.61.center), channel_id=1, source_target_pairs={{0,15},{1,2},{2,1},{3,4},{4,3},{5,6},{6,5},{7,8},{8,7},{9,10},{10,... | collective-permute-start | bytes 294920 | tf_op jit(solution)/shard_map/ppermute | solution.py:846
  36.5 7.7 %collective-permute-start.11 = (f32[64,128]{1,0:T(8,128)S(1)}, f32[64,128]{1,0:T(8,128)S(1)}, u32[]{:S(2)}, u32[]{:S(2)}) collective-permute-start(f32[64,128]{1,0:T(8,128)S(1)} %get-tuple-element.67), channel_id=1, source_target_pairs={{0,16},{16,32},{32,48},{48,64},{64,80},{80,96},{96,112},{112,0},{1... | collective-permute-start | bytes 98312 | tf_op jit(solution)/shard_map/ppermute | solution.py:840
  38.1 6.1 %collective-permute-start.12 = (f32[64,128]{1,0:T(8,128)S(1)}, f32[64,128]{1,0:T(8,128)S(1)}, u32[]{:S(2)}, u32[]{:S(2)}) collective-permute-start(f32[64,128]{1,0:T(8,128)S(1)} %get-tuple-element.68), channel_id=1, source_target_pairs={{0,112},{16,0},{32,16},{48,32},{64,48},{80,64},{96,80},{112,96},{1... | collective-permute-start | bytes 98312 | tf_op jit(solution)/shard_map/ppermute | solution.py:840
  44.4 7.5 %collective-permute-start.13 = (f32[272,128]{1,0:T(8,128)S(1)}, f32[272,128]{1,0:T(8,128)S(1)}, u32[]{:S(2)}, u32[]{:S(2)}) collective-permute-start(f32[272,128]{1,0:T(8,128)S(1)} %shard_map.115.own.sent), channel_id=1, source_target_pairs={{0,15},{1,2},{2,1},{3,4},{4,3},{5,6},{6,5},{7,8},{8,7},{9,10},{10,... | collective-permute-start | bytes 417800 | tf_op jit(solution)/shard_map/ppermute | solution.py:846
  46.5 5.4 %collective-permute-start.14 = (f32[272,128]{1,0:T(8,128)S(1)}, f32[272,128]{1,0:T(8,128)S(1)}, u32[]{:S(2)}, u32[]{:S(2)}) collective-permute-start(f32[272,128]{1,0:T(8,128)S(1)} %shard_map.115.own.sent), channel_id=1, source_target_pairs={{0,1},{1,0},{2,3},{3,2},{4,5},{5,4},{6,7},{7,6},{8,9},{9,8},{10,11... | collective-permute-start | bytes 417800 | tf_op jit(solution)/shard_map/ppermute | solution.py:846
  52.1 6.2 %collective-permute-start.15 = (f32[200,128]{1,0:T(8,128)S(1)}, f32[200,128]{1,0:T(8,128)S(1)}, u32[]{:S(2)}, u32[]{:S(2)}) collective-permute-start(f32[200,128]{1,0:T(8,128)S(1)} %shard_map.117), channel_id=1, source_target_pairs={{0,8},{1,9},{2,10},{3,11},{4,12},{5,13},{6,14},{7,15},{8,0},{9,1},... | collective-permute-start | bytes 307208 | tf_op jit(solution)/shard_map/ppermute | solution.py:840

commit v3 on v2

--- a/solution.py
+++ b/solution.py
@@ -74,6 +74,11 @@
     return [[linear * g[c][d] + bulk * cof[c][d] for d in range(3)] for c in range(3)]
 
 
+def dead_lane():
+    tile = lax.axis_index("gy")
+    return lax.axis_size("gy") * BLOCK // 2 + BLOCK // 2 - 1 - tile * BLOCK
+
+
 def forces_kernel(layers, later, *refs):
     start, end = layers
     count = end - start
@@ -92,7 +97,7 @@
     z[:, 0:8, :] = jnp.zeros((3 * count, 8, BLOCK), F32)
     lanes = iota((ROWS_DEV, BLOCK), 1)
     rows = iota((ROWS_DEV, BLOCK), 0)
-    keep = (lanes < BLOCK - 1) & (rows < ROWS_DEV - 1)
+    keep = (lanes < BLOCK - 1) & (rows < ROWS_DEV - 1) & (lanes != dead_lane())
     mask[...] = keep.astype(F32)
 
     def chunk(i, _):
@@ -150,8 +155,8 @@
     lax.fori_loop(0, ROWS_DEV // 8, chunk, 0)
 
 
-FIRST_LOW = 11
-SECOND_LOW = 5
+FIRST_LOW = 10
+SECOND_LOW = 3
 
 
 def planes(count, rows=ROWS_DEV):
@@ -191,17 +196,17 @@
         first[plane : plane + 1, :] = u[plane, 0:1, :]
         last[plane : plane + 1, :] = u[plane, ROWS_DEV - 1 : ROWS_DEV, :]
     for k in range(DEPTH - 1):
-        last[PLANES + k : PLANES + k + 1, :] = shear[k, :, :]
-
-
-def pack(u, shear_row):
+        last[PLANES + k : PLANES + k + 1, :] = shear[k, ROWS_DEV - 1 : ROWS_DEV, :]
+
+
+def pack(u, shear):
     return call(
         pack_kernel,
         (out(SURF), out(64), out(64)),
         [VMEM, VMEM],
         (VMEM,) * 3,
         [],
-        (u, shear_row),
+        (u, shear),
         1000,
         400_000,
     )
@@ -217,7 +222,7 @@
     for plane in range(PLANES):
         held = put_column(held, u[plane, 0:ROWS_DEV, :], plane)
     for k in range(DEPTH - 1):
-        held = put_column(held, shear[k, :, :], PLANES + k)
+        held = put_column(held, shear[k, 0:ROWS_DEV, :], PLANES + k)
     strip[0:ROWS_DEV, :] = held
     strip[ROWS_DEV:STRIP, :] = jnp.zeros((STRIP - ROWS_DEV, BLOCK), F32)
 
@@ -291,9 +296,7 @@
     gx = lax.axis_index("gx")
     lanes = iota((DEPTH, BLOCK), 1)
     sub = iota((DEPTH, BLOCK), 0)
-    cols_all = lax.axis_size("gy") * BLOCK
-    column = lanes + lax.axis_index("gy") * BLOCK
-    keep = (lanes < BLOCK - 1) & (sub < DEPTH - 1) & (column != cols_all // 2 + BLOCK // 2 - 1)
+    keep = (lanes < BLOCK - 1) & (sub < DEPTH - 1) & (lanes != dead_lane())
     top_moduli = jnp.where(keep & (gx > 0), moduli_above, 0.0)
     bottom_moduli = jnp.where(keep & (gx < lax.axis_size("gx") - 1), own_moduli, 0.0)
     top = row_ring(above, first, top_moduli, True)
@@ -452,6 +455,7 @@
 
 
 RAW = SURF + 8
+PARTIAL = SURF + 16
 
 
 def first_contact_kernel(
@@ -472,6 +476,7 @@
         three(surface), [three(across), three(sent), three(within)], three(normals), gap[...], mortar,
         place[...], lhs, prod,
     )
+    u_out[SURF:PARTIAL, :] = jnp.zeros((PARTIAL - SURF, BLOCK), F32)
     sub = iota((ROWS_DEV, BLOCK), 0)
     for c in range(3):
         here = slice(c * ROWS_DEV, (c + 1) * ROWS_DEV)
@@ -508,7 +513,7 @@
 def first_contact(*args):
     return call(
         first_contact_kernel,
-        (out(ROWS_DEV * 8), out(SURF), out(SURF), out(ROWS_DEV), out(2 * PLANES)),
+        (out(ROWS_DEV * 8), out(PARTIAL), out(SURF), out(ROWS_DEV), out(2 * PLANES)),
         [VMEM] * 14,
         (VMEM,) * 5,
         [pltpu.VMEM((ROWS_DEV * 8, BLOCK), F32)],
@@ -687,12 +692,10 @@
     return jnp.where(odd, halo_of(across[at, :], within[at, :]), sent[at, :])
 
 
-FIRST_FINAL = 2
-
-
 def last_update_kernel(
-    u, v_low, v_high, sent, across, within, first, last, above, below, old_sent, old_across,
-    old_within, old_above, old_last, u_hbm, v_hbm, u_out, v_out, sems,
+    u, shear, old_v, comb_own, v_high, sent, across, within, first, last, above, below, old_sent,
+    old_across, old_within, old_above, old_last, u_hbm, v_hbm, v_low, u_out, v_out, z, mask,
+    comb_home, sems,
 ):
     own, halo = strips_around(sent, across, within, above[...], below[...])
     ring = column_ring(own, halo, old_moduli(old_sent, old_across, old_within))
@@ -702,14 +705,11 @@
     )
     sub = iota((ROWS_DEV, BLOCK), 0)
     copies = []
-    begin = FIRST_FINAL
-    for k in range(FIRST_FINAL, DEPTH):
+    begin = SECOND_LOW
+    for k in range(SECOND_LOW, DEPTH):
         for c in range(3):
             plane = c * DEPTH + k
-            if k < SECOND_LOW:
-                v = v_low[c * SECOND_LOW + k, :, :]
-            else:
-                v = v_high[c * (DEPTH - SECOND_LOW) + k - SECOND_LOW, :, :]
+            v = v_high[c * (DEPTH - SECOND_LOW) + k - SECOND_LOW, :, :]
             new = v + from_strip(ring, plane)
             new = new + jnp.where(
                 sub == 0, jnp.broadcast_to(top[c][k : k + 1], sub.shape), 0.0
@@ -719,7 +719,7 @@
             )
             v_out[plane, :, :] = new
             u_out[plane, :, :] = u[plane, 0:ROWS_DEV, :] + TIME_STEP * new
-        if k in (3, 7, 11, 15):
+        if k in (4, 7, 11, 15):
             for c in range(3):
                 group = pl.ds(c * DEPTH + begin, k + 1 - begin)
                 for source, target in ((u_out, u_hbm), (v_out, v_hbm)):
@@ -729,6 +729,7 @@
                     copy.start()
                     copies.append(copy)
             begin = k + 1
+    forces_kernel((0, SECOND_LOW), True, u, shear, old_v, comb_own, v_low, z, mask, comb_home)
     for copy in copies:
         copy.wait()
 
@@ -736,12 +737,15 @@
 def last_update(*args):
     return call(
         last_update_kernel,
-        (planes(PLANES), planes(PLANES)),
-        [VMEM] * 15,
-        (ANY,) * 2,
+        (planes(PLANES), planes(PLANES), planes(3 * SECOND_LOW)),
+        [VMEM] * 17,
+        (ANY, ANY, VMEM),
         [
             pltpu.VMEM((PLANES, ROWS_DEV, BLOCK), F32),
             pltpu.VMEM((PLANES, ROWS_DEV, BLOCK), F32),
+            pltpu.VMEM((3 * SECOND_LOW, STRIP, BLOCK), F32),
+            pltpu.VMEM((ROWS_DEV, BLOCK), F32),
+            pltpu.VMEM((3, STRIP, BLOCK), F32),
             pltpu.SemaphoreType.DMA((24,)),
         ],
         args,
@@ -782,7 +786,7 @@
         old_last[PLANES:64, :], old_above[PLANES:64, :],
     )
     sub = iota((ROWS_DEV, BLOCK), 0)
-    for k in range(FIRST_FINAL):
+    for k in range(SECOND_LOW):
         for c in range(3):
             plane = c * DEPTH + k
             new = v_low[c * SECOND_LOW + k, :, :] + from_strip(ring, plane)
@@ -797,12 +801,12 @@
                 here = slice(c * ROWS_DEV, (c + 1) * ROWS_DEV)
                 new = new + TIME_STEP * (slave[here, :] + comb[here, :])
                 old_u = old_u + TIME_STEP * TIME_STEP * comb_own[here, :]
-            v_out[c * FIRST_FINAL + k, :, :] = new
-            u_out[c * FIRST_FINAL + k, :, :] = old_u + TIME_STEP * new
+            v_out[c * SECOND_LOW + k, :, :] = new
+            u_out[c * SECOND_LOW + k, :, :] = old_u + TIME_STEP * new
     copies = []
     for c in range(3):
-        source_at = pl.ds(c * FIRST_FINAL, FIRST_FINAL)
-        target_at = pl.ds(c * DEPTH, FIRST_FINAL)
+        source_at = pl.ds(c * SECOND_LOW, SECOND_LOW)
+        target_at = pl.ds(c * DEPTH, SECOND_LOW)
         for source, target in ((u_out, u_hbm), (v_out, v_hbm)):
             copies.append(
                 pltpu.make_async_copy(
@@ -821,8 +825,8 @@
         in_specs=[VMEM] * 17 + [ANY] * 2,
         out_specs=(ANY,) * 2,
         scratch_shapes=[
-            pltpu.VMEM((3 * FIRST_FINAL, ROWS_DEV, BLOCK), F32),
-            pltpu.VMEM((3 * FIRST_FINAL, ROWS_DEV, BLOCK), F32),
+            pltpu.VMEM((3 * SECOND_LOW, ROWS_DEV, BLOCK), F32),
+            pltpu.VMEM((3 * SECOND_LOW, ROWS_DEV, BLOCK), F32),
             pltpu.VMEM((64, BLOCK), F32),
             pltpu.VMEM((64, BLOCK), F32),
             pltpu.VMEM((PLANES, BLOCK), F32),
@@ -850,24 +854,12 @@
     half = lax.axis_size("gy") // 2
     flat_normals = normals.reshape(SURF, BLOCK)
     flat_mortar = mortar.reshape(ROWS_DEV * BLOCK, BLOCK)
-    alive = jnp.arange(ROWS_DEV, dtype=jnp.int32)[:, None] < live_rows
-    place = owner * ROWS_DEV + blocks + jnp.where(alive, LIVE, 0)
-    pairing = (flat_normals, gap_zero, flat_mortar, place)
-
     shape = displacement.shape
-    rows = lax.axis_index("gx") * ROWS_DEV + jnp.arange(ROWS_DEV, dtype=jnp.int32)
-    cols = lax.axis_index("gy") * BLOCK + jnp.arange(BLOCK, dtype=jnp.int32)
-    rows_all = lax.axis_size("gx") * ROWS_DEV
-    cols_all = lax.axis_size("gy") * BLOCK
-    valid = (rows < rows_all - 1)[:, None] & (
-        (cols < cols_all - 1) & (cols != cols_all // 2 + BLOCK // 2 - 1)
-    )[None, :]
     displacement = jnp.pad(
         displacement.reshape(PLANES, ROWS_DEV, BLOCK), ((0, 0), (0, STRIP - ROWS_DEV), (0, 0))
     )
-    surface, first, last = pack(displacement, shear[:, ROWS_DEV - 1 :, :])
-    surface, shear = lax.optimization_barrier((surface, shear))
-    shear = jnp.where(valid, shear, 0.0)
+    shear = jnp.pad(shear, ((0, 0), (0, STRIP - ROWS_DEV), (0, 0)))
+    surface, first, last = pack(displacement, shear)
     opposite = moved(surface, "gy", half)
     above = moved(last, "gx", 1)
     below = moved(first, "gx", -1)
@@ -879,7 +871,12 @@
     sent = message(opposite, above, below, strip)
     across = exchanged(sent, 1)
     within = exchanged(sent, 0)
-    sent, displacement = lax.optimization_barrier((sent, displacement))
+    sent, displacement, owner, blocks, live_rows = lax.optimization_barrier(
+        (sent, displacement, owner, blocks, live_rows)
+    )
+    alive = jnp.arange(ROWS_DEV, dtype=jnp.int32)[:, None] < live_rows
+    place = owner * ROWS_DEV + blocks + jnp.where(alive, LIVE, 0)
+    pairing = (flat_normals, gap_zero, flat_mortar, place)
     low = inner_forces((0, FIRST_LOW), displacement, shear)
 
     lhs, part_u, part_v, ring, rows = first_contact(
@@ -914,11 +911,10 @@
     comb = last_collect(sent2, across3, within3, above2, below2)
     comb_last = moved(comb, "gy", half)
     comb, u = lax.optimization_barrier((comb, u))
-    low = inner_forces((0, SECOND_LOW), u, shear, v, comb_own)
     around = (
         sent2, across3, within3, first2, last2, above2, below2, sent, across, within, above, last
     )
-    final = last_update(u, low, high, *around)
+    *final, low = last_update(u, shear, v, comb_own, high, *around)
     u, v = last_surface(u, low, slave, comb_own, comb_last, *around, *final)
     return u.reshape(shape), v.reshape(shape)
 

time: 60.1 us -> 59.5 us (0.990)
  starting transfers between devices: 24.3 us -> 27.2 us
  other arithmetic: 1.85 us -> 0.26 us
  waiting for transfers between devices: 8.4 us -> 6.94 us
  Pallas kernels: 20.8 us -> 20 us
    ppermute x8, waiting for transfers between devices: 4.36 us -> 2.23 us  [moved(): return lax.ppermute(x, axis, [(i, (i + by) % count) for i in range(count)])]
    ppermute x8, starting transfers between devices: 18 us -> 20.1 us  [moved(): return lax.ppermute(x, axis, [(i, (i + by) % count) for i in range(count)])]
    mul x1, other arithmetic: 1.71 us -> 0.24 us  [local(): damped = DAMPING * velocity.reshape(PLANES, ROWS_DEV, BLOCK)]
    pad x0 -> x1, local copies, waits for them, and re-layouts: none -> 1.07 us  [local(): shear = jnp.pad(shear, ((0, 0), (0, STRIP - ROWS_DEV), (0, 0)))]
    pallas_call x16 -> x15, Pallas kernels: 19.3 us -> 18.2 us  [call(): pl.pallas_call(kernel, out_shape=out_shape, in_specs=in_specs, out_specs=...]
    slice x1 -> x0, local copies, waits for them, and re-layouts: 0.84 us -> none  [local(): surface, first, last = pack(displacement, shear[:, ROWS_DEV - 1:, :])]
    ppermute x8, starting transfers between devices: 6.29 us -> 7.08 us  [exchanged(): return lax.ppermute(x, 'gy', [(i, j % count) for i, j in pairs])]
    ppermute x8, waiting for transfers between devices: 4.04 us -> 4.71 us  [exchanged(): return lax.ppermute(x, 'gy', [(i, j % count) for i, j in pairs])]
  transfers between devices with their start and end apart: 16 -> 16, of which waited for: 4 -> 5; matrix products, arithmetic and copies ran while one was open for 3% -> 1% of each run, Pallas kernels for 27% -> 27%
where the time goes in v3:
time: 59.5 us; the launch traced here: 59.1 us
  starting transfers between devices  27.2 us (46%)
  Pallas kernels  20 us (34%)
  waiting for transfers between devices  6.94 us (12%)
  local copies, waits for them, and re-layouts  3.26 us (5%)
  between operations  1.52 us (3%)
    ppermute x8, starting transfers between devices, moved(): return lax.ppermute(x, axis, [(i, (i + by) % count) for i in range(count)])  20.1 us
    pallas_call x15, Pallas kernels, call(): pl.pallas_call(kernel, out_shape=out_shape, in_specs=in_specs, out_specs=...  18.2 us
    ppermute x8, starting transfers between devices, exchanged(): return lax.ppermute(x, 'gy', [(i, j % count) for i, j in pairs])  7.08 us
    ppermute x8, waiting for transfers between devices, exchanged(): return lax.ppermute(x, 'gy', [(i, j % count) for i, j in pairs])  4.71 us
    ppermute x8, waiting for transfers between devices, moved(): return lax.ppermute(x, axis, [(i, (i + by) % count) for i in range(count)])  2.23 us
    pallas_call x1, Pallas kernels, last_surface(): pl.pallas_call(last_surface_kernel, out_shape=(planes(PLANES), planes(PLA...  1.75 us
    pad x1, local copies, waits for them, and re-layouts, local(): jnp.pad(displacement.reshape(PLANES, ROWS_DEV, BLOCK), ((0, 0), (0, STRIP...  1.54 us
  transfers between devices with their start and end apart: 16, of which 5 were waited for; matrix products, arithmetic and copies ran while one was open for 1% of the time, Pallas kernels for 27%

profile of v3, /device:TPU:0, one launch (start us, length us, event | category | flops | bytes accessed | tf_op | source)
XLA Modules:
  0.0 59.1 jit_solution(3285955180272214742)
XLA Ops:
  0.6 1.1 %pad.9.shear.refs_1_ = f32[15,72,128]{2,1,0:T(8,128)S(1)} pad(f32[15,64,128]{2,1,0:T(8,128)} %param.11, f32[]{:T(128)} %constant.1.clone.1), padding=0_0x0_8x0_0 | pad | bytes 1044484 | tf_op jit(solution)/shard_map/jit(_pad)/pad | solution.py:861
  1.7 1.5 %pad.8.u.refs_0_ = f32[48,72,128]{2,1,0:T(8,128)S(1)} pad(f32[48,64,128]{2,1,0:T(8,128)} %bitcast.16, f32[]{:T(128)} %constant.1.clone.1), padding=0_0x0_8x0_0 | pad | bytes 3342340 | tf_op jit(solution)/shard_map/jit(_pad)/pad | solution.py:858
  3.3 3.2 %collective-permute-start.1 = (f32[64,128]{1,0:T(8,128)S(1)}, f32[64,128]{1,0:T(8,128)S(1)}, u32[]{:S(2)}, u32[]{:S(2)}) collective-permute-start(f32[64,128]{1,0:T(8,128)S(1)} %get-tuple-element.45.last.old_last), channel_id=1, source_target_pairs={{0,16},{16,32},{32,48},{48,64},{64,80},{80,96},{96,112},{112,0},{1... | collective-permute-start | bytes 98312 | tf_op jit(solution)/shard_map/ppermute | solution.py:844
  6.5 2.5 %collective-permute-start.2 = (f32[64,128]{1,0:T(8,128)S(1)}, f32[64,128]{1,0:T(8,128)S(1)}, u32[]{:S(2)}, u32[]{:S(2)}) collective-permute-start(f32[64,128]{1,0:T(8,128)S(1)} %get-tuple-element.46.first), channel_id=1, source_target_pairs={{0,112},{16,0},{32,16},{48,32},{64,48},{80,64},{96,80},{112,96},{1... | collective-permute-start | bytes 98312 | tf_op jit(solution)/shard_map/ppermute | solution.py:844
  9.0 4.0 %collective-permute-start = (f32[192,128]{1,0:T(8,128)S(1)}, f32[192,128]{1,0:T(8,128)S(1)}, u32[]{:S(2)}, u32[]{:S(2)}) collective-permute-start(f32[192,128]{1,0:T(8,128)S(1)} %get-tuple-element.44.surface), channel_id=1, source_target_pairs={{0,8},{1,9},{2,10},{3,11},{4,12},{5,13},{6,14},{7,15},{8,0},{9,1},... | collective-permute-start | bytes 294920 | tf_op jit(solution)/shard_map/ppermute | solution.py:844
  13.0 0.2 broadcast_multiply_fusion
  13.3 0.6 %shard_map.105.strip = f32[72,128]{1,0:T(8,128)S(1)} custom-call(f32[48,72,128]{2,1,0:T(8,128)S(1)} %pad.8.u.refs_0_, f32[15,72,128]{2,1,0:T(8,128)S(1)} %pad.9.shear.refs_1_), custom_call_target="tpu_custom_call" | custom-call | flops 1000 | bytes 1000 | tf_op jit(solution)/shard_map/pallas_call | solution.py:37
  13.9 0.5 copy-done.1
  15.1 0.5 collective-permute-done.surface
  15.7 2.4 %collective-permute-start.3 = (f32[264,128]{1,0:T(8,128)S(1)}, f32[264,128]{1,0:T(8,128)S(1)}, u32[]{:S(2)}, u32[]{:S(2)}) collective-permute-start(f32[264,128]{1,0:T(8,128)S(1)} %shard_map.106.sent.old_sent), channel_id=1, source_target_pairs={{0,15},{1,2},{2,1},{3,4},{4,3},{5,6},{6,5},{7,8},{8,7},{9,10},{10,... | collective-permute-start | bytes 405512 | tf_op jit(solution)/shard_map/ppermute | solution.py:850
  18.3 2.8 %shard_map.107.low = f32[30,64,128]{2,1,0:T(8,128)S(1)} custom-call(f32[48,72,128]{2,1,0:T(8,128)S(1)} %pad.8.u.refs_0_, f32[15,72,128]{2,1,0:T(8,128)S(1)} %pad.9.shear.refs_1_), custom_call_target="tpu_custom_call" | custom-call | flops 1000 | bytes 1000 | tf_op jit(solution)/shard_map/pallas_call | solution.py:37
  21.1 1.6 %collective-permute-done.3.across.old_across = f32[264,128]{1,0:T(8,128)S(1)} collective-permute-done((f32[264,128]{1,0:T(8,128)S(1)}, f32[264,128]{1,0:T(8,128)S(1)}, u32[]{:S(2)}, u32[]{:S(2)}) %collective-permute-start.3) | collective-permute-done | bytes 135200 | tf_op jit(solution)/shard_map/ppermute | solution.py:850
  22.7 1.5 %shard_map.108 = (f32[512,128]{1,0:T(8,128)S(1)}, f32[208,128]{1,0:T(8,128)S(1)}, f32[192,128]{1,0:T(8,128)S(1)}, f32[64,128]{1,0:T(8,128)S(1)}, f32[96,128]{1,0:T(8,128)S(1)}) custom-call(f32[192,128]{1,0:T(8,128)S(1)} %get-tuple-element.44.surface, f32[264,128]{1,0:T(8,128)S(1)} %shard_map.106.sent.old_sent, ...), custom_call_target="tpu_custom_call" | custom-call | flops 1000 | bytes 1000 | tf_op jit(solution)/shard_map/pallas_call | solution.py:37
  24.2 2.2 %collective-permute-start.5 = (f32[208,128]{1,0:T(8,128)S(1)}, f32[208,128]{1,0:T(8,128)S(1)}, u32[]{:S(2)}, u32[]{:S(2)}) collective-permute-start(f32[208,128]{1,0:T(8,128)S(1)} %get-tuple-element.54.surface.partial.refs_3_), channel_id=1, source_target_pairs={{0,8},{1,9},{2,10},{3,11},{4,12},{5,13},{6,14},{7,15},{8,0},{9,1},... | collective-permute-start | bytes 319496 | tf_op jit(solution)/shard_map/ppermute | solution.py:844
  26.4 0.7 %shard_map.109.own = f32[200,128]{1,0:T(8,128)S(1)} custom-call(f32[512,128]{1,0:T(8,128)S(1)} %get-tuple-element.55.lhs, bf16[8192,128]{1,0:T(8,128)(2,1)S(1)} %bitcast.10, s32[64,1]{1,0:T(8,128)S(1)} %select_add_fusion.place), custom_call_target="tpu_custom_call" | custom-call | flops 1000 | bytes 1000 | tf_op jit(solution)/shard_map/pallas_call | solution.py:37
  27.1 0.8 %collective-permute-start.6 = (f32[200,128]{1,0:T(8,128)S(1)}, f32[200,128]{1,0:T(8,128)S(1)}, u32[]{:S(2)}, u32[]{:S(2)}) collective-permute-start(f32[200,128]{1,0:T(8,128)S(1)} %shard_map.109.own), channel_id=1, source_target_pairs={{0,15},{1,2},{2,1},{3,4},{4,3},{5,6},{6,5},{7,8},{8,7},{9,10},{10,... | collective-permute-start | bytes 307208 | tf_op jit(solution)/shard_map/ppermute | solution.py:850
  27.9 0.4 collective-permute-start.7
  28.3 2.1 %shard_map.110.high = f32[18,64,128]{2,1,0:T(8,128)S(1)} custom-call(f32[48,72,128]{2,1,0:T(8,128)S(1)} %pad.8.u.refs_0_, f32[15,72,128]{2,1,0:T(8,128)S(1)} %pad.9.shear.refs_1_), custom_call_target="tpu_custom_call" | custom-call | flops 1000 | bytes 1000 | tf_op jit(solution)/shard_map/pallas_call | solution.py:37
  30.4 0.9 %shard_map.111 = (f32[48,72,128]{2,1,0:T(8,128)S(1)}, f32[48,64,128]{2,1,0:T(8,128)S(1)}, f32[72,128]{1,0:T(8,128)S(1)}, f32[64,128]{1,0:T(8,128)S(1)}, f32[64,128]{1,0:T(8,128)S(1)}) custom-call(f32[48,72,128]{2,1,0:T(8,128)S(1)} %pad.8.u.refs_0_, f32[48,64,128]{2,1,0:T(8,128)S(1)} %bitcast.12, f32[30,64,128]{2,1,0:T(8,128)S(1)} %shard_map.107.low, ...), custom_call_target="tpu_custom_call" | custom-call | flops 1000 | bytes 1000 | tf_op jit(solution)/shard_map/pallas_call | solution.py:37
  31.3 2.0 %collective-permute-done.6.left = f32[200,128]{1,0:T(8,128)S(1)} collective-permute-done((f32[200,128]{1,0:T(8,128)S(1)}, f32[200,128]{1,0:T(8,128)S(1)}, u32[]{:S(2)}, u32[]{:S(2)}) %collective-permute-start.6) | collective-permute-done | bytes 102432 | tf_op jit(solution)/shard_map/ppermute | solution.py:850
  33.7 1.1 %collective-permute-start.8 = (f32[192,128]{1,0:T(8,128)S(1)}, f32[192,128]{1,0:T(8,128)S(1)}, u32[]{:S(2)}, u32[]{:S(2)}) collective-permute-start(f32[192,128]{1,0:T(8,128)S(1)} %get-tuple-element.63), channel_id=1, source_target_pairs={{0,8},{1,9},{2,10},{3,11},{4,12},{5,13},{6,14},{7,15},{8,0},{9,1},... | collective-permute-start | bytes 294920 | tf_op jit(solution)/shard_map/ppermute | solution.py:844
  34.8 1.5 %collective-permute-start.9 = (f32[192,128]{1,0:T(8,128)S(1)}, f32[192,128]{1,0:T(8,128)S(1)}, u32[]{:S(2)}, u32[]{:S(2)}) collective-permute-start(f32[192,128]{1,0:T(8,128)S(1)} %get-tuple-element.64.center), channel_id=1, source_target_pairs={{0,15},{1,2},{2,1},{3,4},{4,3},{5,6},{6,5},{7,8},{8,7},{9,10},{10,... | collective-permute-start | bytes 294920 | tf_op jit(solution)/shard_map/ppermute | solution.py:850
  36.3 0.7 %collective-permute-start.11 = (f32[64,128]{1,0:T(8,128)S(1)}, f32[64,128]{1,0:T(8,128)S(1)}, u32[]{:S(2)}, u32[]{:S(2)}) collective-permute-start(f32[64,128]{1,0:T(8,128)S(1)} %get-tuple-element.70), channel_id=1, source_target_pairs={{0,16},{16,32},{32,48},{48,64},{64,80},{80,96},{96,112},{112,0},{1... | collective-permute-start | bytes 98312 | tf_op jit(solution)/shard_map/ppermute | solution.py:844
  37.0 5.0 %collective-permute-start.12 = (f32[64,128]{1,0:T(8,128)S(1)}, f32[64,128]{1,0:T(8,128)S(1)}, u32[]{:S(2)}, u32[]{:S(2)}) collective-permute-start(f32[64,128]{1,0:T(8,128)S(1)} %get-tuple-element.71), channel_id=1, source_target_pairs={{0,112},{16,0},{32,16},{48,32},{64,48},{80,64},{96,80},{112,96},{1... | collective-permute-start | bytes 98312 | tf_op jit(solution)/shard_map/ppermute | solution.py:844
  42.0 2.0 %shard_map.113 = (f32[200,128]{1,0:T(8,128)S(1)}, f32[64,128]{1,0:T(8,128)S(1)}, f32[192,128]{1,0:T(8,128)S(1)}) custom-call(f32[208,128]{1,0:T(8,128)S(1)} %get-tuple-element.54.surface.partial.refs_3_, f32[192,128]{1,0:T(8,128)S(1)} %collective-permute-done.8.comb.comb_own, f32[192,128]{1,0:T(8,128)S(1)} %get-tuple-element.64.center, ...), custom_call_target="tpu_custom_call" | custom-call | flops 1000 | bytes 1000 | tf_op jit(solution)/shard_map/pallas_call | solution.py:37
  44.2 1.9 %collective-permute-start.13 = (f32[272,128]{1,0:T(8,128)S(1)}, f32[272,128]{1,0:T(8,128)S(1)}, u32[]{:S(2)}, u32[]{:S(2)}) collective-permute-start(f32[272,128]{1,0:T(8,128)S(1)} %shard_map.115.own.sent), channel_id=1, source_target_pairs={{0,15},{1,2},{2,1},{3,4},{4,3},{5,6},{6,5},{7,8},{8,7},{9,10},{10,... | collective-permute-start | bytes 417800 | tf_op jit(solution)/shard_map/ppermute | solution.py:850
  46.1 3.7 %shard_map.116.v_high = f32[39,64,128]{2,1,0:T(8,128)S(1)} custom-call(f32[48,72,128]{2,1,0:T(8,128)S(1)} %get-tuple-element.78.refs_0_.u, f32[15,72,128]{2,1,0:T(8,128)S(1)} %pad.9.shear.refs_1_, f32[48,64,128]{2,1,0:T(8,128)S(1)} %get-tuple-element.75.refs_2_.old_v, f32[208,128]{1,0:T(8,128)S(1)} %get-tuple-element.54.surface.partial.refs_3_), custom_call_target="tpu_custom_call" | custom-call | flops 1000 | bytes 1000 | tf_op jit(solution)/shard_map/pallas_call | solution.py:37
  49.8 1.0 %collective-permute-done.13.across = f32[272,128]{1,0:T(8,128)S(1)} collective-permute-done((f32[272,128]{1,0:T(8,128)S(1)}, f32[272,128]{1,0:T(8,128)S(1)}, u32[]{:S(2)}, u32[]{:S(2)}) %collective-permute-start.13) | collective-permute-done | bytes 139296 | tf_op jit(solution)/shard_map/ppermute | solution.py:850
  51.1 1.4 %collective-permute-start.15 = (f32[200,128]{1,0:T(8,128)S(1)}, f32[200,128]{1,0:T(8,128)S(1)}, u32[]{:S(2)}, u32[]{:S(2)}) collective-permute-start(f32[200,128]{1,0:T(8,128)S(1)} %shard_map.117), channel_id=1, source_target_pairs={{0,8},{1,9},{2,10},{3,11},{4,12},{5,13},{6,14},{7,15},{8,0},{9,1},... | collective-permute-start | bytes 307208 | tf_op jit(solution)/shard_map/ppermute | solution.py:844
  52.5 3.1 %shard_map.118 = (f32[48,64,128]{2,1,0:T(8,128)}, f32[48,64,128]{2,1,0:T(8,128)}, f32[9,64,128]{2,1,0:T(8,128)S(1)}) custom-call(f32[48,72,128]{2,1,0:T(8,128)S(1)} %get-tuple-element.78.refs_0_.u, f32[15,72,128]{2,1,0:T(8,128)S(1)} %pad.9.shear.refs_1_, f32[48,64,128]{2,1,0:T(8,128)S(1)} %get-tuple-element.75.refs_2_.old_v, ...), custom_call_target="tpu_custom_call" | custom-call | flops 1000 | bytes 1000 | tf_op jit(solution)/shard_map/pallas_call | solution.py:37
  55.6 1.7 %collective-permute-done.15.comb = f32[200,128]{1,0:T(8,128)S(1)} collective-permute-done((f32[200,128]{1,0:T(8,128)S(1)}, f32[200,128]{1,0:T(8,128)S(1)}, u32[]{:S(2)}, u32[]{:S(2)}) %collective-permute-start.15) | collective-permute-done | bytes 102432 | tf_op jit(solution)/shard_map/ppermute | solution.py:844
  57.4 1.7 %shard_map.119 = (f32[48,64,128]{2,1,0:T(8,128)}, f32[48,64,128]{2,1,0:T(8,128)}) custom-call(f32[48,72,128]{2,1,0:T(8,128)S(1)} %get-tuple-element.78.refs_0_.u, f32[9,64,128]{2,1,0:T(8,128)S(1)} %get-tuple-element.80.v_low, f32[192,128]{1,0:T(8,128)S(1)} %get-tuple-element.81.slave, ...), custom_call_target="tpu_custom_call", output_to_operand_aliasing={{0}: (17, {}), {1}: (18, {})} | custom-call | flops 1000 | bytes 1000 | tf_op jit(solution)/shard_map/pallas_call | solution.py:822
  (39 shorter events, 1.0 us)
Async XLA Ops:
  3.3 9.7 %copy-start.5 = (f32[3,16,64,128]{3,2,1,0:T(8,128)S(1)}, f32[3,16,64,128]{3,2,1,0:T(8,128)}, u32[]{:S(2)}) copy-start(f32[3,16,64,128]{3,2,1,0:T(8,128)} %param.10) | copy-start | bytes 4718596
  3.3 11.7 %collective-permute-start.1 = (f32[64,128]{1,0:T(8,128)S(1)}, f32[64,128]{1,0:T(8,128)S(1)}, u32[]{:S(2)}, u32[]{:S(2)}) collective-permute-start(f32[64,128]{1,0:T(8,128)S(1)} %get-tuple-element.45.last.old_last), channel_id=1, source_target_pairs={{0,16},{16,32},{32,48},{48,64},{64,80},{80,96},{96,112},{112,0},{1... | collective-permute-start | bytes 98312 | tf_op jit(solution)/shard_map/ppermute | solution.py:844
  6.5 8.6 %collective-permute-start.2 = (f32[64,128]{1,0:T(8,128)S(1)}, f32[64,128]{1,0:T(8,128)S(1)}, u32[]{:S(2)}, u32[]{:S(2)}) collective-permute-start(f32[64,128]{1,0:T(8,128)S(1)} %get-tuple-element.46.first), channel_id=1, source_target_pairs={{0,112},{16,0},{32,16},{48,32},{64,48},{80,64},{96,80},{112,96},{1... | collective-permute-start | bytes 98312 | tf_op jit(solution)/shard_map/ppermute | solution.py:844
  9.0 6.6 %collective-permute-start = (f32[192,128]{1,0:T(8,128)S(1)}, f32[192,128]{1,0:T(8,128)S(1)}, u32[]{:S(2)}, u32[]{:S(2)}) collective-permute-start(f32[192,128]{1,0:T(8,128)S(1)} %get-tuple-element.44.surface), channel_id=1, source_target_pairs={{0,8},{1,9},{2,10},{3,11},{4,12},{5,13},{6,14},{7,15},{8,0},{9,1},... | collective-permute-start | bytes 294920 | tf_op jit(solution)/shard_map/ppermute | solution.py:844
  13.2 1.1 %copy-start.1 = (f32[3,16,64,128]{3,2,1,0:T(8,128)}, f32[3,16,64,128]{3,2,1,0:T(8,128)S(1)}, u32[]{:S(2)}) copy-start(f32[3,16,64,128]{3,2,1,0:T(8,128)S(1)} %broadcast_multiply_fusion) | copy-start | bytes 4718596
  13.3 4.9 %copy-start.6 = (s32[64,1]{0,1:T(1,128)S(1)}, s32[64,1]{0,1:T(1,128)}, u32[]{:S(2)}) copy-start(s32[64,1]{0,1:T(1,128)} %param.16) | copy-start | bytes 772
  13.3 4.9 %copy-start.7 = (s32[64,1]{0,1:T(1,128)S(1)}, s32[64,1]{0,1:T(1,128)}, u32[]{:S(2)}) copy-start(s32[64,1]{0,1:T(1,128)} %param.15) | copy-start | bytes 772
  15.7 7.0 %collective-permute-start.3 = (f32[264,128]{1,0:T(8,128)S(1)}, f32[264,128]{1,0:T(8,128)S(1)}, u32[]{:S(2)}, u32[]{:S(2)}) collective-permute-start(f32[264,128]{1,0:T(8,128)S(1)} %shard_map.106.sent.old_sent), channel_id=1, source_target_pairs={{0,15},{1,2},{2,1},{3,4},{4,3},{5,6},{6,5},{7,8},{8,7},{9,10},{10,... | collective-permute-start | bytes 405512 | tf_op jit(solution)/shard_map/ppermute | solution.py:850
  18.1 4.6 %collective-permute-start.4 = (f32[264,128]{1,0:T(8,128)S(1)}, f32[264,128]{1,0:T(8,128)S(1)}, u32[]{:S(2)}, u32[]{:S(2)}) collective-permute-start(f32[264,128]{1,0:T(8,128)S(1)} %shard_map.106.sent.old_sent), channel_id=1, source_target_pairs={{0,1},{1,0},{2,3},{3,2},{4,5},{5,4},{6,7},{7,6},{8,9},{9,8},{10,11... | collective-permute-start | bytes 405512 | tf_op jit(solution)/shard_map/ppermute | solution.py:850
  18.2 4.5 %copy-start = (bf16[64,1,128,128]{3,2,1,0:T(8,128)(2,1)S(1)}, bf16[64,1,128,128]{3,2,1,0:T(8,128)(2,1)}, u32[]{:S(2)}) copy-start(bf16[64,1,128,128]{3,2,1,0:T(8,128)(2,1)} %param.14) | copy-start | bytes 6291460
  18.2 4.5 %copy-start.3 = (f32[3,64,128]{2,1,0:T(8,128)S(1)}, f32[3,64,128]{2,1,0:T(8,128)}, u32[]{:S(2)}) copy-start(f32[3,64,128]{2,1,0:T(8,128)} %param.12) | copy-start | bytes 294916
  18.3 4.5 %copy-start.4 = (f32[64,128]{1,0:T(8,128)S(1)}, f32[64,128]{1,0:T(8,128)}, u32[]{:S(2)}) copy-start(f32[64,128]{1,0:T(8,128)} %gap.3) | copy-start | bytes 98308
  24.2 9.1 %collective-permute-start.5 = (f32[208,128]{1,0:T(8,128)S(1)}, f32[208,128]{1,0:T(8,128)S(1)}, u32[]{:S(2)}, u32[]{:S(2)}) collective-permute-start(f32[208,128]{1,0:T(8,128)S(1)} %get-tuple-element.54.surface.partial.refs_3_), channel_id=1, source_target_pairs={{0,8},{1,9},{2,10},{3,11},{4,12},{5,13},{6,14},{7,15},{8,0},{9,1},... | collective-permute-start | bytes 319496 | tf_op jit(solution)/shard_map/ppermute | solution.py:844
  27.1 3.3 %copy-start.2 = (f32[3,16,64,128]{3,2,1,0:T(8,128)S(1)}, f32[3,16,64,128]{3,2,1,0:T(8,128)}, u32[]{:S(2)}) copy-start(f32[3,16,64,128]{3,2,1,0:T(8,128)} %copy-done.1) | copy-start | bytes 4718596
  27.1 6.3 %collective-permute-start.6 = (f32[200,128]{1,0:T(8,128)S(1)}, f32[200,128]{1,0:T(8,128)S(1)}, u32[]{:S(2)}, u32[]{:S(2)}) collective-permute-start(f32[200,128]{1,0:T(8,128)S(1)} %shard_map.109.own), channel_id=1, source_target_pairs={{0,15},{1,2},{2,1},{3,4},{4,3},{5,6},{6,5},{7,8},{8,7},{9,10},{10,... | collective-permute-start | bytes 307208 | tf_op jit(solution)/shard_map/ppermute | solution.py:850
  27.9 5.5 %collective-permute-start.7 = (f32[200,128]{1,0:T(8,128)S(1)}, f32[200,128]{1,0:T(8,128)S(1)}, u32[]{:S(2)}, u32[]{:S(2)}) collective-permute-start(f32[200,128]{1,0:T(8,128)S(1)} %shard_map.109.own), channel_id=1, source_target_pairs={{0,1},{1,0},{2,3},{3,2},{4,5},{5,4},{6,7},{7,6},{8,9},{9,8},{10,11... | collective-permute-start | bytes 307208 | tf_op jit(solution)/shard_map/ppermute | solution.py:850
  33.6 8.4 %collective-permute-start.10 = (f32[192,128]{1,0:T(8,128)S(1)}, f32[192,128]{1,0:T(8,128)S(1)}, u32[]{:S(2)}, u32[]{:S(2)}) collective-permute-start(f32[192,128]{1,0:T(8,128)S(1)} %get-tuple-element.64.center), channel_id=1, source_target_pairs={{0,1},{1,0},{2,3},{3,2},{4,5},{5,4},{6,7},{7,6},{8,9},{9,8},{10,11... | collective-permute-start | bytes 294920 | tf_op jit(solution)/shard_map/ppermute | solution.py:850
  33.7 8.3 %collective-permute-start.8 = (f32[192,128]{1,0:T(8,128)S(1)}, f32[192,128]{1,0:T(8,128)S(1)}, u32[]{:S(2)}, u32[]{:S(2)}) collective-permute-start(f32[192,128]{1,0:T(8,128)S(1)} %get-tuple-element.63), channel_id=1, source_target_pairs={{0,8},{1,9},{2,10},{3,11},{4,12},{5,13},{6,14},{7,15},{8,0},{9,1},... | collective-permute-start | bytes 294920 | tf_op jit(solution)/shard_map/ppermute | solution.py:844
  34.8 7.2 %collective-permute-start.9 = (f32[192,128]{1,0:T(8,128)S(1)}, f32[192,128]{1,0:T(8,128)S(1)}, u32[]{:S(2)}, u32[]{:S(2)}) collective-permute-start(f32[192,128]{1,0:T(8,128)S(1)} %get-tuple-element.64.center), channel_id=1, source_target_pairs={{0,15},{1,2},{2,1},{3,4},{4,3},{5,6},{6,5},{7,8},{8,7},{9,10},{10,... | collective-permute-start | bytes 294920 | tf_op jit(solution)/shard_map/ppermute | solution.py:850
  36.3 7.7 %collective-permute-start.11 = (f32[64,128]{1,0:T(8,128)S(1)}, f32[64,128]{1,0:T(8,128)S(1)}, u32[]{:S(2)}, u32[]{:S(2)}) collective-permute-start(f32[64,128]{1,0:T(8,128)S(1)} %get-tuple-element.70), channel_id=1, source_target_pairs={{0,16},{16,32},{32,48},{48,64},{64,80},{80,96},{96,112},{112,0},{1... | collective-permute-start | bytes 98312 | tf_op jit(solution)/shard_map/ppermute | solution.py:844
  37.0 7.0 %collective-permute-start.12 = (f32[64,128]{1,0:T(8,128)S(1)}, f32[64,128]{1,0:T(8,128)S(1)}, u32[]{:S(2)}, u32[]{:S(2)}) collective-permute-start(f32[64,128]{1,0:T(8,128)S(1)} %get-tuple-element.71), channel_id=1, source_target_pairs={{0,112},{16,0},{32,16},{48,32},{64,48},{80,64},{96,80},{112,96},{1... | collective-permute-start | bytes 98312 | tf_op jit(solution)/shard_map/ppermute | solution.py:844
  44.2 6.7 %collective-permute-start.13 = (f32[272,128]{1,0:T(8,128)S(1)}, f32[272,128]{1,0:T(8,128)S(1)}, u32[]{:S(2)}, u32[]{:S(2)}) collective-permute-start(f32[272,128]{1,0:T(8,128)S(1)} %shard_map.115.own.sent), channel_id=1, source_target_pairs={{0,15},{1,2},{2,1},{3,4},{4,3},{5,6},{6,5},{7,8},{8,7},{9,10},{10,... | collective-permute-start | bytes 417800 | tf_op jit(solution)/shard_map/ppermute | solution.py:850
  46.1 4.8 %collective-permute-start.14 = (f32[272,128]{1,0:T(8,128)S(1)}, f32[272,128]{1,0:T(8,128)S(1)}, u32[]{:S(2)}, u32[]{:S(2)}) collective-permute-start(f32[272,128]{1,0:T(8,128)S(1)} %shard_map.115.own.sent), channel_id=1, source_target_pairs={{0,1},{1,0},{2,3},{3,2},{4,5},{5,4},{6,7},{7,6},{8,9},{9,8},{10,11... | collective-permute-start | bytes 417800 | tf_op jit(solution)/shard_map/ppermute | solution.py:850
  51.1 6.2 %collective-permute-start.15 = (f32[200,128]{1,0:T(8,128)S(1)}, f32[200,128]{1,0:T(8,128)S(1)}, u32[]{:S(2)}, u32[]{:S(2)}) collective-permute-start(f32[200,128]{1,0:T(8,128)S(1)} %shard_map.117), channel_id=1, source_target_pairs={{0,8},{1,9},{2,10},{3,11},{4,12},{5,13},{6,14},{7,15},{8,0},{9,1},... | collective-permute-start | bytes 307208 | tf_op jit(solution)/shard_map/ppermute | solution.py:844

commit v4 on v3

--- a/solution.py
+++ b/solution.py
@@ -157,6 +157,7 @@
 
 FIRST_LOW = 10
 SECOND_LOW = 3
+FIRST_FINAL = 2
 
 
 def planes(count, rows=ROWS_DEV):
@@ -249,19 +250,26 @@
     return jnp.sum(jnp.where(lanes // 2 == sub, both, 0.0), axis=0, keepdims=True)
 
 
-def message_kernel(surface, above, below, strip, message):
+def message_kernel(surface, above, below, strip, message, longer):
     message[0:SURF, :] = surface[...]
     message[SURF : SURF + STRIP, :] = strip[...]
     message[SURF + ROWS_DEV : SURF + ROWS_DEV + 1, :] = ends_of_row(below[...])
     message[SURF + STRIP - 1 : SURF + STRIP, :] = ends_of_row(above[...])
+    lengthen(message, longer)
+
+
+def lengthen(message, longer):
+    rows = message.shape[0]
+    longer[0:rows, :] = message[...]
+    longer[rows : rows + MORE, :] = jnp.zeros((MORE, BLOCK), F32)
 
 
 def message(surface, above, below, strip):
     return call(
         message_kernel,
-        out(SURF + STRIP),
+        (out(SURF + STRIP), out(SURF + STRIP + MORE)),
         [VMEM] * 4,
-        VMEM,
+        (VMEM,) * 2,
         [],
         (surface, above, below, strip),
         100_000,
@@ -455,7 +463,8 @@
 
 
 RAW = SURF + 8
-PARTIAL = SURF + 16
+MORE = 8
+PARTIAL = RAW + 2 * MORE
 
 
 def first_contact_kernel(
@@ -490,19 +499,20 @@
         u_out[here, :] = surface[here, :] + TIME_STEP * new
 
 
-def reaction_kernel(lhs, mortar, place, raw_out, prod):
+def reaction_kernel(lhs, mortar, place, raw_out, longer, prod):
     raw = reactions(lhs, mortar, prod)
     raw_out[SURF:RAW, :] = jnp.broadcast_to(place_table(place[...] & (LIVE - 1)), (8, BLOCK))
     for c in range(3):
         raw_out[c * ROWS_DEV : (c + 1) * ROWS_DEV, :] = raw[c]
+    lengthen(raw_out, longer)
 
 
 def reaction(*args):
     return call(
         reaction_kernel,
-        out(RAW),
+        (out(RAW), out(RAW + MORE)),
         [VMEM] * 3,
-        VMEM,
+        (VMEM,) * 2,
         [pltpu.VMEM((ROWS_DEV * 8, BLOCK), F32)],
         args,
         2_000_000,
@@ -579,17 +589,20 @@
     )
 
 
-def collect_kernel(partial, own, left, right, comb_out, u_out):
+def collect_kernel(partial, own, left, right, comb_out, u_out, longer):
     comb = collected([(three(x), x[SURF : SURF + 1, :]) for x in (left, own, right)])
     for c in range(3):
         here = slice(c * ROWS_DEV, (c + 1) * ROWS_DEV)
         comb_out[here, :] = comb[c]
         u_out[here, :] = partial[here, :] + TIME_STEP * TIME_STEP * comb[c]
+    comb_out[SURF : SURF + 2 * MORE, :] = jnp.zeros((2 * MORE, BLOCK), F32)
+    lengthen(u_out, longer)
 
 
 def collect(*args):
     return call(
-        collect_kernel, (out(SURF), out(SURF)), [VMEM] * 4, (VMEM,) * 2, [], args, 1_000_000, 600_000
+        collect_kernel, (out(SURF + 2 * MORE), out(SURF), out(SURF + MORE)), [VMEM] * 4,
+        (VMEM,) * 3, [], args, 1_000_000, 600_000,
     )
 
 
@@ -643,17 +656,19 @@
     )
 
 
-def second_message_kernel(raw, strip, above, below, message):
+def second_message_kernel(raw, strip, above, below, message, longer):
     message[0:RAW, :] = raw[...]
     message[RAW : RAW + ROWS_DEV, :] = strip[...]
     message[RAW + ROWS_DEV : RAW + STRIP, :] = jnp.zeros((STRIP - ROWS_DEV, BLOCK), F32)
     message[RAW + ROWS_DEV : RAW + ROWS_DEV + 1, :] = ends_of_row(below[...])
     message[RAW + STRIP - 1 : RAW + STRIP, :] = ends_of_row(above[...])
+    lengthen(message, longer)
 
 
 def second_message(*args):
     return call(
-        second_message_kernel, out(RAW + STRIP), [VMEM] * 4, VMEM, [], args, 100_000, 300_000
+        second_message_kernel, (out(RAW + STRIP), out(RAW + STRIP + MORE)), [VMEM] * 4,
+        (VMEM,) * 2, [], args, 100_000, 300_000,
     )
 
 
@@ -730,6 +745,24 @@
                     copies.append(copy)
             begin = k + 1
     forces_kernel((0, SECOND_LOW), True, u, shear, old_v, comb_own, v_low, z, mask, comb_home)
+    for k in range(FIRST_FINAL, SECOND_LOW):
+        for c in range(3):
+            plane = c * DEPTH + k
+            new = v_low[c * SECOND_LOW + k, :, :] + from_strip(ring, plane)
+            new = new + jnp.where(
+                sub == 0, jnp.broadcast_to(top[c][k : k + 1], sub.shape), 0.0
+            )
+            new = new + jnp.where(
+                sub == ROWS_DEV - 1, jnp.broadcast_to(bottom[c][k : k + 1], sub.shape), 0.0
+            )
+            v_out[plane, :, :] = new
+            u_out[plane, :, :] = u[plane, 0:ROWS_DEV, :] + TIME_STEP * new
+    for c in range(3):
+        group = pl.ds(c * DEPTH + FIRST_FINAL, SECOND_LOW - FIRST_FINAL)
+        for source, target in ((u_out, u_hbm), (v_out, v_hbm)):
+            copy = pltpu.make_async_copy(source.at[group], target.at[group], sems.at[len(copies)])
+            copy.start()
+            copies.append(copy)
     for copy in copies:
         copy.wait()
 
@@ -746,7 +779,7 @@
             pltpu.VMEM((3 * SECOND_LOW, STRIP, BLOCK), F32),
             pltpu.VMEM((ROWS_DEV, BLOCK), F32),
             pltpu.VMEM((3, STRIP, BLOCK), F32),
-            pltpu.SemaphoreType.DMA((24,)),
+            pltpu.SemaphoreType.DMA((30,)),
         ],
         args,
         10_000_000,
@@ -786,8 +819,9 @@
         old_last[PLANES:64, :], old_above[PLANES:64, :],
     )
     sub = iota((ROWS_DEV, BLOCK), 0)
-    for k in range(SECOND_LOW):
-        for c in range(3):
+    copies = []
+    for c in range(3):
+        for k in range(FIRST_FINAL):
             plane = c * DEPTH + k
             new = v_low[c * SECOND_LOW + k, :, :] + from_strip(ring, plane)
             new = new + jnp.where(
@@ -801,12 +835,10 @@
                 here = slice(c * ROWS_DEV, (c + 1) * ROWS_DEV)
                 new = new + TIME_STEP * (slave[here, :] + comb[here, :])
                 old_u = old_u + TIME_STEP * TIME_STEP * comb_own[here, :]
-            v_out[c * SECOND_LOW + k, :, :] = new
-            u_out[c * SECOND_LOW + k, :, :] = old_u + TIME_STEP * new
-    copies = []
-    for c in range(3):
-        source_at = pl.ds(c * SECOND_LOW, SECOND_LOW)
-        target_at = pl.ds(c * DEPTH, SECOND_LOW)
+            v_out[c * FIRST_FINAL + k, :, :] = new
+            u_out[c * FIRST_FINAL + k, :, :] = old_u + TIME_STEP * new
+        source_at = pl.ds(c * FIRST_FINAL, FIRST_FINAL)
+        target_at = pl.ds(c * DEPTH, FIRST_FINAL)
         for source, target in ((u_out, u_hbm), (v_out, v_hbm)):
             copies.append(
                 pltpu.make_async_copy(
@@ -825,8 +857,8 @@
         in_specs=[VMEM] * 17 + [ANY] * 2,
         out_specs=(ANY,) * 2,
         scratch_shapes=[
-            pltpu.VMEM((3 * SECOND_LOW, ROWS_DEV, BLOCK), F32),
-            pltpu.VMEM((3 * SECOND_LOW, ROWS_DEV, BLOCK), F32),
+            pltpu.VMEM((3 * FIRST_FINAL, ROWS_DEV, BLOCK), F32),
+            pltpu.VMEM((3 * FIRST_FINAL, ROWS_DEV, BLOCK), F32),
             pltpu.VMEM((64, BLOCK), F32),
             pltpu.VMEM((64, BLOCK), F32),
             pltpu.VMEM((PLANES, BLOCK), F32),
@@ -858,7 +890,6 @@
     displacement = jnp.pad(
         displacement.reshape(PLANES, ROWS_DEV, BLOCK), ((0, 0), (0, STRIP - ROWS_DEV), (0, 0))
     )
-    shear = jnp.pad(shear, ((0, 0), (0, STRIP - ROWS_DEV), (0, 0)))
     surface, first, last = pack(displacement, shear)
     opposite = moved(surface, "gy", half)
     above = moved(last, "gx", 1)
@@ -868,9 +899,9 @@
     damped = DAMPING * velocity.reshape(PLANES, ROWS_DEV, BLOCK)
     surface_v = damped.reshape(3, DEPTH, ROWS_DEV, BLOCK)[:, 0].reshape(SURF, BLOCK)
     strip, surface_v = lax.optimization_barrier((strip, surface_v))
-    sent = message(opposite, above, below, strip)
+    sent, longer = message(opposite, above, below, strip)
     across = exchanged(sent, 1)
-    within = exchanged(sent, 0)
+    within = exchanged(longer, 0)
     sent, displacement, owner, blocks, live_rows = lax.optimization_barrier(
         (sent, displacement, owner, blocks, live_rows)
     )
@@ -884,25 +915,25 @@
         surface_v, *pairing,
     )
     part_opposite = moved(part_u, "gy", half)
-    raw = reaction(lhs, flat_mortar, place)
-    raw_across = exchanged(raw, 1)
+    raw, longer = reaction(lhs, flat_mortar, place)
+    raw_across = exchanged(longer, 1)
     raw_within = exchanged(raw, 0)
     raw, displacement = lax.optimization_barrier((raw, displacement))
     high = inner_forces((FIRST_LOW, DEPTH), displacement, shear)
     u, v, strip, first2, last2 = update(displacement, damped, low, high, ring, rows, part_u, part_v)
 
     raw, first2 = lax.optimization_barrier((raw, first2))
-    comb, center = collect(part_opposite, raw, raw_across, raw_within)
+    comb, center, longer = collect(part_opposite, raw, raw_across, raw_within)
     comb_own = moved(comb, "gy", half)
-    across2 = exchanged(center, 1)
+    across2 = exchanged(longer, 1)
     within2 = exchanged(center, 0)
     first3, last3 = outer_rows(first2, last2, center)
     above2 = moved(last3, "gx", 1)
     below2 = moved(first3, "gx", -1)
 
     raw, strip, slave = second_contact(part_u, comb_own, center, across2, within2, strip, *pairing)
-    sent2 = second_message(raw, strip, above2, below2)
-    across3 = exchanged(sent2, 1)
+    sent2, longer = second_message(raw, strip, above2, below2)
+    across3 = exchanged(longer, 1)
     within3 = exchanged(sent2, 0)
     sent2, u = lax.optimization_barrier((sent2, u))
     high = inner_forces((SECOND_LOW, DEPTH), u, shear, v, part_u)

time: 59.5 us -> 60 us (level)
  waiting for transfers between devices: 6.94 us -> 8.97 us
  local copies, waits for them, and re-layouts: 3.26 us -> 1.75 us
    pad x1 -> x0, local copies, waits for them, and re-layouts: 1.07 us -> none  [local(): shear = jnp.pad(shear, ((0, 0), (0, STRIP - ROWS_DEV), (0, 0)))]
    ppermute x8, waiting for transfers between devices: 2.23 us -> 3.27 us  [moved(): return lax.ppermute(x, axis, [(i, (i + by) % count) for i in range(count)])]
    ppermute x8, waiting for transfers between devices: 4.71 us -> 5.7 us  [exchanged(): return lax.ppermute(x, 'gy', [(i, j % count) for i, j in pairs])]
    pallas_call x15, Pallas kernels: 18.2 us -> 18.9 us  [call(): pl.pallas_call(kernel, out_shape=out_shape, in_specs=in_specs, out_specs=...]
    ppermute x8, starting transfers between devices: 20.1 us -> 19.4 us  [moved(): return lax.ppermute(x, axis, [(i, (i + by) % count) for i in range(count)])]
  transfers between devices with their start and end apart: 16 -> 16, of which waited for: 5 -> 5; matrix products, arithmetic and copies ran while one was open for 1% -> 1% of each run, Pallas kernels for 27% -> 28%
where the time goes in v4:
time: 60 us; the launch traced here: 59.9 us
  starting transfers between devices  26.9 us (45%)
  Pallas kernels  20.5 us (34%)
  waiting for transfers between devices  8.97 us (15%)
  local copies, waits for them, and re-layouts  1.75 us (3%)
  between operations  1.54 us (3%)
    ppermute x8, starting transfers between devices, moved(): return lax.ppermute(x, axis, [(i, (i + by) % count) for i in range(count)])  19.4 us
    pallas_call x15, Pallas kernels, call(): pl.pallas_call(kernel, out_shape=out_shape, in_specs=in_specs, out_specs=...  18.9 us
    ppermute x8, starting transfers between devices, exchanged(): return lax.ppermute(x, 'gy', [(i, j % count) for i, j in pairs])  7.47 us
    ppermute x8, waiting for transfers between devices, exchanged(): return lax.ppermute(x, 'gy', [(i, j % count) for i, j in pairs])  5.7 us
    ppermute x8, waiting for transfers between devices, moved(): return lax.ppermute(x, axis, [(i, (i + by) % count) for i in range(count)])  3.27 us
    pad x1, local copies, waits for them, and re-layouts, local(): jnp.pad(displacement.reshape(PLANES, ROWS_DEV, BLOCK), ((0, 0), (0, STRIP...  1.59 us
    pallas_call x1, Pallas kernels, last_surface(): pl.pallas_call(last_surface_kernel, out_shape=(planes(PLANES), planes(PLA...  1.52 us
  transfers between devices with their start and end apart: 16, of which 5 were waited for; matrix products, arithmetic and copies ran while one was open for 1% of the time, Pallas kernels for 28%

profile of v4, /device:TPU:0, one launch (start us, length us, event | category | flops | bytes accessed | tf_op | source)
XLA Modules:
  0.0 59.9 jit_solution(6753058656927997165)
XLA Ops:
  0.6 1.6 %pad.4.u.refs_0_ = f32[48,72,128]{2,1,0:T(8,128)S(1)} pad(f32[48,64,128]{2,1,0:T(8,128)} %bitcast.16, f32[]{:T(128)} %constant.1.clone.1), padding=0_0x0_8x0_0 | pad | bytes 3342340 | tf_op jit(solution)/shard_map/jit(_pad)/pad | solution.py:890
  2.3 5.6 %collective-permute-start.2 = (f32[64,128]{1,0:T(8,128)S(1)}, f32[64,128]{1,0:T(8,128)S(1)}, u32[]{:S(2)}, u32[]{:S(2)}) collective-permute-start(f32[64,128]{1,0:T(8,128)S(1)} %get-tuple-element.53.first), channel_id=1, source_target_pairs={{0,112},{16,0},{32,16},{48,32},{64,48},{80,64},{96,80},{112,96},{1... | collective-permute-start | bytes 98312 | tf_op jit(solution)/shard_map/ppermute | solution.py:876
  8.0 3.9 %collective-permute-start = (f32[192,128]{1,0:T(8,128)S(1)}, f32[192,128]{1,0:T(8,128)S(1)}, u32[]{:S(2)}, u32[]{:S(2)}) collective-permute-start(f32[192,128]{1,0:T(8,128)S(1)} %get-tuple-element.51.surface), channel_id=1, source_target_pairs={{0,8},{1,9},{2,10},{3,11},{4,12},{5,13},{6,14},{7,15},{8,0},{9,1},... | collective-permute-start | bytes 294920 | tf_op jit(solution)/shard_map/ppermute | solution.py:876
  11.8 0.2 broadcast_multiply_fusion
  12.1 0.6 %shard_map.105.strip = f32[72,128]{1,0:T(8,128)S(1)} custom-call(f32[48,72,128]{2,1,0:T(8,128)S(1)} %pad.4.u.refs_0_, f32[15,64,128]{2,1,0:T(8,128)S(1)} %copy-done.1), custom_call_target="tpu_custom_call" | custom-call | flops 1000 | bytes 1000 | tf_op jit(solution)/shard_map/pallas_call | solution.py:37
  13.4 2.1 %collective-permute-done.1.above.old_above = f32[64,128]{1,0:T(8,128)S(1)} collective-permute-done((f32[64,128]{1,0:T(8,128)S(1)}, f32[64,128]{1,0:T(8,128)S(1)}, u32[]{:S(2)}, u32[]{:S(2)}) %collective-permute-start.1) | collective-permute-done | bytes 32800 | tf_op jit(solution)/shard_map/ppermute | solution.py:876
  15.5 0.1 shard_map.106
  15.6 2.2 %collective-permute-start.3 = (f32[264,128]{1,0:T(8,128)S(1)}, f32[264,128]{1,0:T(8,128)S(1)}, u32[]{:S(2)}, u32[]{:S(2)}) collective-permute-start(f32[264,128]{1,0:T(8,128)S(1)} %get-tuple-element.56.sent.old_sent), channel_id=1, source_target_pairs={{0,15},{1,2},{2,1},{3,4},{4,3},{5,6},{6,5},{7,8},{8,7},{9,10},{10,... | collective-permute-start | bytes 405512 | tf_op jit(solution)/shard_map/ppermute | solution.py:882
  18.0 2.8 %shard_map.107.low = f32[30,64,128]{2,1,0:T(8,128)S(1)} custom-call(f32[48,72,128]{2,1,0:T(8,128)S(1)} %pad.4.u.refs_0_, f32[15,64,128]{2,1,0:T(8,128)S(1)} %copy-done.1), custom_call_target="tpu_custom_call" | custom-call | flops 1000 | bytes 1000 | tf_op jit(solution)/shard_map/pallas_call | solution.py:37
  20.8 2.4 %collective-permute-done.3.across.old_across = f32[264,128]{1,0:T(8,128)S(1)} collective-permute-done((f32[264,128]{1,0:T(8,128)S(1)}, f32[264,128]{1,0:T(8,128)S(1)}, u32[]{:S(2)}, u32[]{:S(2)}) %collective-permute-start.3) | collective-permute-done | bytes 135200 | tf_op jit(solution)/shard_map/ppermute | solution.py:882
  23.3 1.5 %shard_map.108 = (f32[512,128]{1,0:T(8,128)S(1)}, f32[216,128]{1,0:T(8,128)S(1)}, f32[192,128]{1,0:T(8,128)S(1)}, f32[64,128]{1,0:T(8,128)S(1)}, f32[96,128]{1,0:T(8,128)S(1)}) custom-call(f32[192,128]{1,0:T(8,128)S(1)} %get-tuple-element.51.surface, f32[264,128]{1,0:T(8,128)S(1)} %get-tuple-element.56.sent.old_sent, ...), custom_call_target="tpu_custom_call" | custom-call | flops 1000 | bytes 1000 | tf_op jit(solution)/shard_map/pallas_call | solution.py:37
  24.8 1.7 %collective-permute-start.5 = (f32[216,128]{1,0:T(8,128)S(1)}, f32[216,128]{1,0:T(8,128)S(1)}, u32[]{:S(2)}, u32[]{:S(2)}) collective-permute-start(f32[216,128]{1,0:T(8,128)S(1)} %get-tuple-element.63.surface.partial.refs_3_), channel_id=1, source_target_pairs={{0,8},{1,9},{2,10},{3,11},{4,12},{5,13},{6,14},{7,15},{8,0},{9,1},... | collective-permute-start | bytes 331784 | tf_op jit(solution)/shard_map/ppermute | solution.py:876
  26.5 0.7 %shard_map.109 = (f32[200,128]{1,0:T(8,128)S(1)}, f32[208,128]{1,0:T(8,128)S(1)}) custom-call(f32[512,128]{1,0:T(8,128)S(1)} %get-tuple-element.64.lhs, bf16[8192,128]{1,0:T(8,128)(2,1)S(1)} %bitcast.10, s32[64,1]{1,0:T(8,128)S(1)} %select_add_fusion.place), custom_call_target="tpu_custom_call" | custom-call | flops 1000 | bytes 1000 | tf_op jit(solution)/shard_map/pallas_call | solution.py:37
  27.2 1.8 %collective-permute-start.6 = (f32[208,128]{1,0:T(8,128)S(1)}, f32[208,128]{1,0:T(8,128)S(1)}, u32[]{:S(2)}, u32[]{:S(2)}) collective-permute-start(f32[208,128]{1,0:T(8,128)S(1)} %get-tuple-element.73), channel_id=1, source_target_pairs={{0,15},{1,2},{2,1},{3,4},{4,3},{5,6},{6,5},{7,8},{8,7},{9,10},{10,... | collective-permute-start | bytes 319496 | tf_op jit(solution)/shard_map/ppermute | solution.py:882
  29.0 2.1 %shard_map.110.high = f32[18,64,128]{2,1,0:T(8,128)S(1)} custom-call(f32[48,72,128]{2,1,0:T(8,128)S(1)} %pad.4.u.refs_0_, f32[15,64,128]{2,1,0:T(8,128)S(1)} %copy-done.1), custom_call_target="tpu_custom_call" | custom-call | flops 1000 | bytes 1000 | tf_op jit(solution)/shard_map/pallas_call | solution.py:37
  31.2 0.9 %shard_map.111 = (f32[48,72,128]{2,1,0:T(8,128)S(1)}, f32[48,64,128]{2,1,0:T(8,128)S(1)}, f32[72,128]{1,0:T(8,128)S(1)}, f32[64,128]{1,0:T(8,128)S(1)}, f32[64,128]{1,0:T(8,128)S(1)}) custom-call(f32[48,72,128]{2,1,0:T(8,128)S(1)} %pad.4.u.refs_0_, f32[48,64,128]{2,1,0:T(8,128)S(1)} %bitcast.12, f32[30,64,128]{2,1,0:T(8,128)S(1)} %shard_map.107.low, ...), custom_call_target="tpu_custom_call" | custom-call | flops 1000 | bytes 1000 | tf_op jit(solution)/shard_map/pallas_call | solution.py:37
  32.1 1.4 %collective-permute-done.6.left = f32[208,128]{1,0:T(8,128)S(1)} collective-permute-done((f32[208,128]{1,0:T(8,128)S(1)}, f32[208,128]{1,0:T(8,128)S(1)}, u32[]{:S(2)}, u32[]{:S(2)}) %collective-permute-start.6) | collective-permute-done | bytes 106528 | tf_op jit(solution)/shard_map/ppermute | solution.py:882
  33.5 0.2 shard_map.112
  33.7 1.3 %collective-permute-start.8 = (f32[208,128]{1,0:T(8,128)S(1)}, f32[208,128]{1,0:T(8,128)S(1)}, u32[]{:S(2)}, u32[]{:S(2)}) collective-permute-start(f32[208,128]{1,0:T(8,128)S(1)} %get-tuple-element.74), channel_id=1, source_target_pairs={{0,8},{1,9},{2,10},{3,11},{4,12},{5,13},{6,14},{7,15},{8,0},{9,1},... | collective-permute-start | bytes 319496 | tf_op jit(solution)/shard_map/ppermute | solution.py:876
  35.1 0.8 %collective-permute-start.9 = (f32[200,128]{1,0:T(8,128)S(1)}, f32[200,128]{1,0:T(8,128)S(1)}, u32[]{:S(2)}, u32[]{:S(2)}) collective-permute-start(f32[200,128]{1,0:T(8,128)S(1)} %get-tuple-element.76), channel_id=1, source_target_pairs={{0,15},{1,2},{2,1},{3,4},{4,3},{5,6},{6,5},{7,8},{8,7},{9,10},{10,... | collective-permute-start | bytes 307208 | tf_op jit(solution)/shard_map/ppermute | solution.py:882
  35.9 0.5 collective-permute-start.11
  36.5 5.2 %collective-permute-start.12 = (f32[64,128]{1,0:T(8,128)S(1)}, f32[64,128]{1,0:T(8,128)S(1)}, u32[]{:S(2)}, u32[]{:S(2)}) collective-permute-start(f32[64,128]{1,0:T(8,128)S(1)} %get-tuple-element.83), channel_id=1, source_target_pairs={{0,112},{16,0},{32,16},{48,32},{64,48},{80,64},{96,80},{112,96},{1... | collective-permute-start | bytes 98312 | tf_op jit(solution)/shard_map/ppermute | solution.py:876
  41.6 2.0 %shard_map.113 = (f32[200,128]{1,0:T(8,128)S(1)}, f32[64,128]{1,0:T(8,128)S(1)}, f32[192,128]{1,0:T(8,128)S(1)}) custom-call(f32[216,128]{1,0:T(8,128)S(1)} %get-tuple-element.63.surface.partial.refs_3_, f32[208,128]{1,0:T(8,128)S(1)} %collective-permute-done.8.comb.comb_own, f32[192,128]{1,0:T(8,128)S(1)} %get-tuple-element.75.center, ...), custom_call_target="tpu_custom_call" | custom-call | flops 1000 | bytes 1000 | tf_op jit(solution)/shard_map/pallas_call | solution.py:37
  43.7 0.1 shard_map.115
  43.8 2.5 %collective-permute-start.13 = (f32[280,128]{1,0:T(8,128)S(1)}, f32[280,128]{1,0:T(8,128)S(1)}, u32[]{:S(2)}, u32[]{:S(2)}) collective-permute-start(f32[280,128]{1,0:T(8,128)S(1)} %get-tuple-element.90), channel_id=1, source_target_pairs={{0,15},{1,2},{2,1},{3,4},{4,3},{5,6},{6,5},{7,8},{8,7},{9,10},{10,... | collective-permute-start | bytes 430088 | tf_op jit(solution)/shard_map/ppermute | solution.py:882
  46.3 3.7 %shard_map.116.v_high = f32[39,64,128]{2,1,0:T(8,128)S(1)} custom-call(f32[48,72,128]{2,1,0:T(8,128)S(1)} %get-tuple-element.92.refs_0_.u, f32[15,64,128]{2,1,0:T(8,128)S(1)} %copy-done.1, f32[48,64,128]{2,1,0:T(8,128)S(1)} %get-tuple-element.88.refs_2_.old_v, f32[216,128]{1,0:T(8,128)S(1)} %get-tuple-element.63.surface.partial.refs_3_), custom_call_target="tpu_custom_call" | custom-call | flops 1000 | bytes 1000 | tf_op jit(solution)/shard_map/pallas_call | solution.py:37
  50.1 1.8 %collective-permute-done.13.across = f32[280,128]{1,0:T(8,128)S(1)} collective-permute-done((f32[280,128]{1,0:T(8,128)S(1)}, f32[280,128]{1,0:T(8,128)S(1)}, u32[]{:S(2)}, u32[]{:S(2)}) %collective-permute-start.13) | collective-permute-done | bytes 143392 | tf_op jit(solution)/shard_map/ppermute | solution.py:882
  51.9 0.2 shard_map.117
  52.1 1.2 %collective-permute-start.15 = (f32[200,128]{1,0:T(8,128)S(1)}, f32[200,128]{1,0:T(8,128)S(1)}, u32[]{:S(2)}, u32[]{:S(2)}) collective-permute-start(f32[200,128]{1,0:T(8,128)S(1)} %shard_map.117), channel_id=1, source_target_pairs={{0,8},{1,9},{2,10},{3,11},{4,12},{5,13},{6,14},{7,15},{8,0},{9,1},... | collective-permute-start | bytes 307208 | tf_op jit(solution)/shard_map/ppermute | solution.py:876
  53.3 3.9 %shard_map.118 = (f32[48,64,128]{2,1,0:T(8,128)}, f32[48,64,128]{2,1,0:T(8,128)}, f32[9,64,128]{2,1,0:T(8,128)S(1)}) custom-call(f32[48,72,128]{2,1,0:T(8,128)S(1)} %get-tuple-element.92.refs_0_.u, f32[15,64,128]{2,1,0:T(8,128)S(1)} %copy-done.1, f32[48,64,128]{2,1,0:T(8,128)S(1)} %get-tuple-element.88.refs_2_.old_v, ...), custom_call_target="tpu_custom_call" | custom-call | flops 1000 | bytes 1000 | tf_op jit(solution)/shard_map/pallas_call | solution.py:37
  57.2 1.2 %collective-permute-done.15.comb = f32[200,128]{1,0:T(8,128)S(1)} collective-permute-done((f32[200,128]{1,0:T(8,128)S(1)}, f32[200,128]{1,0:T(8,128)S(1)}, u32[]{:S(2)}, u32[]{:S(2)}) %collective-permute-start.15) | collective-permute-done | bytes 102432 | tf_op jit(solution)/shard_map/ppermute | solution.py:876
  58.4 1.5 %shard_map.119 = (f32[48,64,128]{2,1,0:T(8,128)}, f32[48,64,128]{2,1,0:T(8,128)}) custom-call(f32[48,72,128]{2,1,0:T(8,128)S(1)} %get-tuple-element.92.refs_0_.u, f32[9,64,128]{2,1,0:T(8,128)S(1)} %get-tuple-element.94.v_low, f32[192,128]{1,0:T(8,128)S(1)} %get-tuple-element.95.slave, ...), custom_call_target="tpu_custom_call", output_to_operand_aliasing={{0}: (17, {}), {1}: (18, {})} | custom-call | flops 1000 | bytes 1000 | tf_op jit(solution)/shard_map/pallas_call | solution.py:854
  (40 shorter events, 0.4 us)
Async XLA Ops:
  0.6 1.6 %copy-start.1 = (f32[15,64,128]{2,1,0:T(8,128)S(1)}, f32[15,64,128]{2,1,0:T(8,128)}, u32[]{:S(2)}) copy-start(f32[15,64,128]{2,1,0:T(8,128)} %shear.5) | copy-start | bytes 1474564
  2.3 9.6 %copy-start.6 = (f32[3,16,64,128]{3,2,1,0:T(8,128)S(1)}, f32[3,16,64,128]{3,2,1,0:T(8,128)}, u32[]{:S(2)}) copy-start(f32[3,16,64,128]{3,2,1,0:T(8,128)} %param.10) | copy-start | bytes 4718596
  2.3 11.1 %collective-permute-start.2 = (f32[64,128]{1,0:T(8,128)S(1)}, f32[64,128]{1,0:T(8,128)S(1)}, u32[]{:S(2)}, u32[]{:S(2)}) collective-permute-start(f32[64,128]{1,0:T(8,128)S(1)} %get-tuple-element.53.first), channel_id=1, source_target_pairs={{0,112},{16,0},{32,16},{48,32},{64,48},{80,64},{96,80},{112,96},{1... | collective-permute-start | bytes 98312 | tf_op jit(solution)/shard_map/ppermute | solution.py:876
  7.9 7.5 %collective-permute-start.1 = (f32[64,128]{1,0:T(8,128)S(1)}, f32[64,128]{1,0:T(8,128)S(1)}, u32[]{:S(2)}, u32[]{:S(2)}) collective-permute-start(f32[64,128]{1,0:T(8,128)S(1)} %get-tuple-element.52.last.old_last), channel_id=1, source_target_pairs={{0,16},{16,32},{32,48},{48,64},{64,80},{80,96},{96,112},{112,0},{1... | collective-permute-start | bytes 98312 | tf_op jit(solution)/shard_map/ppermute | solution.py:876
  8.0 7.5 %collective-permute-start = (f32[192,128]{1,0:T(8,128)S(1)}, f32[192,128]{1,0:T(8,128)S(1)}, u32[]{:S(2)}, u32[]{:S(2)}) collective-permute-start(f32[192,128]{1,0:T(8,128)S(1)} %get-tuple-element.51.surface), channel_id=1, source_target_pairs={{0,8},{1,9},{2,10},{3,11},{4,12},{5,13},{6,14},{7,15},{8,0},{9,1},... | collective-permute-start | bytes 294920 | tf_op jit(solution)/shard_map/ppermute | solution.py:876
  12.1 1.3 %copy-start.2 = (f32[3,16,64,128]{3,2,1,0:T(8,128)}, f32[3,16,64,128]{3,2,1,0:T(8,128)S(1)}, u32[]{:S(2)}) copy-start(f32[3,16,64,128]{3,2,1,0:T(8,128)S(1)} %broadcast_multiply_fusion) | copy-start | bytes 4718596
  12.1 5.7 %copy-start.7 = (s32[64,1]{0,1:T(1,128)S(1)}, s32[64,1]{0,1:T(1,128)}, u32[]{:S(2)}) copy-start(s32[64,1]{0,1:T(1,128)} %param.16) | copy-start | bytes 772
  12.1 5.7 %copy-start.8 = (s32[64,1]{0,1:T(1,128)S(1)}, s32[64,1]{0,1:T(1,128)}, u32[]{:S(2)}) copy-start(s32[64,1]{0,1:T(1,128)} %param.15) | copy-start | bytes 772
  15.6 7.6 %collective-permute-start.3 = (f32[264,128]{1,0:T(8,128)S(1)}, f32[264,128]{1,0:T(8,128)S(1)}, u32[]{:S(2)}, u32[]{:S(2)}) collective-permute-start(f32[264,128]{1,0:T(8,128)S(1)} %get-tuple-element.56.sent.old_sent), channel_id=1, source_target_pairs={{0,15},{1,2},{2,1},{3,4},{4,3},{5,6},{6,5},{7,8},{8,7},{9,10},{10,... | collective-permute-start | bytes 405512 | tf_op jit(solution)/shard_map/ppermute | solution.py:882
  17.9 5.4 %copy-start = (bf16[64,1,128,128]{3,2,1,0:T(8,128)(2,1)S(1)}, bf16[64,1,128,128]{3,2,1,0:T(8,128)(2,1)}, u32[]{:S(2)}) copy-start(bf16[64,1,128,128]{3,2,1,0:T(8,128)(2,1)} %param.14) | copy-start | bytes 6291460
  17.9 5.4 %copy-start.4 = (f32[3,64,128]{2,1,0:T(8,128)S(1)}, f32[3,64,128]{2,1,0:T(8,128)}, u32[]{:S(2)}) copy-start(f32[3,64,128]{2,1,0:T(8,128)} %param.12) | copy-start | bytes 294916
  17.9 5.4 %copy-start.5 = (f32[64,128]{1,0:T(8,128)S(1)}, f32[64,128]{1,0:T(8,128)}, u32[]{:S(2)}) copy-start(f32[64,128]{1,0:T(8,128)} %gap.3) | copy-start | bytes 98308
  17.9 5.4 %collective-permute-start.4 = (f32[272,128]{1,0:T(8,128)S(1)}, f32[272,128]{1,0:T(8,128)S(1)}, u32[]{:S(2)}, u32[]{:S(2)}) collective-permute-start(f32[272,128]{1,0:T(8,128)S(1)} %get-tuple-element.57), channel_id=1, source_target_pairs={{0,1},{1,0},{2,3},{3,2},{4,5},{5,4},{6,7},{7,6},{8,9},{9,8},{10,11... | collective-permute-start | bytes 417800 | tf_op jit(solution)/shard_map/ppermute | solution.py:882
  24.8 8.7 %collective-permute-start.5 = (f32[216,128]{1,0:T(8,128)S(1)}, f32[216,128]{1,0:T(8,128)S(1)}, u32[]{:S(2)}, u32[]{:S(2)}) collective-permute-start(f32[216,128]{1,0:T(8,128)S(1)} %get-tuple-element.63.surface.partial.refs_3_), channel_id=1, source_target_pairs={{0,8},{1,9},{2,10},{3,11},{4,12},{5,13},{6,14},{7,15},{8,0},{9,1},... | collective-permute-start | bytes 331784 | tf_op jit(solution)/shard_map/ppermute | solution.py:876
  27.2 4.0 %copy-start.3 = (f32[3,16,64,128]{3,2,1,0:T(8,128)S(1)}, f32[3,16,64,128]{3,2,1,0:T(8,128)}, u32[]{:S(2)}) copy-start(f32[3,16,64,128]{3,2,1,0:T(8,128)} %copy-done.2) | copy-start | bytes 4718596
  27.2 6.3 %collective-permute-start.6 = (f32[208,128]{1,0:T(8,128)S(1)}, f32[208,128]{1,0:T(8,128)S(1)}, u32[]{:S(2)}, u32[]{:S(2)}) collective-permute-start(f32[208,128]{1,0:T(8,128)S(1)} %get-tuple-element.73), channel_id=1, source_target_pairs={{0,15},{1,2},{2,1},{3,4},{4,3},{5,6},{6,5},{7,8},{8,7},{9,10},{10,... | collective-permute-start | bytes 319496 | tf_op jit(solution)/shard_map/ppermute | solution.py:882
  29.0 3.0 %collective-permute-start.7 = (f32[200,128]{1,0:T(8,128)S(1)}, f32[200,128]{1,0:T(8,128)S(1)}, u32[]{:S(2)}, u32[]{:S(2)}) collective-permute-start(f32[200,128]{1,0:T(8,128)S(1)} %get-tuple-element.72.own), channel_id=1, source_target_pairs={{0,1},{1,0},{2,3},{3,2},{4,5},{5,4},{6,7},{7,6},{8,9},{9,8},{10,11... | collective-permute-start | bytes 307208 | tf_op jit(solution)/shard_map/ppermute | solution.py:882
  33.7 7.9 %collective-permute-start.8 = (f32[208,128]{1,0:T(8,128)S(1)}, f32[208,128]{1,0:T(8,128)S(1)}, u32[]{:S(2)}, u32[]{:S(2)}) collective-permute-start(f32[208,128]{1,0:T(8,128)S(1)} %get-tuple-element.74), channel_id=1, source_target_pairs={{0,8},{1,9},{2,10},{3,11},{4,12},{5,13},{6,14},{7,15},{8,0},{9,1},... | collective-permute-start | bytes 319496 | tf_op jit(solution)/shard_map/ppermute | solution.py:876
  35.1 6.6 %collective-permute-start.9 = (f32[200,128]{1,0:T(8,128)S(1)}, f32[200,128]{1,0:T(8,128)S(1)}, u32[]{:S(2)}, u32[]{:S(2)}) collective-permute-start(f32[200,128]{1,0:T(8,128)S(1)} %get-tuple-element.76), channel_id=1, source_target_pairs={{0,15},{1,2},{2,1},{3,4},{4,3},{5,6},{6,5},{7,8},{8,7},{9,10},{10,... | collective-permute-start | bytes 307208 | tf_op jit(solution)/shard_map/ppermute | solution.py:882
  35.9 5.7 %collective-permute-start.10 = (f32[192,128]{1,0:T(8,128)S(1)}, f32[192,128]{1,0:T(8,128)S(1)}, u32[]{:S(2)}, u32[]{:S(2)}) collective-permute-start(f32[192,128]{1,0:T(8,128)S(1)} %get-tuple-element.75.center), channel_id=1, source_target_pairs={{0,1},{1,0},{2,3},{3,2},{4,5},{5,4},{6,7},{7,6},{8,9},{9,8},{10,11... | collective-permute-start | bytes 294920 | tf_op jit(solution)/shard_map/ppermute | solution.py:882
  35.9 7.7 %collective-permute-start.11 = (f32[64,128]{1,0:T(8,128)S(1)}, f32[64,128]{1,0:T(8,128)S(1)}, u32[]{:S(2)}, u32[]{:S(2)}) collective-permute-start(f32[64,128]{1,0:T(8,128)S(1)} %get-tuple-element.82), channel_id=1, source_target_pairs={{0,16},{16,32},{32,48},{48,64},{64,80},{80,96},{96,112},{112,0},{1... | collective-permute-start | bytes 98312 | tf_op jit(solution)/shard_map/ppermute | solution.py:876
  36.5 7.2 %collective-permute-start.12 = (f32[64,128]{1,0:T(8,128)S(1)}, f32[64,128]{1,0:T(8,128)S(1)}, u32[]{:S(2)}, u32[]{:S(2)}) collective-permute-start(f32[64,128]{1,0:T(8,128)S(1)} %get-tuple-element.83), channel_id=1, source_target_pairs={{0,112},{16,0},{32,16},{48,32},{64,48},{80,64},{96,80},{112,96},{1... | collective-permute-start | bytes 98312 | tf_op jit(solution)/shard_map/ppermute | solution.py:876
  43.8 8.1 %collective-permute-start.13 = (f32[280,128]{1,0:T(8,128)S(1)}, f32[280,128]{1,0:T(8,128)S(1)}, u32[]{:S(2)}, u32[]{:S(2)}) collective-permute-start(f32[280,128]{1,0:T(8,128)S(1)} %get-tuple-element.90), channel_id=1, source_target_pairs={{0,15},{1,2},{2,1},{3,4},{4,3},{5,6},{6,5},{7,8},{8,7},{9,10},{10,... | collective-permute-start | bytes 430088 | tf_op jit(solution)/shard_map/ppermute | solution.py:882
  46.3 3.7 %collective-permute-start.14 = (f32[272,128]{1,0:T(8,128)S(1)}, f32[272,128]{1,0:T(8,128)S(1)}, u32[]{:S(2)}, u32[]{:S(2)}) collective-permute-start(f32[272,128]{1,0:T(8,128)S(1)} %get-tuple-element.89.own.sent), channel_id=1, source_target_pairs={{0,1},{1,0},{2,3},{3,2},{4,5},{5,4},{6,7},{7,6},{8,9},{9,8},{10,11... | collective-permute-start | bytes 417800 | tf_op jit(solution)/shard_map/ppermute | solution.py:882
  52.1 6.2 %collective-permute-start.15 = (f32[200,128]{1,0:T(8,128)S(1)}, f32[200,128]{1,0:T(8,128)S(1)}, u32[]{:S(2)}, u32[]{:S(2)}) collective-permute-start(f32[200,128]{1,0:T(8,128)S(1)} %shard_map.117), channel_id=1, source_target_pairs={{0,8},{1,9},{2,10},{3,11},{4,12},{5,13},{6,14},{7,15},{8,0},{9,1},... | collective-permute-start | bytes 307208 | tf_op jit(solution)/shard_map/ppermute | solution.py:876

commit v5 on v4

--- a/solution.py
+++ b/solution.py
@@ -250,12 +250,11 @@
     return jnp.sum(jnp.where(lanes // 2 == sub, both, 0.0), axis=0, keepdims=True)
 
 
-def message_kernel(surface, above, below, strip, message, longer):
+def message_kernel(surface, above, below, strip, message):
     message[0:SURF, :] = surface[...]
     message[SURF : SURF + STRIP, :] = strip[...]
     message[SURF + ROWS_DEV : SURF + ROWS_DEV + 1, :] = ends_of_row(below[...])
     message[SURF + STRIP - 1 : SURF + STRIP, :] = ends_of_row(above[...])
-    lengthen(message, longer)
 
 
 def lengthen(message, longer):
@@ -267,9 +266,9 @@
 def message(surface, above, below, strip):
     return call(
         message_kernel,
-        (out(SURF + STRIP), out(SURF + STRIP + MORE)),
+        out(SURF + STRIP),
         [VMEM] * 4,
-        (VMEM,) * 2,
+        VMEM,
         [],
         (surface, above, below, strip),
         100_000,
@@ -890,6 +889,7 @@
     displacement = jnp.pad(
         displacement.reshape(PLANES, ROWS_DEV, BLOCK), ((0, 0), (0, STRIP - ROWS_DEV), (0, 0))
     )
+    shear = jnp.pad(shear, ((0, 0), (0, STRIP - ROWS_DEV), (0, 0)))
     surface, first, last = pack(displacement, shear)
     opposite = moved(surface, "gy", half)
     above = moved(last, "gx", 1)
@@ -899,9 +899,9 @@
     damped = DAMPING * velocity.reshape(PLANES, ROWS_DEV, BLOCK)
     surface_v = damped.reshape(3, DEPTH, ROWS_DEV, BLOCK)[:, 0].reshape(SURF, BLOCK)
     strip, surface_v = lax.optimization_barrier((strip, surface_v))
-    sent, longer = message(opposite, above, below, strip)
+    sent = message(opposite, above, below, strip)
     across = exchanged(sent, 1)
-    within = exchanged(longer, 0)
+    within = exchanged(sent, 0)
     sent, displacement, owner, blocks, live_rows = lax.optimization_barrier(
         (sent, displacement, owner, blocks, live_rows)
     )

time: 60 us -> 59.6 us (level)
  waiting for transfers between devices: 8.97 us -> 6.64 us
  local copies, waits for them, and re-layouts: 1.75 us -> 3.26 us
    ppermute x8, waiting for transfers between devices: 3.27 us -> 1.35 us  [moved(): return lax.ppermute(x, axis, [(i, (i + by) % count) for i in range(count)])]
    pad x0 -> x1, local copies, waits for them, and re-layouts: none -> 1.07 us  [local(): shear = jnp.pad(shear, ((0, 0), (0, STRIP - ROWS_DEV), (0, 0)))]
    ppermute x8, starting transfers between devices: 19.4 us -> 20.2 us  [moved(): return lax.ppermute(x, axis, [(i, (i + by) % count) for i in range(count)])]
where the time goes in v5:
time: 59.6 us; the launch traced here: 59.4 us
  starting transfers between devices  27.2 us (46%)
  Pallas kernels  20.5 us (34%)
  waiting for transfers between devices  6.64 us (11%)
  local copies, waits for them, and re-layouts  3.26 us (5%)
  between operations  1.53 us (3%)
    ppermute x8, starting transfers between devices, moved(): return lax.ppermute(x, axis, [(i, (i + by) % count) for i in range(count)])  20.2 us
    pallas_call x15, Pallas kernels, call(): pl.pallas_call(kernel, out_shape=out_shape, in_specs=in_specs, out_specs=...  19 us
    ppermute x8, starting transfers between devices, exchanged(): return lax.ppermute(x, 'gy', [(i, j % count) for i, j in pairs])  6.99 us
    ppermute x8, waiting for transfers between devices, exchanged(): return lax.ppermute(x, 'gy', [(i, j % count) for i, j in pairs])  5.29 us
    pad x1, local copies, waits for them, and re-layouts, local(): jnp.pad(displacement.reshape(PLANES, ROWS_DEV, BLOCK), ((0, 0), (0, STRIP...  1.54 us
    pallas_call x1, Pallas kernels, last_surface(): pl.pallas_call(last_surface_kernel, out_shape=(planes(PLANES), planes(PLA...  1.53 us
    ppermute x8, waiting for transfers between devices, moved(): return lax.ppermute(x, axis, [(i, (i + by) % count) for i in range(count)])  1.35 us
  transfers between devices with their start and end apart: 16, of which 5 were waited for; matrix products, arithmetic and copies ran while one was open for 1% of the time, Pallas kernels for 28%

profile of v5, /device:TPU:0, one launch (start us, length us, event | category | flops | bytes accessed | tf_op | source)
XLA Modules:
  0.0 59.4 jit_solution(16226060411636400524)
XLA Ops:
  0.6 1.1 %pad.9.shear.refs_1_ = f32[15,72,128]{2,1,0:T(8,128)S(1)} pad(f32[15,64,128]{2,1,0:T(8,128)} %param.11, f32[]{:T(128)} %constant.1.clone.1), padding=0_0x0_8x0_0 | pad | bytes 1044484 | tf_op jit(solution)/shard_map/jit(_pad)/pad | solution.py:892
  1.7 1.5 %pad.8.u.refs_0_ = f32[48,72,128]{2,1,0:T(8,128)S(1)} pad(f32[48,64,128]{2,1,0:T(8,128)} %bitcast.16, f32[]{:T(128)} %constant.1.clone.1), padding=0_0x0_8x0_0 | pad | bytes 3342340 | tf_op jit(solution)/shard_map/jit(_pad)/pad | solution.py:889
  3.3 3.2 %collective-permute-start.1 = (f32[64,128]{1,0:T(8,128)S(1)}, f32[64,128]{1,0:T(8,128)S(1)}, u32[]{:S(2)}, u32[]{:S(2)}) collective-permute-start(f32[64,128]{1,0:T(8,128)S(1)} %get-tuple-element.50.last.old_last), channel_id=1, source_target_pairs={{0,16},{16,32},{32,48},{48,64},{64,80},{80,96},{96,112},{112,0},{1... | collective-permute-start | bytes 98312 | tf_op jit(solution)/shard_map/ppermute | solution.py:875
  6.5 2.5 %collective-permute-start.2 = (f32[64,128]{1,0:T(8,128)S(1)}, f32[64,128]{1,0:T(8,128)S(1)}, u32[]{:S(2)}, u32[]{:S(2)}) collective-permute-start(f32[64,128]{1,0:T(8,128)S(1)} %get-tuple-element.51.first), channel_id=1, source_target_pairs={{0,112},{16,0},{32,16},{48,32},{64,48},{80,64},{96,80},{112,96},{1... | collective-permute-start | bytes 98312 | tf_op jit(solution)/shard_map/ppermute | solution.py:875
  9.0 4.0 %collective-permute-start = (f32[192,128]{1,0:T(8,128)S(1)}, f32[192,128]{1,0:T(8,128)S(1)}, u32[]{:S(2)}, u32[]{:S(2)}) collective-permute-start(f32[192,128]{1,0:T(8,128)S(1)} %get-tuple-element.49.surface), channel_id=1, source_target_pairs={{0,8},{1,9},{2,10},{3,11},{4,12},{5,13},{6,14},{7,15},{8,0},{9,1},... | collective-permute-start | bytes 294920 | tf_op jit(solution)/shard_map/ppermute | solution.py:875
  13.3 0.6 %shard_map.105.strip = f32[72,128]{1,0:T(8,128)S(1)} custom-call(f32[48,72,128]{2,1,0:T(8,128)S(1)} %pad.8.u.refs_0_, f32[15,72,128]{2,1,0:T(8,128)S(1)} %pad.9.shear.refs_1_), custom_call_target="tpu_custom_call" | custom-call | flops 1000 | bytes 1000 | tf_op jit(solution)/shard_map/pallas_call | solution.py:37
  13.9 0.5 copy-done.1
  15.1 0.5 collective-permute-done.surface
  15.7 2.4 %collective-permute-start.3 = (f32[264,128]{1,0:T(8,128)S(1)}, f32[264,128]{1,0:T(8,128)S(1)}, u32[]{:S(2)}, u32[]{:S(2)}) collective-permute-start(f32[264,128]{1,0:T(8,128)S(1)} %shard_map.106.sent.old_sent), channel_id=1, source_target_pairs={{0,15},{1,2},{2,1},{3,4},{4,3},{5,6},{6,5},{7,8},{8,7},{9,10},{10,... | collective-permute-start | bytes 405512 | tf_op jit(solution)/shard_map/ppermute | solution.py:881
  18.3 2.8 %shard_map.107.low = f32[30,64,128]{2,1,0:T(8,128)S(1)} custom-call(f32[48,72,128]{2,1,0:T(8,128)S(1)} %pad.8.u.refs_0_, f32[15,72,128]{2,1,0:T(8,128)S(1)} %pad.9.shear.refs_1_), custom_call_target="tpu_custom_call" | custom-call | flops 1000 | bytes 1000 | tf_op jit(solution)/shard_map/pallas_call | solution.py:37
  21.1 1.6 %collective-permute-done.3.across.old_across = f32[264,128]{1,0:T(8,128)S(1)} collective-permute-done((f32[264,128]{1,0:T(8,128)S(1)}, f32[264,128]{1,0:T(8,128)S(1)}, u32[]{:S(2)}, u32[]{:S(2)}) %collective-permute-start.3) | collective-permute-done | bytes 135200 | tf_op jit(solution)/shard_map/ppermute | solution.py:881
  22.7 1.5 %shard_map.108 = (f32[512,128]{1,0:T(8,128)S(1)}, f32[216,128]{1,0:T(8,128)S(1)}, f32[192,128]{1,0:T(8,128)S(1)}, f32[64,128]{1,0:T(8,128)S(1)}, f32[96,128]{1,0:T(8,128)S(1)}) custom-call(f32[192,128]{1,0:T(8,128)S(1)} %get-tuple-element.49.surface, f32[264,128]{1,0:T(8,128)S(1)} %shard_map.106.sent.old_sent, ...), custom_call_target="tpu_custom_call" | custom-call | flops 1000 | bytes 1000 | tf_op jit(solution)/shard_map/pallas_call | solution.py:37
  24.2 2.2 %collective-permute-start.5 = (f32[216,128]{1,0:T(8,128)S(1)}, f32[216,128]{1,0:T(8,128)S(1)}, u32[]{:S(2)}, u32[]{:S(2)}) collective-permute-start(f32[216,128]{1,0:T(8,128)S(1)} %get-tuple-element.59.surface.partial.refs_3_), channel_id=1, source_target_pairs={{0,8},{1,9},{2,10},{3,11},{4,12},{5,13},{6,14},{7,15},{8,0},{9,1},... | collective-permute-start | bytes 331784 | tf_op jit(solution)/shard_map/ppermute | solution.py:875
  26.4 0.7 %shard_map.109 = (f32[200,128]{1,0:T(8,128)S(1)}, f32[208,128]{1,0:T(8,128)S(1)}) custom-call(f32[512,128]{1,0:T(8,128)S(1)} %get-tuple-element.60.lhs, bf16[8192,128]{1,0:T(8,128)(2,1)S(1)} %bitcast.10, s32[64,1]{1,0:T(8,128)S(1)} %select_add_fusion.place), custom_call_target="tpu_custom_call" | custom-call | flops 1000 | bytes 1000 | tf_op jit(solution)/shard_map/pallas_call | solution.py:37
  27.1 0.8 %collective-permute-start.6 = (f32[208,128]{1,0:T(8,128)S(1)}, f32[208,128]{1,0:T(8,128)S(1)}, u32[]{:S(2)}, u32[]{:S(2)}) collective-permute-start(f32[208,128]{1,0:T(8,128)S(1)} %get-tuple-element.69), channel_id=1, source_target_pairs={{0,15},{1,2},{2,1},{3,4},{4,3},{5,6},{6,5},{7,8},{8,7},{9,10},{10,... | collective-permute-start | bytes 319496 | tf_op jit(solution)/shard_map/ppermute | solution.py:881
  27.9 0.4 collective-permute-start.7
  28.3 2.1 %shard_map.110.high = f32[18,64,128]{2,1,0:T(8,128)S(1)} custom-call(f32[48,72,128]{2,1,0:T(8,128)S(1)} %pad.8.u.refs_0_, f32[15,72,128]{2,1,0:T(8,128)S(1)} %pad.9.shear.refs_1_), custom_call_target="tpu_custom_call" | custom-call | flops 1000 | bytes 1000 | tf_op jit(solution)/shard_map/pallas_call | solution.py:37
  30.4 0.9 %shard_map.111 = (f32[48,72,128]{2,1,0:T(8,128)S(1)}, f32[48,64,128]{2,1,0:T(8,128)S(1)}, f32[72,128]{1,0:T(8,128)S(1)}, f32[64,128]{1,0:T(8,128)S(1)}, f32[64,128]{1,0:T(8,128)S(1)}) custom-call(f32[48,72,128]{2,1,0:T(8,128)S(1)} %pad.8.u.refs_0_, f32[48,64,128]{2,1,0:T(8,128)S(1)} %bitcast.12, f32[30,64,128]{2,1,0:T(8,128)S(1)} %shard_map.107.low, ...), custom_call_target="tpu_custom_call" | custom-call | flops 1000 | bytes 1000 | tf_op jit(solution)/shard_map/pallas_call | solution.py:37
  31.3 2.1 %collective-permute-done.6.left = f32[208,128]{1,0:T(8,128)S(1)} collective-permute-done((f32[208,128]{1,0:T(8,128)S(1)}, f32[208,128]{1,0:T(8,128)S(1)}, u32[]{:S(2)}, u32[]{:S(2)}) %collective-permute-start.6) | collective-permute-done | bytes 106528 | tf_op jit(solution)/shard_map/ppermute | solution.py:881
  33.4 0.2 shard_map.112
  33.7 1.2 %collective-permute-start.8 = (f32[208,128]{1,0:T(8,128)S(1)}, f32[208,128]{1,0:T(8,128)S(1)}, u32[]{:S(2)}, u32[]{:S(2)}) collective-permute-start(f32[208,128]{1,0:T(8,128)S(1)} %get-tuple-element.70), channel_id=1, source_target_pairs={{0,8},{1,9},{2,10},{3,11},{4,12},{5,13},{6,14},{7,15},{8,0},{9,1},... | collective-permute-start | bytes 319496 | tf_op jit(solution)/shard_map/ppermute | solution.py:875
  34.8 0.6 collective-permute-start.9
  35.4 1.1 %collective-permute-start.11 = (f32[64,128]{1,0:T(8,128)S(1)}, f32[64,128]{1,0:T(8,128)S(1)}, u32[]{:S(2)}, u32[]{:S(2)}) collective-permute-start(f32[64,128]{1,0:T(8,128)S(1)} %get-tuple-element.78), channel_id=1, source_target_pairs={{0,16},{16,32},{32,48},{48,64},{64,80},{80,96},{96,112},{112,0},{1... | collective-permute-start | bytes 98312 | tf_op jit(solution)/shard_map/ppermute | solution.py:875
  36.5 4.6 %collective-permute-start.12 = (f32[64,128]{1,0:T(8,128)S(1)}, f32[64,128]{1,0:T(8,128)S(1)}, u32[]{:S(2)}, u32[]{:S(2)}) collective-permute-start(f32[64,128]{1,0:T(8,128)S(1)} %get-tuple-element.79), channel_id=1, source_target_pairs={{0,112},{16,0},{32,16},{48,32},{64,48},{80,64},{96,80},{112,96},{1... | collective-permute-start | bytes 98312 | tf_op jit(solution)/shard_map/ppermute | solution.py:875
  41.1 2.0 %shard_map.113 = (f32[200,128]{1,0:T(8,128)S(1)}, f32[64,128]{1,0:T(8,128)S(1)}, f32[192,128]{1,0:T(8,128)S(1)}) custom-call(f32[216,128]{1,0:T(8,128)S(1)} %get-tuple-element.59.surface.partial.refs_3_, f32[208,128]{1,0:T(8,128)S(1)} %collective-permute-done.8.comb.comb_own, f32[192,128]{1,0:T(8,128)S(1)} %get-tuple-element.71.center, ...), custom_call_target="tpu_custom_call" | custom-call | flops 1000 | bytes 1000 | tf_op jit(solution)/shard_map/pallas_call | solution.py:37
  43.3 2.8 %collective-permute-start.13 = (f32[280,128]{1,0:T(8,128)S(1)}, f32[280,128]{1,0:T(8,128)S(1)}, u32[]{:S(2)}, u32[]{:S(2)}) collective-permute-start(f32[280,128]{1,0:T(8,128)S(1)} %get-tuple-element.86), channel_id=1, source_target_pairs={{0,15},{1,2},{2,1},{3,4},{4,3},{5,6},{6,5},{7,8},{8,7},{9,10},{10,... | collective-permute-start | bytes 430088 | tf_op jit(solution)/shard_map/ppermute | solution.py:881
  46.1 3.7 %shard_map.116.v_high = f32[39,64,128]{2,1,0:T(8,128)S(1)} custom-call(f32[48,72,128]{2,1,0:T(8,128)S(1)} %get-tuple-element.88.refs_0_.u, f32[15,72,128]{2,1,0:T(8,128)S(1)} %pad.9.shear.refs_1_, f32[48,64,128]{2,1,0:T(8,128)S(1)} %get-tuple-element.84.refs_2_.old_v, f32[216,128]{1,0:T(8,128)S(1)} %get-tuple-element.59.surface.partial.refs_3_), custom_call_target="tpu_custom_call" | custom-call | flops 1000 | bytes 1000 | tf_op jit(solution)/shard_map/pallas_call | solution.py:37
  49.8 1.6 %collective-permute-done.13.across = f32[280,128]{1,0:T(8,128)S(1)} collective-permute-done((f32[280,128]{1,0:T(8,128)S(1)}, f32[280,128]{1,0:T(8,128)S(1)}, u32[]{:S(2)}, u32[]{:S(2)}) %collective-permute-start.13) | collective-permute-done | bytes 143392 | tf_op jit(solution)/shard_map/ppermute | solution.py:881
  51.6 1.5 %collective-permute-start.15 = (f32[200,128]{1,0:T(8,128)S(1)}, f32[200,128]{1,0:T(8,128)S(1)}, u32[]{:S(2)}, u32[]{:S(2)}) collective-permute-start(f32[200,128]{1,0:T(8,128)S(1)} %shard_map.117), channel_id=1, source_target_pairs={{0,8},{1,9},{2,10},{3,11},{4,12},{5,13},{6,14},{7,15},{8,0},{9,1},... | collective-permute-start | bytes 307208 | tf_op jit(solution)/shard_map/ppermute | solution.py:875
  53.2 3.9 %shard_map.118 = (f32[48,64,128]{2,1,0:T(8,128)}, f32[48,64,128]{2,1,0:T(8,128)}, f32[9,64,128]{2,1,0:T(8,128)S(1)}) custom-call(f32[48,72,128]{2,1,0:T(8,128)S(1)} %get-tuple-element.88.refs_0_.u, f32[15,72,128]{2,1,0:T(8,128)S(1)} %pad.9.shear.refs_1_, f32[48,64,128]{2,1,0:T(8,128)S(1)} %get-tuple-element.84.refs_2_.old_v, ...), custom_call_target="tpu_custom_call" | custom-call | flops 1000 | bytes 1000 | tf_op jit(solution)/shard_map/pallas_call | solution.py:37
  57.1 0.8 %collective-permute-done.15.comb = f32[200,128]{1,0:T(8,128)S(1)} collective-permute-done((f32[200,128]{1,0:T(8,128)S(1)}, f32[200,128]{1,0:T(8,128)S(1)}, u32[]{:S(2)}, u32[]{:S(2)}) %collective-permute-start.15) | collective-permute-done | bytes 102432 | tf_op jit(solution)/shard_map/ppermute | solution.py:875
  57.9 1.5 %shard_map.119 = (f32[48,64,128]{2,1,0:T(8,128)}, f32[48,64,128]{2,1,0:T(8,128)}) custom-call(f32[48,72,128]{2,1,0:T(8,128)S(1)} %get-tuple-element.88.refs_0_.u, f32[9,64,128]{2,1,0:T(8,128)S(1)} %get-tuple-element.90.v_low, f32[192,128]{1,0:T(8,128)S(1)} %get-tuple-element.91.slave, ...), custom_call_target="tpu_custom_call", output_to_operand_aliasing={{0}: (17, {}), {1}: (18, {})} | custom-call | flops 1000 | bytes 1000 | tf_op jit(solution)/shard_map/pallas_call | solution.py:853
  (39 shorter events, 1.0 us)
Async XLA Ops:
  3.3 9.7 %copy-start.5 = (f32[3,16,64,128]{3,2,1,0:T(8,128)S(1)}, f32[3,16,64,128]{3,2,1,0:T(8,128)}, u32[]{:S(2)}) copy-start(f32[3,16,64,128]{3,2,1,0:T(8,128)} %param.10) | copy-start | bytes 4718596
  3.3 11.7 %collective-permute-start.1 = (f32[64,128]{1,0:T(8,128)S(1)}, f32[64,128]{1,0:T(8,128)S(1)}, u32[]{:S(2)}, u32[]{:S(2)}) collective-permute-start(f32[64,128]{1,0:T(8,128)S(1)} %get-tuple-element.50.last.old_last), channel_id=1, source_target_pairs={{0,16},{16,32},{32,48},{48,64},{64,80},{80,96},{96,112},{112,0},{1... | collective-permute-start | bytes 98312 | tf_op jit(solution)/shard_map/ppermute | solution.py:875
  6.5 8.6 %collective-permute-start.2 = (f32[64,128]{1,0:T(8,128)S(1)}, f32[64,128]{1,0:T(8,128)S(1)}, u32[]{:S(2)}, u32[]{:S(2)}) collective-permute-start(f32[64,128]{1,0:T(8,128)S(1)} %get-tuple-element.51.first), channel_id=1, source_target_pairs={{0,112},{16,0},{32,16},{48,32},{64,48},{80,64},{96,80},{112,96},{1... | collective-permute-start | bytes 98312 | tf_op jit(solution)/shard_map/ppermute | solution.py:875
  9.0 6.6 %collective-permute-start = (f32[192,128]{1,0:T(8,128)S(1)}, f32[192,128]{1,0:T(8,128)S(1)}, u32[]{:S(2)}, u32[]{:S(2)}) collective-permute-start(f32[192,128]{1,0:T(8,128)S(1)} %get-tuple-element.49.surface), channel_id=1, source_target_pairs={{0,8},{1,9},{2,10},{3,11},{4,12},{5,13},{6,14},{7,15},{8,0},{9,1},... | collective-permute-start | bytes 294920 | tf_op jit(solution)/shard_map/ppermute | solution.py:875
  13.2 1.1 %copy-start.1 = (f32[3,16,64,128]{3,2,1,0:T(8,128)}, f32[3,16,64,128]{3,2,1,0:T(8,128)S(1)}, u32[]{:S(2)}) copy-start(f32[3,16,64,128]{3,2,1,0:T(8,128)S(1)} %broadcast_multiply_fusion) | copy-start | bytes 4718596
  13.3 4.9 %copy-start.6 = (s32[64,1]{0,1:T(1,128)S(1)}, s32[64,1]{0,1:T(1,128)}, u32[]{:S(2)}) copy-start(s32[64,1]{0,1:T(1,128)} %param.16) | copy-start | bytes 772
  13.3 4.9 %copy-start.7 = (s32[64,1]{0,1:T(1,128)S(1)}, s32[64,1]{0,1:T(1,128)}, u32[]{:S(2)}) copy-start(s32[64,1]{0,1:T(1,128)} %param.15) | copy-start | bytes 772
  15.7 7.0 %collective-permute-start.3 = (f32[264,128]{1,0:T(8,128)S(1)}, f32[264,128]{1,0:T(8,128)S(1)}, u32[]{:S(2)}, u32[]{:S(2)}) collective-permute-start(f32[264,128]{1,0:T(8,128)S(1)} %shard_map.106.sent.old_sent), channel_id=1, source_target_pairs={{0,15},{1,2},{2,1},{3,4},{4,3},{5,6},{6,5},{7,8},{8,7},{9,10},{10,... | collective-permute-start | bytes 405512 | tf_op jit(solution)/shard_map/ppermute | solution.py:881
  18.1 4.6 %collective-permute-start.4 = (f32[264,128]{1,0:T(8,128)S(1)}, f32[264,128]{1,0:T(8,128)S(1)}, u32[]{:S(2)}, u32[]{:S(2)}) collective-permute-start(f32[264,128]{1,0:T(8,128)S(1)} %shard_map.106.sent.old_sent), channel_id=1, source_target_pairs={{0,1},{1,0},{2,3},{3,2},{4,5},{5,4},{6,7},{7,6},{8,9},{9,8},{10,11... | collective-permute-start | bytes 405512 | tf_op jit(solution)/shard_map/ppermute | solution.py:881
  18.2 4.5 %copy-start = (bf16[64,1,128,128]{3,2,1,0:T(8,128)(2,1)S(1)}, bf16[64,1,128,128]{3,2,1,0:T(8,128)(2,1)}, u32[]{:S(2)}) copy-start(bf16[64,1,128,128]{3,2,1,0:T(8,128)(2,1)} %param.14) | copy-start | bytes 6291460
  18.2 4.5 %copy-start.3 = (f32[3,64,128]{2,1,0:T(8,128)S(1)}, f32[3,64,128]{2,1,0:T(8,128)}, u32[]{:S(2)}) copy-start(f32[3,64,128]{2,1,0:T(8,128)} %param.12) | copy-start | bytes 294916
  18.3 4.5 %copy-start.4 = (f32[64,128]{1,0:T(8,128)S(1)}, f32[64,128]{1,0:T(8,128)}, u32[]{:S(2)}) copy-start(f32[64,128]{1,0:T(8,128)} %gap.3) | copy-start | bytes 98308
  24.2 9.2 %collective-permute-start.5 = (f32[216,128]{1,0:T(8,128)S(1)}, f32[216,128]{1,0:T(8,128)S(1)}, u32[]{:S(2)}, u32[]{:S(2)}) collective-permute-start(f32[216,128]{1,0:T(8,128)S(1)} %get-tuple-element.59.surface.partial.refs_3_), channel_id=1, source_target_pairs={{0,8},{1,9},{2,10},{3,11},{4,12},{5,13},{6,14},{7,15},{8,0},{9,1},... | collective-permute-start | bytes 331784 | tf_op jit(solution)/shard_map/ppermute | solution.py:875
  27.1 3.3 %copy-start.2 = (f32[3,16,64,128]{3,2,1,0:T(8,128)S(1)}, f32[3,16,64,128]{3,2,1,0:T(8,128)}, u32[]{:S(2)}) copy-start(f32[3,16,64,128]{3,2,1,0:T(8,128)} %copy-done.1) | copy-start | bytes 4718596
  27.1 6.3 %collective-permute-start.6 = (f32[208,128]{1,0:T(8,128)S(1)}, f32[208,128]{1,0:T(8,128)S(1)}, u32[]{:S(2)}, u32[]{:S(2)}) collective-permute-start(f32[208,128]{1,0:T(8,128)S(1)} %get-tuple-element.69), channel_id=1, source_target_pairs={{0,15},{1,2},{2,1},{3,4},{4,3},{5,6},{6,5},{7,8},{8,7},{9,10},{10,... | collective-permute-start | bytes 319496 | tf_op jit(solution)/shard_map/ppermute | solution.py:881
  27.9 3.4 %collective-permute-start.7 = (f32[200,128]{1,0:T(8,128)S(1)}, f32[200,128]{1,0:T(8,128)S(1)}, u32[]{:S(2)}, u32[]{:S(2)}) collective-permute-start(f32[200,128]{1,0:T(8,128)S(1)} %get-tuple-element.68.own), channel_id=1, source_target_pairs={{0,1},{1,0},{2,3},{3,2},{4,5},{5,4},{6,7},{7,6},{8,9},{9,8},{10,11... | collective-permute-start | bytes 307208 | tf_op jit(solution)/shard_map/ppermute | solution.py:881
  33.7 7.5 %collective-permute-start.8 = (f32[208,128]{1,0:T(8,128)S(1)}, f32[208,128]{1,0:T(8,128)S(1)}, u32[]{:S(2)}, u32[]{:S(2)}) collective-permute-start(f32[208,128]{1,0:T(8,128)S(1)} %get-tuple-element.70), channel_id=1, source_target_pairs={{0,8},{1,9},{2,10},{3,11},{4,12},{5,13},{6,14},{7,15},{8,0},{9,1},... | collective-permute-start | bytes 319496 | tf_op jit(solution)/shard_map/ppermute | solution.py:875
  34.8 6.3 %collective-permute-start.9 = (f32[200,128]{1,0:T(8,128)S(1)}, f32[200,128]{1,0:T(8,128)S(1)}, u32[]{:S(2)}, u32[]{:S(2)}) collective-permute-start(f32[200,128]{1,0:T(8,128)S(1)} %get-tuple-element.72), channel_id=1, source_target_pairs={{0,15},{1,2},{2,1},{3,4},{4,3},{5,6},{6,5},{7,8},{8,7},{9,10},{10,... | collective-permute-start | bytes 307208 | tf_op jit(solution)/shard_map/ppermute | solution.py:881
  35.4 5.7 %collective-permute-start.10 = (f32[192,128]{1,0:T(8,128)S(1)}, f32[192,128]{1,0:T(8,128)S(1)}, u32[]{:S(2)}, u32[]{:S(2)}) collective-permute-start(f32[192,128]{1,0:T(8,128)S(1)} %get-tuple-element.71.center), channel_id=1, source_target_pairs={{0,1},{1,0},{2,3},{3,2},{4,5},{5,4},{6,7},{7,6},{8,9},{9,8},{10,11... | collective-permute-start | bytes 294920 | tf_op jit(solution)/shard_map/ppermute | solution.py:881
  35.4 7.7 %collective-permute-start.11 = (f32[64,128]{1,0:T(8,128)S(1)}, f32[64,128]{1,0:T(8,128)S(1)}, u32[]{:S(2)}, u32[]{:S(2)}) collective-permute-start(f32[64,128]{1,0:T(8,128)S(1)} %get-tuple-element.78), channel_id=1, source_target_pairs={{0,16},{16,32},{32,48},{48,64},{64,80},{80,96},{96,112},{112,0},{1... | collective-permute-start | bytes 98312 | tf_op jit(solution)/shard_map/ppermute | solution.py:875
  36.5 6.6 %collective-permute-start.12 = (f32[64,128]{1,0:T(8,128)S(1)}, f32[64,128]{1,0:T(8,128)S(1)}, u32[]{:S(2)}, u32[]{:S(2)}) collective-permute-start(f32[64,128]{1,0:T(8,128)S(1)} %get-tuple-element.79), channel_id=1, source_target_pairs={{0,112},{16,0},{32,16},{48,32},{64,48},{80,64},{96,80},{112,96},{1... | collective-permute-start | bytes 98312 | tf_op jit(solution)/shard_map/ppermute | solution.py:875
  43.3 8.1 %collective-permute-start.13 = (f32[280,128]{1,0:T(8,128)S(1)}, f32[280,128]{1,0:T(8,128)S(1)}, u32[]{:S(2)}, u32[]{:S(2)}) collective-permute-start(f32[280,128]{1,0:T(8,128)S(1)} %get-tuple-element.86), channel_id=1, source_target_pairs={{0,15},{1,2},{2,1},{3,4},{4,3},{5,6},{6,5},{7,8},{8,7},{9,10},{10,... | collective-permute-start | bytes 430088 | tf_op jit(solution)/shard_map/ppermute | solution.py:881
  46.1 3.7 %collective-permute-start.14 = (f32[272,128]{1,0:T(8,128)S(1)}, f32[272,128]{1,0:T(8,128)S(1)}, u32[]{:S(2)}, u32[]{:S(2)}) collective-permute-start(f32[272,128]{1,0:T(8,128)S(1)} %get-tuple-element.85.own.sent), channel_id=1, source_target_pairs={{0,1},{1,0},{2,3},{3,2},{4,5},{5,4},{6,7},{7,6},{8,9},{9,8},{10,11... | collective-permute-start | bytes 417800 | tf_op jit(solution)/shard_map/ppermute | solution.py:881
  51.6 6.2 %collective-permute-start.15 = (f32[200,128]{1,0:T(8,128)S(1)}, f32[200,128]{1,0:T(8,128)S(1)}, u32[]{:S(2)}, u32[]{:S(2)}) collective-permute-start(f32[200,128]{1,0:T(8,128)S(1)} %shard_map.117), channel_id=1, source_target_pairs={{0,8},{1,9},{2,10},{3,11},{4,12},{5,13},{6,14},{7,15},{8,0},{9,1},... | collective-permute-start | bytes 307208 | tf_op jit(solution)/shard_map/ppermute | solution.py:875

commit v6 on v3

--- a/solution.py
+++ b/solution.py
@@ -155,7 +155,7 @@
     lax.fori_loop(0, ROWS_DEV // 8, chunk, 0)
 
 
-FIRST_LOW = 10
+FIRST_LOW = 11
 SECOND_LOW = 3
 
 

time: 59.5 us -> 59.5 us (level)
  no operation moved by 1% of the time
where the time goes in v6:
time: 59.5 us; the launch traced here: 59.1 us
  starting transfers between devices  27.2 us (46%)
  Pallas kernels  20.2 us (34%)
  waiting for transfers between devices  6.71 us (11%)
  local copies, waits for them, and re-layouts  3.26 us (5%)
  between operations  1.52 us (3%)
    ppermute x8, starting transfers between devices, moved(): return lax.ppermute(x, axis, [(i, (i + by) % count) for i in range(count)])  20.1 us
    pallas_call x15, Pallas kernels, call(): pl.pallas_call(kernel, out_shape=out_shape, in_specs=in_specs, out_specs=...  18.4 us
    ppermute x8, starting transfers between devices, exchanged(): return lax.ppermute(x, 'gy', [(i, j % count) for i, j in pairs])  7.12 us
    ppermute x8, waiting for transfers between devices, exchanged(): return lax.ppermute(x, 'gy', [(i, j % count) for i, j in pairs])  4.5 us
    ppermute x8, waiting for transfers between devices, moved(): return lax.ppermute(x, axis, [(i, (i + by) % count) for i in range(count)])  2.21 us
    pallas_call x1, Pallas kernels, last_surface(): pl.pallas_call(last_surface_kernel, out_shape=(planes(PLANES), planes(PLA...  1.75 us
    pad x1, local copies, waits for them, and re-layouts, local(): jnp.pad(displacement.reshape(PLANES, ROWS_DEV, BLOCK), ((0, 0), (0, STRIP...  1.54 us
  transfers between devices with their start and end apart: 16, of which 5 were waited for; matrix products, arithmetic and copies ran while one was open for 1% of the time, Pallas kernels for 27%

profile of v6, /device:TPU:0, one launch (start us, length us, event | category | flops | bytes accessed | tf_op | source)
XLA Modules:
  0.0 59.1 jit_solution(16975133464801247131)
XLA Ops:
  0.6 1.1 %pad.9.shear.refs_1_ = f32[15,72,128]{2,1,0:T(8,128)S(1)} pad(f32[15,64,128]{2,1,0:T(8,128)} %param.11, f32[]{:T(128)} %constant.1.clone.1), padding=0_0x0_8x0_0 | pad | bytes 1044484 | tf_op jit(solution)/shard_map/jit(_pad)/pad | solution.py:861
  1.7 1.5 %pad.8.u.refs_0_ = f32[48,72,128]{2,1,0:T(8,128)S(1)} pad(f32[48,64,128]{2,1,0:T(8,128)} %bitcast.16, f32[]{:T(128)} %constant.1.clone.1), padding=0_0x0_8x0_0 | pad | bytes 3342340 | tf_op jit(solution)/shard_map/jit(_pad)/pad | solution.py:858
  3.3 3.2 %collective-permute-start.1 = (f32[64,128]{1,0:T(8,128)S(1)}, f32[64,128]{1,0:T(8,128)S(1)}, u32[]{:S(2)}, u32[]{:S(2)}) collective-permute-start(f32[64,128]{1,0:T(8,128)S(1)} %get-tuple-element.45.last.old_last), channel_id=1, source_target_pairs={{0,16},{16,32},{32,48},{48,64},{64,80},{80,96},{96,112},{112,0},{1... | collective-permute-start | bytes 98312 | tf_op jit(solution)/shard_map/ppermute | solution.py:844
  6.5 2.5 %collective-permute-start.2 = (f32[64,128]{1,0:T(8,128)S(1)}, f32[64,128]{1,0:T(8,128)S(1)}, u32[]{:S(2)}, u32[]{:S(2)}) collective-permute-start(f32[64,128]{1,0:T(8,128)S(1)} %get-tuple-element.46.first), channel_id=1, source_target_pairs={{0,112},{16,0},{32,16},{48,32},{64,48},{80,64},{96,80},{112,96},{1... | collective-permute-start | bytes 98312 | tf_op jit(solution)/shard_map/ppermute | solution.py:844
  9.0 4.0 %collective-permute-start = (f32[192,128]{1,0:T(8,128)S(1)}, f32[192,128]{1,0:T(8,128)S(1)}, u32[]{:S(2)}, u32[]{:S(2)}) collective-permute-start(f32[192,128]{1,0:T(8,128)S(1)} %get-tuple-element.44.surface), channel_id=1, source_target_pairs={{0,8},{1,9},{2,10},{3,11},{4,12},{5,13},{6,14},{7,15},{8,0},{9,1},... | collective-permute-start | bytes 294920 | tf_op jit(solution)/shard_map/ppermute | solution.py:844
  13.0 0.2 broadcast_multiply_fusion
  13.3 0.6 %shard_map.105.strip = f32[72,128]{1,0:T(8,128)S(1)} custom-call(f32[48,72,128]{2,1,0:T(8,128)S(1)} %pad.8.u.refs_0_, f32[15,72,128]{2,1,0:T(8,128)S(1)} %pad.9.shear.refs_1_), custom_call_target="tpu_custom_call" | custom-call | flops 1000 | bytes 1000 | tf_op jit(solution)/shard_map/pallas_call | solution.py:37
  13.9 0.5 copy-done.1
  15.1 0.5 collective-permute-done.surface
  15.7 2.4 %collective-permute-start.3 = (f32[264,128]{1,0:T(8,128)S(1)}, f32[264,128]{1,0:T(8,128)S(1)}, u32[]{:S(2)}, u32[]{:S(2)}) collective-permute-start(f32[264,128]{1,0:T(8,128)S(1)} %shard_map.106.sent.old_sent), channel_id=1, source_target_pairs={{0,15},{1,2},{2,1},{3,4},{4,3},{5,6},{6,5},{7,8},{8,7},{9,10},{10,... | collective-permute-start | bytes 405512 | tf_op jit(solution)/shard_map/ppermute | solution.py:850
  18.3 3.1 %shard_map.107.low = f32[33,64,128]{2,1,0:T(8,128)S(1)} custom-call(f32[48,72,128]{2,1,0:T(8,128)S(1)} %pad.8.u.refs_0_, f32[15,72,128]{2,1,0:T(8,128)S(1)} %pad.9.shear.refs_1_), custom_call_target="tpu_custom_call" | custom-call | flops 1000 | bytes 1000 | tf_op jit(solution)/shard_map/pallas_call | solution.py:37
  21.4 1.3 %collective-permute-done.3.across.old_across = f32[264,128]{1,0:T(8,128)S(1)} collective-permute-done((f32[264,128]{1,0:T(8,128)S(1)}, f32[264,128]{1,0:T(8,128)S(1)}, u32[]{:S(2)}, u32[]{:S(2)}) %collective-permute-start.3) | collective-permute-done | bytes 135200 | tf_op jit(solution)/shard_map/ppermute | solution.py:850
  22.7 1.5 %shard_map.108 = (f32[512,128]{1,0:T(8,128)S(1)}, f32[208,128]{1,0:T(8,128)S(1)}, f32[192,128]{1,0:T(8,128)S(1)}, f32[64,128]{1,0:T(8,128)S(1)}, f32[96,128]{1,0:T(8,128)S(1)}) custom-call(f32[192,128]{1,0:T(8,128)S(1)} %get-tuple-element.44.surface, f32[264,128]{1,0:T(8,128)S(1)} %shard_map.106.sent.old_sent, ...), custom_call_target="tpu_custom_call" | custom-call | flops 1000 | bytes 1000 | tf_op jit(solution)/shard_map/pallas_call | solution.py:37
  24.2 2.2 %collective-permute-start.5 = (f32[208,128]{1,0:T(8,128)S(1)}, f32[208,128]{1,0:T(8,128)S(1)}, u32[]{:S(2)}, u32[]{:S(2)}) collective-permute-start(f32[208,128]{1,0:T(8,128)S(1)} %get-tuple-element.54.surface.partial.refs_3_), channel_id=1, source_target_pairs={{0,8},{1,9},{2,10},{3,11},{4,12},{5,13},{6,14},{7,15},{8,0},{9,1},... | collective-permute-start | bytes 319496 | tf_op jit(solution)/shard_map/ppermute | solution.py:844
  26.4 0.7 %shard_map.109.own = f32[200,128]{1,0:T(8,128)S(1)} custom-call(f32[512,128]{1,0:T(8,128)S(1)} %get-tuple-element.55.lhs, bf16[8192,128]{1,0:T(8,128)(2,1)S(1)} %bitcast.10, s32[64,1]{1,0:T(8,128)S(1)} %select_add_fusion.place), custom_call_target="tpu_custom_call" | custom-call | flops 1000 | bytes 1000 | tf_op jit(solution)/shard_map/pallas_call | solution.py:37
  27.1 0.9 %collective-permute-start.6 = (f32[200,128]{1,0:T(8,128)S(1)}, f32[200,128]{1,0:T(8,128)S(1)}, u32[]{:S(2)}, u32[]{:S(2)}) collective-permute-start(f32[200,128]{1,0:T(8,128)S(1)} %shard_map.109.own), channel_id=1, source_target_pairs={{0,15},{1,2},{2,1},{3,4},{4,3},{5,6},{6,5},{7,8},{8,7},{9,10},{10,... | collective-permute-start | bytes 307208 | tf_op jit(solution)/shard_map/ppermute | solution.py:850
  28.0 0.3 collective-permute-start.7
  28.3 2.0 %shard_map.110.high = f32[15,64,128]{2,1,0:T(8,128)S(1)} custom-call(f32[48,72,128]{2,1,0:T(8,128)S(1)} %pad.8.u.refs_0_, f32[15,72,128]{2,1,0:T(8,128)S(1)} %pad.9.shear.refs_1_), custom_call_target="tpu_custom_call" | custom-call | flops 1000 | bytes 1000 | tf_op jit(solution)/shard_map/pallas_call | solution.py:37
  30.3 0.9 %shard_map.111 = (f32[48,72,128]{2,1,0:T(8,128)S(1)}, f32[48,64,128]{2,1,0:T(8,128)S(1)}, f32[72,128]{1,0:T(8,128)S(1)}, f32[64,128]{1,0:T(8,128)S(1)}, f32[64,128]{1,0:T(8,128)S(1)}) custom-call(f32[48,72,128]{2,1,0:T(8,128)S(1)} %pad.8.u.refs_0_, f32[48,64,128]{2,1,0:T(8,128)S(1)} %bitcast.12, f32[33,64,128]{2,1,0:T(8,128)S(1)} %shard_map.107.low, ...), custom_call_target="tpu_custom_call" | custom-call | flops 1000 | bytes 1000 | tf_op jit(solution)/shard_map/pallas_call | solution.py:37
  31.2 2.1 %collective-permute-done.6.left = f32[200,128]{1,0:T(8,128)S(1)} collective-permute-done((f32[200,128]{1,0:T(8,128)S(1)}, f32[200,128]{1,0:T(8,128)S(1)}, u32[]{:S(2)}, u32[]{:S(2)}) %collective-permute-start.6) | collective-permute-done | bytes 102432 | tf_op jit(solution)/shard_map/ppermute | solution.py:850
  33.7 1.1 %collective-permute-start.8 = (f32[192,128]{1,0:T(8,128)S(1)}, f32[192,128]{1,0:T(8,128)S(1)}, u32[]{:S(2)}, u32[]{:S(2)}) collective-permute-start(f32[192,128]{1,0:T(8,128)S(1)} %get-tuple-element.63), channel_id=1, source_target_pairs={{0,8},{1,9},{2,10},{3,11},{4,12},{5,13},{6,14},{7,15},{8,0},{9,1},... | collective-permute-start | bytes 294920 | tf_op jit(solution)/shard_map/ppermute | solution.py:844
  34.8 1.5 %collective-permute-start.9 = (f32[192,128]{1,0:T(8,128)S(1)}, f32[192,128]{1,0:T(8,128)S(1)}, u32[]{:S(2)}, u32[]{:S(2)}) collective-permute-start(f32[192,128]{1,0:T(8,128)S(1)} %get-tuple-element.64.center), channel_id=1, source_target_pairs={{0,15},{1,2},{2,1},{3,4},{4,3},{5,6},{6,5},{7,8},{8,7},{9,10},{10,... | collective-permute-start | bytes 294920 | tf_op jit(solution)/shard_map/ppermute | solution.py:850
  36.3 0.7 %collective-permute-start.11 = (f32[64,128]{1,0:T(8,128)S(1)}, f32[64,128]{1,0:T(8,128)S(1)}, u32[]{:S(2)}, u32[]{:S(2)}) collective-permute-start(f32[64,128]{1,0:T(8,128)S(1)} %get-tuple-element.70), channel_id=1, source_target_pairs={{0,16},{16,32},{32,48},{48,64},{64,80},{80,96},{96,112},{112,0},{1... | collective-permute-start | bytes 98312 | tf_op jit(solution)/shard_map/ppermute | solution.py:844
  37.0 5.0 %collective-permute-start.12 = (f32[64,128]{1,0:T(8,128)S(1)}, f32[64,128]{1,0:T(8,128)S(1)}, u32[]{:S(2)}, u32[]{:S(2)}) collective-permute-start(f32[64,128]{1,0:T(8,128)S(1)} %get-tuple-element.71), channel_id=1, source_target_pairs={{0,112},{16,0},{32,16},{48,32},{64,48},{80,64},{96,80},{112,96},{1... | collective-permute-start | bytes 98312 | tf_op jit(solution)/shard_map/ppermute | solution.py:844
  42.1 2.0 %shard_map.113 = (f32[200,128]{1,0:T(8,128)S(1)}, f32[64,128]{1,0:T(8,128)S(1)}, f32[192,128]{1,0:T(8,128)S(1)}) custom-call(f32[208,128]{1,0:T(8,128)S(1)} %get-tuple-element.54.surface.partial.refs_3_, f32[192,128]{1,0:T(8,128)S(1)} %collective-permute-done.8.comb.comb_own, f32[192,128]{1,0:T(8,128)S(1)} %get-tuple-element.64.center, ...), custom_call_target="tpu_custom_call" | custom-call | flops 1000 | bytes 1000 | tf_op jit(solution)/shard_map/pallas_call | solution.py:37
  44.2 1.9 %collective-permute-start.13 = (f32[272,128]{1,0:T(8,128)S(1)}, f32[272,128]{1,0:T(8,128)S(1)}, u32[]{:S(2)}, u32[]{:S(2)}) collective-permute-start(f32[272,128]{1,0:T(8,128)S(1)} %shard_map.115.own.sent), channel_id=1, source_target_pairs={{0,15},{1,2},{2,1},{3,4},{4,3},{5,6},{6,5},{7,8},{8,7},{9,10},{10,... | collective-permute-start | bytes 417800 | tf_op jit(solution)/shard_map/ppermute | solution.py:850
  46.1 3.7 %shard_map.116.v_high = f32[39,64,128]{2,1,0:T(8,128)S(1)} custom-call(f32[48,72,128]{2,1,0:T(8,128)S(1)} %get-tuple-element.78.refs_0_.u, f32[15,72,128]{2,1,0:T(8,128)S(1)} %pad.9.shear.refs_1_, f32[48,64,128]{2,1,0:T(8,128)S(1)} %get-tuple-element.75.refs_2_.old_v, f32[208,128]{1,0:T(8,128)S(1)} %get-tuple-element.54.surface.partial.refs_3_), custom_call_target="tpu_custom_call" | custom-call | flops 1000 | bytes 1000 | tf_op jit(solution)/shard_map/pallas_call | solution.py:37
  49.8 1.1 %collective-permute-done.13.across = f32[272,128]{1,0:T(8,128)S(1)} collective-permute-done((f32[272,128]{1,0:T(8,128)S(1)}, f32[272,128]{1,0:T(8,128)S(1)}, u32[]{:S(2)}, u32[]{:S(2)}) %collective-permute-start.13) | collective-permute-done | bytes 139296 | tf_op jit(solution)/shard_map/ppermute | solution.py:850
  51.1 1.4 %collective-permute-start.15 = (f32[200,128]{1,0:T(8,128)S(1)}, f32[200,128]{1,0:T(8,128)S(1)}, u32[]{:S(2)}, u32[]{:S(2)}) collective-permute-start(f32[200,128]{1,0:T(8,128)S(1)} %shard_map.117), channel_id=1, source_target_pairs={{0,8},{1,9},{2,10},{3,11},{4,12},{5,13},{6,14},{7,15},{8,0},{9,1},... | collective-permute-start | bytes 307208 | tf_op jit(solution)/shard_map/ppermute | solution.py:844
  52.6 3.1 %shard_map.118 = (f32[48,64,128]{2,1,0:T(8,128)}, f32[48,64,128]{2,1,0:T(8,128)}, f32[9,64,128]{2,1,0:T(8,128)S(1)}) custom-call(f32[48,72,128]{2,1,0:T(8,128)S(1)} %get-tuple-element.78.refs_0_.u, f32[15,72,128]{2,1,0:T(8,128)S(1)} %pad.9.shear.refs_1_, f32[48,64,128]{2,1,0:T(8,128)S(1)} %get-tuple-element.75.refs_2_.old_v, ...), custom_call_target="tpu_custom_call" | custom-call | flops 1000 | bytes 1000 | tf_op jit(solution)/shard_map/pallas_call | solution.py:37
  55.7 1.7 %collective-permute-done.15.comb = f32[200,128]{1,0:T(8,128)S(1)} collective-permute-done((f32[200,128]{1,0:T(8,128)S(1)}, f32[200,128]{1,0:T(8,128)S(1)}, u32[]{:S(2)}, u32[]{:S(2)}) %collective-permute-start.15) | collective-permute-done | bytes 102432 | tf_op jit(solution)/shard_map/ppermute | solution.py:844
  57.4 1.7 %shard_map.119 = (f32[48,64,128]{2,1,0:T(8,128)}, f32[48,64,128]{2,1,0:T(8,128)}) custom-call(f32[48,72,128]{2,1,0:T(8,128)S(1)} %get-tuple-element.78.refs_0_.u, f32[9,64,128]{2,1,0:T(8,128)S(1)} %get-tuple-element.80.v_low, f32[192,128]{1,0:T(8,128)S(1)} %get-tuple-element.81.slave, ...), custom_call_target="tpu_custom_call", output_to_operand_aliasing={{0}: (17, {}), {1}: (18, {})} | custom-call | flops 1000 | bytes 1000 | tf_op jit(solution)/shard_map/pallas_call | solution.py:822
  (39 shorter events, 1.0 us)
Async XLA Ops:
  3.3 9.7 %copy-start.5 = (f32[3,16,64,128]{3,2,1,0:T(8,128)S(1)}, f32[3,16,64,128]{3,2,1,0:T(8,128)}, u32[]{:S(2)}) copy-start(f32[3,16,64,128]{3,2,1,0:T(8,128)} %param.10) | copy-start | bytes 4718596
  3.3 11.7 %collective-permute-start.1 = (f32[64,128]{1,0:T(8,128)S(1)}, f32[64,128]{1,0:T(8,128)S(1)}, u32[]{:S(2)}, u32[]{:S(2)}) collective-permute-start(f32[64,128]{1,0:T(8,128)S(1)} %get-tuple-element.45.last.old_last), channel_id=1, source_target_pairs={{0,16},{16,32},{32,48},{48,64},{64,80},{80,96},{96,112},{112,0},{1... | collective-permute-start | bytes 98312 | tf_op jit(solution)/shard_map/ppermute | solution.py:844
  6.5 8.6 %collective-permute-start.2 = (f32[64,128]{1,0:T(8,128)S(1)}, f32[64,128]{1,0:T(8,128)S(1)}, u32[]{:S(2)}, u32[]{:S(2)}) collective-permute-start(f32[64,128]{1,0:T(8,128)S(1)} %get-tuple-element.46.first), channel_id=1, source_target_pairs={{0,112},{16,0},{32,16},{48,32},{64,48},{80,64},{96,80},{112,96},{1... | collective-permute-start | bytes 98312 | tf_op jit(solution)/shard_map/ppermute | solution.py:844
  9.0 6.6 %collective-permute-start = (f32[192,128]{1,0:T(8,128)S(1)}, f32[192,128]{1,0:T(8,128)S(1)}, u32[]{:S(2)}, u32[]{:S(2)}) collective-permute-start(f32[192,128]{1,0:T(8,128)S(1)} %get-tuple-element.44.surface), channel_id=1, source_target_pairs={{0,8},{1,9},{2,10},{3,11},{4,12},{5,13},{6,14},{7,15},{8,0},{9,1},... | collective-permute-start | bytes 294920 | tf_op jit(solution)/shard_map/ppermute | solution.py:844
  13.2 1.1 %copy-start.1 = (f32[3,16,64,128]{3,2,1,0:T(8,128)}, f32[3,16,64,128]{3,2,1,0:T(8,128)S(1)}, u32[]{:S(2)}) copy-start(f32[3,16,64,128]{3,2,1,0:T(8,128)S(1)} %broadcast_multiply_fusion) | copy-start | bytes 4718596
  13.3 4.9 %copy-start.6 = (s32[64,1]{0,1:T(1,128)S(1)}, s32[64,1]{0,1:T(1,128)}, u32[]{:S(2)}) copy-start(s32[64,1]{0,1:T(1,128)} %param.16) | copy-start | bytes 772
  13.3 4.9 %copy-start.7 = (s32[64,1]{0,1:T(1,128)S(1)}, s32[64,1]{0,1:T(1,128)}, u32[]{:S(2)}) copy-start(s32[64,1]{0,1:T(1,128)} %param.15) | copy-start | bytes 772
  15.7 7.0 %collective-permute-start.3 = (f32[264,128]{1,0:T(8,128)S(1)}, f32[264,128]{1,0:T(8,128)S(1)}, u32[]{:S(2)}, u32[]{:S(2)}) collective-permute-start(f32[264,128]{1,0:T(8,128)S(1)} %shard_map.106.sent.old_sent), channel_id=1, source_target_pairs={{0,15},{1,2},{2,1},{3,4},{4,3},{5,6},{6,5},{7,8},{8,7},{9,10},{10,... | collective-permute-start | bytes 405512 | tf_op jit(solution)/shard_map/ppermute | solution.py:850
  18.1 4.6 %collective-permute-start.4 = (f32[264,128]{1,0:T(8,128)S(1)}, f32[264,128]{1,0:T(8,128)S(1)}, u32[]{:S(2)}, u32[]{:S(2)}) collective-permute-start(f32[264,128]{1,0:T(8,128)S(1)} %shard_map.106.sent.old_sent), channel_id=1, source_target_pairs={{0,1},{1,0},{2,3},{3,2},{4,5},{5,4},{6,7},{7,6},{8,9},{9,8},{10,11... | collective-permute-start | bytes 405512 | tf_op jit(solution)/shard_map/ppermute | solution.py:850
  18.2 4.5 %copy-start = (bf16[64,1,128,128]{3,2,1,0:T(8,128)(2,1)S(1)}, bf16[64,1,128,128]{3,2,1,0:T(8,128)(2,1)}, u32[]{:S(2)}) copy-start(bf16[64,1,128,128]{3,2,1,0:T(8,128)(2,1)} %param.14) | copy-start | bytes 6291460
  18.2 4.5 %copy-start.3 = (f32[3,64,128]{2,1,0:T(8,128)S(1)}, f32[3,64,128]{2,1,0:T(8,128)}, u32[]{:S(2)}) copy-start(f32[3,64,128]{2,1,0:T(8,128)} %param.12) | copy-start | bytes 294916
  18.3 4.5 %copy-start.4 = (f32[64,128]{1,0:T(8,128)S(1)}, f32[64,128]{1,0:T(8,128)}, u32[]{:S(2)}) copy-start(f32[64,128]{1,0:T(8,128)} %gap.3) | copy-start | bytes 98308
  24.2 9.1 %collective-permute-start.5 = (f32[208,128]{1,0:T(8,128)S(1)}, f32[208,128]{1,0:T(8,128)S(1)}, u32[]{:S(2)}, u32[]{:S(2)}) collective-permute-start(f32[208,128]{1,0:T(8,128)S(1)} %get-tuple-element.54.surface.partial.refs_3_), channel_id=1, source_target_pairs={{0,8},{1,9},{2,10},{3,11},{4,12},{5,13},{6,14},{7,15},{8,0},{9,1},... | collective-permute-start | bytes 319496 | tf_op jit(solution)/shard_map/ppermute | solution.py:844
  27.1 3.2 %copy-start.2 = (f32[3,16,64,128]{3,2,1,0:T(8,128)S(1)}, f32[3,16,64,128]{3,2,1,0:T(8,128)}, u32[]{:S(2)}) copy-start(f32[3,16,64,128]{3,2,1,0:T(8,128)} %copy-done.1) | copy-start | bytes 4718596
  27.1 6.3 %collective-permute-start.6 = (f32[200,128]{1,0:T(8,128)S(1)}, f32[200,128]{1,0:T(8,128)S(1)}, u32[]{:S(2)}, u32[]{:S(2)}) collective-permute-start(f32[200,128]{1,0:T(8,128)S(1)} %shard_map.109.own), channel_id=1, source_target_pairs={{0,15},{1,2},{2,1},{3,4},{4,3},{5,6},{6,5},{7,8},{8,7},{9,10},{10,... | collective-permute-start | bytes 307208 | tf_op jit(solution)/shard_map/ppermute | solution.py:850
  28.0 5.4 %collective-permute-start.7 = (f32[200,128]{1,0:T(8,128)S(1)}, f32[200,128]{1,0:T(8,128)S(1)}, u32[]{:S(2)}, u32[]{:S(2)}) collective-permute-start(f32[200,128]{1,0:T(8,128)S(1)} %shard_map.109.own), channel_id=1, source_target_pairs={{0,1},{1,0},{2,3},{3,2},{4,5},{5,4},{6,7},{7,6},{8,9},{9,8},{10,11... | collective-permute-start | bytes 307208 | tf_op jit(solution)/shard_map/ppermute | solution.py:850
  33.6 8.4 %collective-permute-start.10 = (f32[192,128]{1,0:T(8,128)S(1)}, f32[192,128]{1,0:T(8,128)S(1)}, u32[]{:S(2)}, u32[]{:S(2)}) collective-permute-start(f32[192,128]{1,0:T(8,128)S(1)} %get-tuple-element.64.center), channel_id=1, source_target_pairs={{0,1},{1,0},{2,3},{3,2},{4,5},{5,4},{6,7},{7,6},{8,9},{9,8},{10,11... | collective-permute-start | bytes 294920 | tf_op jit(solution)/shard_map/ppermute | solution.py:850
  33.7 8.3 %collective-permute-start.8 = (f32[192,128]{1,0:T(8,128)S(1)}, f32[192,128]{1,0:T(8,128)S(1)}, u32[]{:S(2)}, u32[]{:S(2)}) collective-permute-start(f32[192,128]{1,0:T(8,128)S(1)} %get-tuple-element.63), channel_id=1, source_target_pairs={{0,8},{1,9},{2,10},{3,11},{4,12},{5,13},{6,14},{7,15},{8,0},{9,1},... | collective-permute-start | bytes 294920 | tf_op jit(solution)/shard_map/ppermute | solution.py:844
  34.8 7.2 %collective-permute-start.9 = (f32[192,128]{1,0:T(8,128)S(1)}, f32[192,128]{1,0:T(8,128)S(1)}, u32[]{:S(2)}, u32[]{:S(2)}) collective-permute-start(f32[192,128]{1,0:T(8,128)S(1)} %get-tuple-element.64.center), channel_id=1, source_target_pairs={{0,15},{1,2},{2,1},{3,4},{4,3},{5,6},{6,5},{7,8},{8,7},{9,10},{10,... | collective-permute-start | bytes 294920 | tf_op jit(solution)/shard_map/ppermute | solution.py:850
  36.3 7.7 %collective-permute-start.11 = (f32[64,128]{1,0:T(8,128)S(1)}, f32[64,128]{1,0:T(8,128)S(1)}, u32[]{:S(2)}, u32[]{:S(2)}) collective-permute-start(f32[64,128]{1,0:T(8,128)S(1)} %get-tuple-element.70), channel_id=1, source_target_pairs={{0,16},{16,32},{32,48},{48,64},{64,80},{80,96},{96,112},{112,0},{1... | collective-permute-start | bytes 98312 | tf_op jit(solution)/shard_map/ppermute | solution.py:844
  37.0 7.1 %collective-permute-start.12 = (f32[64,128]{1,0:T(8,128)S(1)}, f32[64,128]{1,0:T(8,128)S(1)}, u32[]{:S(2)}, u32[]{:S(2)}) collective-permute-start(f32[64,128]{1,0:T(8,128)S(1)} %get-tuple-element.71), channel_id=1, source_target_pairs={{0,112},{16,0},{32,16},{48,32},{64,48},{80,64},{96,80},{112,96},{1... | collective-permute-start | bytes 98312 | tf_op jit(solution)/shard_map/ppermute | solution.py:844
  44.2 6.7 %collective-permute-start.13 = (f32[272,128]{1,0:T(8,128)S(1)}, f32[272,128]{1,0:T(8,128)S(1)}, u32[]{:S(2)}, u32[]{:S(2)}) collective-permute-start(f32[272,128]{1,0:T(8,128)S(1)} %shard_map.115.own.sent), channel_id=1, source_target_pairs={{0,15},{1,2},{2,1},{3,4},{4,3},{5,6},{6,5},{7,8},{8,7},{9,10},{10,... | collective-permute-start | bytes 417800 | tf_op jit(solution)/shard_map/ppermute | solution.py:850
  46.1 4.8 %collective-permute-start.14 = (f32[272,128]{1,0:T(8,128)S(1)}, f32[272,128]{1,0:T(8,128)S(1)}, u32[]{:S(2)}, u32[]{:S(2)}) collective-permute-start(f32[272,128]{1,0:T(8,128)S(1)} %shard_map.115.own.sent), channel_id=1, source_target_pairs={{0,1},{1,0},{2,3},{3,2},{4,5},{5,4},{6,7},{7,6},{8,9},{9,8},{10,11... | collective-permute-start | bytes 417800 | tf_op jit(solution)/shard_map/ppermute | solution.py:850
  51.1 6.2 %collective-permute-start.15 = (f32[200,128]{1,0:T(8,128)S(1)}, f32[200,128]{1,0:T(8,128)S(1)}, u32[]{:S(2)}, u32[]{:S(2)}) collective-permute-start(f32[200,128]{1,0:T(8,128)S(1)} %shard_map.117), channel_id=1, source_target_pairs={{0,8},{1,9},{2,10},{3,11},{4,12},{5,13},{6,14},{7,15},{8,0},{9,1},... | collective-permute-start | bytes 307208 | tf_op jit(solution)/shard_map/ppermute | solution.py:844
